TPU v7x, 32 devices: a whole 2x2x4 slice. The times are simulated.
32 devices in a mesh: dom: 8 (over z, x), col: 4 (over y, core).
Axes of the slice: x: 2, y: 2, z: 4, core: 2. Of those that a mesh axis runs over, the one named last changes fastest.
Arguments:
- a_vals: bfloat16 [512, 96, 864], P('dom', 'col'), may hold values from -0.625 to 0.625
- p_vals: bfloat16 [512, 96, 288], P('dom', 'col'), may hold values from -0.625 to 0.625
- a_cols: int32 [512, 9], P('dom'), may hold values from 0 to 511, as said below
- p_aggs: int32 [512, 3], replicated, may hold values from 0 to 31, as said below
- halo_rows: int32 [8, 2, 32], replicated, may hold values from 0 to 63, as said below
- live_rows: int32 [8], P('dom'), may hold values from 16 to 64, as said below
Outputs:
- galerkin: bfloat16 [3072, 1920], P(('dom', 'col'))
Inputs may be any that keep to these rules, and one draw needn't show every extreme that they name: `a_cols`: row i of partition d = i div 64 holds i in slot 0 and global row numbers of partition d (d * 64 to (d + 1) * 64 - 1) in slots 1 to 4; slots 5 to 8 hold positions 0 to 31. halo_rows[d, e] holds 32 different local row numbers (0 to 63) of partition d in increasing order; where the neighbour exists, every position of the list is named by some row of it. `p_aggs`: the three ids of a row of partition d differ; the first two lie in d * 4 to (d + 1) * 4 - 1, the third in the range of partition d + 1 (of partition d for the last one). `live_rows`: at least one partition has all 64 rows live.
All inputs are finite; a program needn't handle non-finite values.
Results may differ from a plain program's by a relative error of at most 0.005.
Values may be sent and summed in bfloat16 or wider, within the bound.
No kernel may reach another device: no remote copies, remote signals or barrier semaphores. Data moves between devices by JAX's collectives and lax.ppermute only.
A program may use at most 256 MiB of HBM per device.

v0:
```python
import jax
import jax.numpy as jnp
from jax import lax
from jax.sharding import PartitionSpec as P

BW = 96
BC = 96
KA = 9
KP = 3
NAG = 4
NB = 64


HIGH = lax.Precision.HIGHEST


def with_halo(value, sides, width):
    for axis, dim in sides:
        count, length = (lax.axis_size(axis), value.shape[dim])
        up = [(i, (i + 1) % count) for i in range(count - 1)]
        down = [(j, i) for i, j in up]
        last = lax.slice_in_dim(value, length - width, length, axis=dim)
        initial = lax.slice_in_dim(value, 0, width, axis=dim)
        before = lax.ppermute(last, axis, up)
        after = lax.ppermute(initial, axis, down)
        value = jnp.concatenate([before, value, after], axis=dim)
    return value


def shifted(block, axis, distance):
    devices = range(lax.axis_size(axis))
    route = [(i - distance, i) for i in devices if i - distance in devices]
    return lax.ppermute(block, axis, route)


def local(a_vals, p_vals, a_cols, p_aggs, halo_rows, live_rows):
    part = lax.axis_index("dom")
    parts = lax.axis_size("dom")
    slice_rows = a_vals.shape[1]
    lower_list = halo_rows[jnp.maximum(part - 1, 0), 1]
    upper_list = halo_rows[jnp.minimum(part + 1, parts - 1), 0]
    q_low = a_cols[:, 5:7]
    q_up = a_cols[:, 7:9]
    has_lower = part > 0
    has_upper = part < parts - 1
    low_res = jnp.where(
        has_lower, (part - 1) * NB + jnp.take(lower_list, q_low, axis=0), part * NB + q_low
    )
    up_res = jnp.where(
        has_upper, (part + 1) * NB + jnp.take(upper_list, q_up, axis=0), part * NB + q_up
    )
    columns = jnp.concatenate([a_cols[:, :5], low_res, up_res], axis=1)
    slab_row = columns - (part - 1) * NB
    p_full = lax.all_gather(p_vals, "col", axis=1, tiled=True)
    extended = with_halo(p_full, (("dom", 0),), NB)
    products = []
    for slot in range(KA):
        block = a_vals[:, :, slot * BW : (slot + 1) * BW]
        fetched = jnp.take(extended, slab_row[:, slot], axis=0)
        products.append(
            jnp.einsum("iwv,ivx->iwx", block, fetched, preferred_element_type=jnp.float32)
        )
    stacked = jnp.stack(products, axis=2).reshape(NB, slice_rows, KA * KP, BC)
    used = jnp.take(p_aggs, columns, axis=0).reshape(NB, KA * KP) - (part - 1) * NAG
    select = (used[:, :, None] == jnp.arange(4 * NAG, dtype=jnp.int32)[None, None, :]).astype(
        jnp.float32
    )
    coupled = jnp.einsum("iwsc,isj->iwjc", stacked, select, precision=HIGH)
    coupled = coupled.reshape(NB, slice_rows, 4 * NAG * BC).astype(jnp.bfloat16)
    own_aggs = lax.dynamic_slice_in_dim(p_aggs, part * NB, NB, 0) - part * NAG
    live = (jnp.arange(NB, dtype=jnp.int32) < live_rows[0]).astype(jnp.float32)
    pick = (own_aggs[:, :, None] == jnp.arange(2 * NAG, dtype=jnp.int32)[None, None, :]).astype(
        jnp.float32
    )
    pick = pick * live[:, None, None]
    row_block = 8
    steps_count = NB // row_block
    p_blocks = p_vals.reshape(steps_count, row_block, slice_rows, KP, BC)
    c_blocks = coupled.reshape(steps_count, row_block, slice_rows, 4 * NAG * BC)
    k_blocks = pick.reshape(steps_count, row_block, KP, 2 * NAG)

    def add_rows(total, items):
        p_piece, c_piece, k_piece = items
        term = jnp.einsum("iwmb,iwx->imbx", p_piece, c_piece, preferred_element_type=jnp.float32)
        return (total + jnp.einsum("imj,imbx->jbx", k_piece, term, precision=HIGH), None)

    start_total = jnp.zeros((2 * NAG, BC, 4 * NAG * BC), jnp.float32)
    summed, unused = lax.scan(add_rows, start_total, (p_blocks, c_blocks, k_blocks))
    partial_value = summed.reshape(2 * NAG * BC, 4 * NAG * BC)
    band = NAG * BC
    shares = lax.psum_scatter(
        partial_value.reshape(2, band, 4 * band), "col", scatter_dimension=1, tiled=True
    )
    came = shifted(shares[1], "dom", 1)
    result = jnp.pad(shares[0], ((0, 0), (band, 0))) + jnp.pad(came, ((0, 0), (0, band)))
    return result.astype(jnp.bfloat16)


def solution(mesh):
    in_specs = (P("dom", "col", None), P("dom", "col", None), P("dom", None), P(), P(), P("dom"))
    out_specs = P(("dom", "col"), None)
    return jax.shard_map(local, mesh=mesh, in_specs=in_specs, out_specs=out_specs, check_vma=False)
```

profile of v0, /device:TPU:16, one launch (start us, length us, event | category | flops | bytes accessed | tf_op | source)
XLA Modules:
  0.0 946.9 jit_solution(5159206988305132636)
XLA Ops:
  6.5 0.7 all-gather.2.cloned.1.call-update
  7.3 3.7 reshape.181
  11.1 0.8 fusion.95
  11.9 35.5 %all-gather.2.cloned.1.call-done = bf16[64,96,288]{2,1,0:T(8,128)(2,1)} async-done(((bf16[64,24,288]{2,1,0:T(8,128)(2,1)}), bf16[64,96,288]{2,1,0:T(8,128)(2,1)}) %all-gather.2.cloned.1.call-update) | async-done | bytes 3538960 | tf_op jit(solution)/shard_map/all_gather | solution.py:54
  47.5 3.4 collective-permute-start
  50.9 0.1 reshape.293
  51.0 0.7 fusion.84
  51.7 1.2 gather_fusion.1
  53.2 3.4 collective-permute-start.1
  56.7 1.2 gather_fusion.2
  58.4 0.1 reshape.273
  58.6 0.1 copy.42
  58.7 1.8 gather_fusion
  60.7 0.2 reshape.272
  61.9 0.2 copy.48
  62.3 191.4 %collective-permute-done = bf16[64,96,288]{2,1,0:T(8,128)(2,1)} collective-permute-done((bf16[64,96,288]{2,1,0:T(8,128)(2,1)}, bf16[64,96,288]{2,1,0:T(8,128)(2,1)}, u32[]{:S(2)}, u32[]{:S(2)}) %collective-permute-start) | collective-permute-done | bytes 3538976 | tf_op jit(solution)/shard_map/ppermute | solution.py:24
  253.7 5.0 constant_dynamic-update-slice_fusion.2
  258.7 2.7 constant_dynamic-update-slice_fusion.1
  261.4 4.9 constant_dynamic-update-slice_fusion
  266.3 8.4 gather_fusion.3
  274.7 8.5 gather_fusion.4
  283.2 8.4 gather_fusion.5
  291.5 8.4 gather_fusion.6
  300.0 8.3 gather_fusion.7
  308.3 8.3 gather_fusion.8
  316.6 8.4 gather_fusion.9
  325.0 8.3 gather_fusion.10
  333.3 8.5 gather_fusion.11
  341.9 5.0 bitcast_dynamic-update-slice_fusion.8
  346.8 5.2 bitcast_dynamic-update-slice_fusion.7
  352.1 2.4 bitcast_dynamic-update-slice_fusion.6
  354.5 2.9 bitcast_dynamic-update-slice_fusion.5
  357.4 2.4 bitcast_dynamic-update-slice_fusion.4
  359.8 2.5 bitcast_dynamic-update-slice_fusion.3
  362.3 2.5 bitcast_dynamic-update-slice_fusion.2
  364.8 2.5 bitcast_dynamic-update-slice_fusion.1
  367.3 2.5 bitcast_dynamic-update-slice_fusion
  369.8 30.4 %copy.46 = f32[64,24,9,288]{0,3,2,1:T(8,128)} copy(f32[64,24,9,288]{3,1,0,2:T(8,128)} %bitcast_dynamic-update-slice_fusion) | data formatting | bytes 31850496 | tf_op jit(solution)/shard_map/stack | solution.py:63
  400.2 32.3 %copy.47 = f32[64,24,27,96]{3,2,1,0:T(8,128)} copy(f32[64,24,27,96]{0,3,2,1:T(8,128)} %bitcast.139) | data formatting | bytes 31850496 | tf_op jit(solution)/shard_map/reshape | solution.py:63
  432.5 15.8 %convert_bitcast_fusion = bf16[64,24,16,96]{3,2,1,0:T(8,128)(2,1)} fusion(f32[64,24,27,96]{3,2,1,0:T(8,128)} %copy.47, s32[64,27]{1,0:T(8,128)S(1)} %copy.45), kind=kOutput, calls=%fused_computation.24 | convolution fusion | flops 766798848 | bytes 20650752 | tf_op jit(solution)/shard_map/iwsc,isj->iwjc/dot_general | solution.py:68
  448.4 11.2 %convert_element_type.29 = bf16[8,8,24,1536]{3,2,1,0:T(8,128)(2,1)} reshape(bf16[64,24,16,96]{3,2,1,0:T(8,128)(2,1)} %convert_bitcast_fusion) | data formatting | bytes 9437184 | tf_op jit(solution)/shard_map/convert_element_type | solution.py:69
  459.5 405.0 %while.11 = (s32[]{:T(128)}, f32[8,96,1536]{2,0,1:T(8,128)}, f32[8,8,3,8]{1,3,2,0:T(8,128)S(1)}, bf16[8,8,24,3,96]{4,2,3,1,0:T(8,128)(2,1)S(1)}, bf16[8,8,24,1536]{3,2,1,0:T(8,128)(2,1)}, /*index=5*/s32[]{:T(128)}, s32[]{:T(128)}) while((s32[]{:T(128)}, f32[8,96,1536]{2,0,1:T(8,128)}, f32[8,8,3,8]{1,3,2,0:T(8,128)S(1)}, ...), condition=%wide.region_1.4_spmd.clone, body=%wide.region_0.3_spmd.clone.sunk | while | flops 511967232 | bytes 38499416 | solution.py:88
  459.7 8.1 fusion.106
  467.8 41.9 %bitcast_add_fusion.2 = f32[8,96,1536]{2,0,1:T(8,128)} fusion(f32[8,96,1536]{2,0,1:T(8,128)} %get-tuple-element.151, f32[8,3,96,1536]{3,2,1,0:T(8,128)} %fusion.106, pred[]{:T(512)S(6)} %compare.5, f32[8,8,3,8]{1,3,2,0:T(8,128)S(1)} %get-tuple-element.159, s32[]{:T(128)} %get-tuple-element.150), kind=kOutput, calls=%fused_computation.14.clone.1 | convolution fusion | flops 342097920 | bytes 23605252 | tf_op jit(solution)/shard_map/while/body/eval_jaxpr/imj,imbx->jbx/dot_general | solution.py:85
  509.7 8.1 fusion.106
  517.8 42.6 %bitcast_add_fusion.2 = f32[8,96,1536]{2,0,1:T(8,128)} fusion(f32[8,96,1536]{2,0,1:T(8,128)} %get-tuple-element.151, f32[8,3,96,1536]{3,2,1,0:T(8,128)} %fusion.106, pred[]{:T(512)S(6)} %compare.5, f32[8,8,3,8]{1,3,2,0:T(8,128)S(1)} %get-tuple-element.159, s32[]{:T(128)} %get-tuple-element.150), kind=kOutput, calls=%fused_computation.14.clone.1 | convolution fusion | flops 342097920 | bytes 23605252 | tf_op jit(solution)/shard_map/while/body/eval_jaxpr/imj,imbx->jbx/dot_general | solution.py:85
  560.4 8.1 fusion.106
  568.4 42.6 %bitcast_add_fusion.2 = f32[8,96,1536]{2,0,1:T(8,128)} fusion(f32[8,96,1536]{2,0,1:T(8,128)} %get-tuple-element.151, f32[8,3,96,1536]{3,2,1,0:T(8,128)} %fusion.106, pred[]{:T(512)S(6)} %compare.5, f32[8,8,3,8]{1,3,2,0:T(8,128)S(1)} %get-tuple-element.159, s32[]{:T(128)} %get-tuple-element.150), kind=kOutput, calls=%fused_computation.14.clone.1 | convolution fusion | flops 342097920 | bytes 23605252 | tf_op jit(solution)/shard_map/while/body/eval_jaxpr/imj,imbx->jbx/dot_general | solution.py:85
  611.0 8.1 fusion.106
  619.1 42.6 %bitcast_add_fusion.2 = f32[8,96,1536]{2,0,1:T(8,128)} fusion(f32[8,96,1536]{2,0,1:T(8,128)} %get-tuple-element.151, f32[8,3,96,1536]{3,2,1,0:T(8,128)} %fusion.106, pred[]{:T(512)S(6)} %compare.5, f32[8,8,3,8]{1,3,2,0:T(8,128)S(1)} %get-tuple-element.159, s32[]{:T(128)} %get-tuple-element.150), kind=kOutput, calls=%fused_computation.14.clone.1 | convolution fusion | flops 342097920 | bytes 23605252 | tf_op jit(solution)/shard_map/while/body/eval_jaxpr/imj,imbx->jbx/dot_general | solution.py:85
  661.7 8.1 fusion.106
  669.7 42.6 %bitcast_add_fusion.2 = f32[8,96,1536]{2,0,1:T(8,128)} fusion(f32[8,96,1536]{2,0,1:T(8,128)} %get-tuple-element.151, f32[8,3,96,1536]{3,2,1,0:T(8,128)} %fusion.106, pred[]{:T(512)S(6)} %compare.5, f32[8,8,3,8]{1,3,2,0:T(8,128)S(1)} %get-tuple-element.159, s32[]{:T(128)} %get-tuple-element.150), kind=kOutput, calls=%fused_computation.14.clone.1 | convolution fusion | flops 342097920 | bytes 23605252 | tf_op jit(solution)/shard_map/while/body/eval_jaxpr/imj,imbx->jbx/dot_general | solution.py:85
  712.3 8.1 fusion.106
  720.4 42.6 %bitcast_add_fusion.2 = f32[8,96,1536]{2,0,1:T(8,128)} fusion(f32[8,96,1536]{2,0,1:T(8,128)} %get-tuple-element.151, f32[8,3,96,1536]{3,2,1,0:T(8,128)} %fusion.106, pred[]{:T(512)S(6)} %compare.5, f32[8,8,3,8]{1,3,2,0:T(8,128)S(1)} %get-tuple-element.159, s32[]{:T(128)} %get-tuple-element.150), kind=kOutput, calls=%fused_computation.14.clone.1 | convolution fusion | flops 342097920 | bytes 23605252 | tf_op jit(solution)/shard_map/while/body/eval_jaxpr/imj,imbx->jbx/dot_general | solution.py:85
  763.0 8.1 fusion.106
  771.1 42.6 %bitcast_add_fusion.2 = f32[8,96,1536]{2,0,1:T(8,128)} fusion(f32[8,96,1536]{2,0,1:T(8,128)} %get-tuple-element.151, f32[8,3,96,1536]{3,2,1,0:T(8,128)} %fusion.106, pred[]{:T(512)S(6)} %compare.5, f32[8,8,3,8]{1,3,2,0:T(8,128)S(1)} %get-tuple-element.159, s32[]{:T(128)} %get-tuple-element.150), kind=kOutput, calls=%fused_computation.14.clone.1 | convolution fusion | flops 342097920 | bytes 23605252 | tf_op jit(solution)/shard_map/while/body/eval_jaxpr/imj,imbx->jbx/dot_general | solution.py:85
  813.7 8.1 fusion.106
  821.7 42.6 %bitcast_add_fusion.2 = f32[8,96,1536]{2,0,1:T(8,128)} fusion(f32[8,96,1536]{2,0,1:T(8,128)} %get-tuple-element.151, f32[8,3,96,1536]{3,2,1,0:T(8,128)} %fusion.106, pred[]{:T(512)S(6)} %compare.5, f32[8,8,3,8]{1,3,2,0:T(8,128)S(1)} %get-tuple-element.159, s32[]{:T(128)} %get-tuple-element.150), kind=kOutput, calls=%fused_computation.14.clone.1 | convolution fusion | flops 342097920 | bytes 23605252 | tf_op jit(solution)/shard_map/while/body/eval_jaxpr/imj,imbx->jbx/dot_general | solution.py:85
  864.5 7.2 copy.49
  871.8 48.1 %reduce-scatter.2.cloned.1.call-done = f32[2,96,1536]{2,1,0:T(8,128)} async-done(((f32[2,384,1536]{2,1,0:T(8,128)}), f32[2,96,1536]{2,1,0:T(8,128)}) %reduce-scatter.2.cloned.1.call-update) | async-done | bytes 1179664 | tf_op jit(solution)/shard_map/reduce_scatter | solution.py:91
  919.9 1.3 slice_bitcast_fusion.1
  921.2 3.4 collective-permute-start.2
  924.6 14.5 %collective-permute-done.2 = f32[96,1536]{1,0:T(8,128)S(1)} collective-permute-done((f32[96,1536]{1,0:T(8,128)S(1)}, f32[96,1536]{1,0:T(8,128)S(1)}, u32[]{:S(2)}, u32[]{:S(2)}) %collective-permute-start.2) | collective-permute-done | bytes 589856 | tf_op jit(solution)/shard_map/ppermute | solution.py:33
  939.0 0.8 add_convert_fusion
  (89 shorter events, 1.7 us)
Async XLA Ops:
  6.5 40.9 %all-gather.2.cloned.1.call-start = ((), (), s32[]{:S(2)}) async-start(), calls=%async_computation.1 | async-start | bytes 5898240 | tf_op jit(solution)/shard_map/all_gather | solution.py:54
  7.3 912.6 %reduce-scatter.2.cloned.1.call-start = ((), (), s32[]{:S(2)}) async-start(), calls=%async_computation.2 | async-start | bytes 5898240 | tf_op jit(solution)/shard_map/reduce_scatter | solution.py:91
  47.5 206.3 %collective-permute-start = (bf16[64,96,288]{2,1,0:T(8,128)(2,1)}, bf16[64,96,288]{2,1,0:T(8,128)(2,1)}, u32[]{:S(2)}, u32[]{:S(2)}) collective-permute-start(bf16[64,96,288]{2,1,0:T(8,128)(2,1)} %all-gather.2.cloned.1.call-done), channel_id=1, source_target_pairs={{0,4},{4,8},{8,12},{12,16},{16,20},{20,24},{24,28},{1,5},{5,9},{9,... | collective-permute-start | bytes 10616840 | tf_op jit(solution)/shard_map/ppermute | solution.py:24
  53.2 208.2 %collective-permute-start.1 = (bf16[64,96,288]{2,1,0:T(8,128)(2,1)}, bf16[64,96,288]{2,1,0:T(8,128)(2,1)}, u32[]{:S(2)}, u32[]{:S(2)}) collective-permute-start(bf16[64,96,288]{2,1,0:T(8,128)(2,1)} %all-gather.2.cloned.1.call-done), channel_id=1, source_target_pairs={{4,0},{8,4},{12,8},{16,12},{20,16},{24,20},{28,24},{5,1},{9,5},{13... | collective-permute-start | bytes 10616840 | tf_op jit(solution)/shard_map/ppermute | solution.py:25
  56.7 1.6 copy-start.1
  56.7 1.8 copy-start
  62.3 196.4 %slice-start = ((s8[4718592]{0:T(1024)(128)(4,1)}), s8[4194304]{0:T(1024)(128)(4,1)S(1)}, s32[]{:S(2)}) async-start(s8[4718592]{0:T(1024)(128)(4,1)} %bitcast.141), calls=%async_computation.3 | async-start | bytes 8388608
  62.3 196.4 %slice-start.1 = ((s8[4718592]{0:T(1024)(128)(4,1)}), s8[524288]{0:T(1024)(128)(4,1)S(1)}, s32[]{:S(2)}) async-start(s8[4718592]{0:T(1024)(128)(4,1)} %bitcast.141), calls=%async_computation.4 | async-start | bytes 1048576
  333.3 18.7 %slice-start.14 = ((s8[4718592]{0:T(1024)(128)(4,1)}), s8[524288]{0:T(1024)(128)(4,1)S(1)}, s32[]{:S(2)}) async-start(s8[4718592]{0:T(1024)(128)(4,1)} %bitcast.155), calls=%async_computation.17 | async-start | bytes 1048576
  341.8 10.2 %slice-start.15 = ((s8[4718592]{0:T(1024)(128)(4,1)}), s8[4194304]{0:T(1024)(128)(4,1)S(1)}, s32[]{:S(2)}) async-start(s8[4718592]{0:T(1024)(128)(4,1)} %bitcast.155), calls=%async_computation.18 | async-start | bytes 8388608
  341.8 12.6 %slice-start.12 = ((s8[4718592]{0:T(1024)(128)(4,1)}), s8[4194304]{0:T(1024)(128)(4,1)S(1)}, s32[]{:S(2)}) async-start(s8[4718592]{0:T(1024)(128)(4,1)} %bitcast.153), calls=%async_computation.15 | async-start | bytes 8388608
  346.8 5.2 copy-start.2
  346.8 7.7 slice-start.13
  352.0 5.4 slice-start.10
  352.0 7.8 slice-start.8
  354.5 2.9 slice-start.11
  354.5 5.3 slice-start.9
  357.4 4.9 slice-start.6
  357.4 7.4 slice-start.4
  359.8 2.5 slice-start.7
  359.8 5.0 slice-start.5
  362.3 5.0 slice-start.2
  364.8 2.5 slice-start.3
  921.2 17.8 %collective-permute-start.2 = (f32[96,1536]{1,0:T(8,128)S(1)}, f32[96,1536]{1,0:T(8,128)S(1)}, u32[]{:S(2)}, u32[]{:S(2)}) collective-permute-start(f32[96,1536]{1,0:T(8,128)S(1)} %get-tuple-element.87), channel_id=1, source_target_pairs={{0,4},{4,8},{8,12},{12,16},{16,20},{20,24},{24,28},{1,5},{5,9},{9,... | collective-permute-start | bytes 1769480 | tf_op jit(solution)/shard_map/ppermute | solution.py:33
Sparse Core Ops, SparseCore 0:
  8.9 38.4 all-gather.1
  871.9 47.9 reduce-scatter.1
where the time goes:
time: 952 us; the launch traced here: 947 us
  matrix products  448 us (47%)
  waiting for transfers between devices  290 us (30%)
  local copies, waits for them, and re-layouts  182 us (19%)
  between operations  14.7 us (2%)
  starting transfers between devices  10.1 us (1%)
    dot_general x8, matrix products, add_rows(): jnp.einsum('imj,imbx->jbx', k_piece, term, precision=HIGH)  340 us
    ppermute x1, waiting for transfers between devices, with_halo(): before = lax.ppermute(last, axis, up)  191 us
    gather x9, local copies, waits for them, and re-layouts, local(): fetched = jnp.take(extended, slab_row[:, slot], axis=0)  75.5 us
    dot_general x8, matrix products, add_rows(): jnp.einsum('iwmb,iwx->imbx', p_piece, c_piece, preferred_element_type=jnp...  64.6 us
    reduce_scatter x1, waiting for transfers between devices, local(): lax.psum_scatter(partial_value.reshape(2, band, 4 * band), 'col', scatter...  48.1 us
    all_gather x1, waiting for transfers between devices, local(): p_full = lax.all_gather(p_vals, 'col', axis=1, tiled=True)  35.5 us
    reshape x1, local copies, waits for them, and re-layouts, local(): stacked = jnp.stack(products, axis=2).reshape(NB, slice_rows, KA * KP, BC)  32.3 us
    another operation x1, local copies, waits for them, and re-layouts, local(): stacked = jnp.stack(products, axis=2).reshape(NB, slice_rows, KA * KP, BC)  30.4 us
  transfers between devices with their start and end apart: 5, of which 4 were waited for; matrix products, arithmetic and copies ran while one was open for 2% of the time, Pallas kernels for 0%

commit v1 on v0

v1 whole, which is shorter than its diff:
```python
import jax
import jax.numpy as jnp
from jax import lax
from jax.experimental import pallas as pl
from jax.experimental.pallas import tpu as pltpu
from jax.sharding import PartitionSpec as P

BW = 96
BC = 96
KA = 9
KP = 3
NAG = 4
NB = 64
NS = 32
W = 24
ROWS = NB * W
AXES = ("dom", "col")
VMEM_LIMIT = 56 * 1024 * 1024
F32, BF16 = jnp.float32, jnp.bfloat16


def params():
    return pltpu.CompilerParams(vmem_limit_bytes=VMEM_LIMIT)


def whole_vmem():
    return pl.BlockSpec(memory_space=pltpu.VMEM)


def smem():
    return pl.BlockSpec(memory_space=pltpu.SMEM)


def anywhere():
    return pl.BlockSpec(memory_space=pl.ANY)


def pack_own_kernel(p_ref, out_ref):
    out_ref[0:ROWS, :] = p_ref[:, 0:256]
    for g in range(NB // 16):
        tails = [p_ref[48 * (8 * g + q) : 48 * (8 * g + q) + 48, 256:288] for q in range(8)]
        out_ref[ROWS + 48 * g : ROWS + 48 * g + 48, :] = jnp.concatenate(tails, axis=1)


def pack_halo_kernel(lists_ref, p_ref, down_ref, up_ref, wide_ref):
    def widen(t, carry):
        pair = p_ref[pl.ds(pl.multiple_of(t * 48, 48), 48), :].astype(F32)
        wide_ref[2 * t] = pair[0:24]
        wide_ref[2 * t + 1] = pair[24:48]
        return carry

    lax.fori_loop(0, NB // 2, widen, 0)
    for e, out_ref in ((0, down_ref), (1, up_ref)):
        for g in range(NS // 16):
            tails = []
            for q in range(8):
                t = 8 * g + q
                first = wide_ref[lists_ref[e * NS + 2 * t]]
                second = wide_ref[lists_ref[e * NS + 2 * t + 1]]
                pair = jnp.concatenate([first, second], axis=0).astype(BF16)
                out_ref[48 * t : 48 * t + 48, :] = pair[:, 0:256]
                tails.append(pair[:, 256:288])
            start = NS * W + 48 * g
            out_ref[start : start + 48, :] = jnp.concatenate(tails, axis=1)


def spread_kernel(p_ref, mask_ref, out_ref):
    eye = (
        lax.broadcasted_iota(jnp.int32, (288, 288), 0)
        == lax.broadcasted_iota(jnp.int32, (288, 288), 1)
    ).astype(F32).astype(BF16)
    for n in range(3):
        cols = slice(512 * n, 512 * n + 512)
        flipped = lax.dot_general(
            eye, p_ref[cols, :], (((1,), (1,)), ((), ())), preferred_element_type=F32
        )
        for b in range(8):
            total = jnp.zeros((BC, 512), F32)
            for m in range(KP):
                row = mask_ref[3 * b + m : 3 * b + m + 1, cols]
                total += flipped[BC * m : BC * m + BC] * row
            out_ref[BC * b : BC * b + BC, cols] = total.astype(BF16)


def unpack(count, agg_of, sources_ref, blocks_ref):
    blocks_ref[...] = jnp.zeros_like(blocks_ref)
    lane = lax.broadcasted_iota(jnp.int32, (48, 128), 1)

    def group(g, carry):
        for q in range(8):
            t = 8 * g + q
            parts = [[], [], []]
            for v in range(4):
                rows = pl.ds(pl.multiple_of(t * 48, 48), 48)
                x0 = sources_ref[v, rows, 0:128].astype(F32)
                x1 = sources_ref[v, rows, 128:256].astype(F32)
                tail_rows = pl.ds(pl.multiple_of(count * W + g * 48, 48), 48)
                half = 128 * (q // 4)
                tail = sources_ref[v, tail_rows, half : half + 128].astype(F32)
                shift = (64 - 32 * (q % 4)) % 128
                if shift:
                    tail = pltpu.roll(tail, shift, 1)
                parts[0].append(x0)
                parts[1].append(
                    jnp.where(lane < 32, pltpu.roll(x0, 32, 1), pltpu.roll(x1, 32, 1))
                )
                parts[2].append(jnp.where(lane < 64, pltpu.roll(x1, 64, 1), tail))
            for j in range(KP):
                for odd in range(2):
                    r = 2 * t + odd
                    block = jnp.concatenate([x[24 * odd : 24 * odd + 24] for x in parts[j]], axis=0)
                    at = pl.multiple_of(agg_of(r, j) * 128, 128)
                    blocks_ref[r, :, pl.ds(at, 128)] = block.astype(BF16)
        return carry

    lax.fori_loop(0, count // 16, group, 0)


def fetch(refs, scratch, sems, col):
    copies = [
        pltpu.make_async_copy(ref, scratch.at[jnp.bitwise_xor(col, s)], sems.at[s])
        for s, ref in enumerate(refs)
    ]
    for copy in copies:
        copy.start()
    for copy in copies:
        copy.wait()


def own_kernel(place_ref, cols_ref, aggs_ref, s0, s1, s2, s3, a_ref, low_ref, up_ref, below_ref, above_ref,
               sources, blocks, sems):
    col, first, last = place_ref[0], place_ref[1], place_ref[2]
    fetch((s0, s1, s2, s3), sources, sems, col)
    unpack(NB, lambda r, j: aggs_ref[KP * r + j], sources, blocks)
    pad32 = jnp.zeros((32, 1024), BF16)
    pad64 = jnp.zeros((64, 1024), BF16)

    def pair(t, carry):
        rows = pl.ds(pl.multiple_of(t * 48, 48), 48)
        a = a_ref[rows, 0:512]
        done = []
        for odd in range(2):
            at = KA * (2 * t + odd)
            weights = jnp.concatenate([blocks[cols_ref[at + k]] for k in range(5)] + [pad32], axis=0)
            got = jnp.dot(a[16 * odd : 16 * odd + 32], weights, preferred_element_type=F32)
            done.append(got[8 * odd : 8 * odd + 24])
        total = jnp.concatenate(done, axis=0)
        below_ref[rows, :] = total[:, 0:512]
        above_ref[rows, :] = total[:, 512:1024]
        return carry

    lax.fori_loop(0, NB // 2, pair, 0)

    def edge(a_edge, slot, order):
        def pair(t, carry):
            rows = pl.ds(pl.multiple_of(t * 48, 48), 48)
            a = a_edge[rows, :]
            done = []
            for odd in range(2):
                at = KA * (2 * t + odd) + slot
                pieces = [blocks[cols_ref[at]], blocks[cols_ref[at + 1]]]
                weights = jnp.concatenate(order(pieces, pad64), axis=0)
                got = jnp.dot(a[16 * odd : 16 * odd + 32], weights, preferred_element_type=F32)
                done.append(got[8 * odd : 8 * odd + 24])
            total = jnp.concatenate(done, axis=0)
            below_ref[rows, :] += total[:, 0:512]
            above_ref[rows, :] += total[:, 512:1024]
            return carry

        lax.fori_loop(0, NB // 2, pair, 0)

    @pl.when(first == 1)
    def _():
        edge(low_ref, 5, lambda pieces, pad: pieces + [pad])

    @pl.when(last == 1)
    def _():
        edge(up_ref, 7, lambda pieces, pad: [pad] + pieces)


def make_halo_kernel(upper):
    def kernel(place_ref, cols_ref, list_ref, aggs_ref, s0, s1, s2, s3, a_ref, own_ref, spread_ref,
               send_ref, keep_ref, sources, blocks, coupled, sems):
        fetch((s0, s1, s2, s3), sources, sems, place_ref[0])
        unpack(NS, lambda r, j: aggs_ref[KP * list_ref[r] + j], sources, blocks)
        pad64 = jnp.zeros((64, 1024), BF16)

        def pair(t, carry):
            rows = pl.ds(pl.multiple_of(t * 48, 48), 48)
            a = a_ref[rows, :]
            own = own_ref[rows, :]
            done = []
            for odd in range(2):
                at = KA * (2 * t + odd) + (7 if upper else 5)
                pieces = [blocks[cols_ref[at]], blocks[cols_ref[at + 1]]]
                pieces = [pad64] + pieces if upper else pieces + [pad64]
                weights = jnp.concatenate(pieces, axis=0)
                got = jnp.dot(a[16 * odd : 16 * odd + 32], weights, preferred_element_type=F32)
                done.append(got[8 * odd : 8 * odd + 24])
            total = jnp.concatenate(done, axis=0)
            if upper:
                total = jnp.concatenate([total[:, 0:512] + own, total[:, 512:1024]], axis=1)
            else:
                total = jnp.concatenate([total[:, 0:512], total[:, 512:1024] + own], axis=1)
            coupled[rows, :] = total.astype(BF16)
            return carry

        lax.fori_loop(0, NB // 2, pair, 0)
        lane = lax.broadcasted_iota(jnp.int32, (128, 128), 1)
        for n in range(2):
            for half, out_ref in ((0, send_ref), (1, keep_ref)):
                def tile(m, carry):
                    rows = pl.ds(pl.multiple_of(m * 128, 128), 128)
                    from_rows = pl.ds(pl.multiple_of(384 * half + m * 128, 128), 128)
                    y = jnp.dot(
                        spread_ref[from_rows, :],
                        coupled[:, 512 * n : 512 * n + 512],
                        preferred_element_type=F32,
                    )
                    y0, y1, y2, y3 = [y[:, 128 * c : 128 * c + 128] for c in range(4)]
                    y1, y2, y3 = pltpu.roll(y1, 96, 1), pltpu.roll(y2, 64, 1), pltpu.roll(y3, 32, 1)
                    packed = [
                        jnp.where(lane < 96, y0, y1),
                        jnp.where(lane < 64, y1, y2),
                        jnp.where(lane < 32, y2, y3),
                    ]
                    for c in range(3):
                        at = 384 * n + 128 * c
                        out_ref[rows, at : at + 128] = packed[c].astype(out_ref.dtype)
                    return carry

                lax.fori_loop(0, 3, tile, 0)

    return kernel


def local(a_vals, p_vals, a_cols, p_aggs, halo_rows, live_rows):
    part = lax.axis_index("dom")
    parts = lax.axis_size("dom")
    col = lax.axis_index("col")
    cols_count = lax.axis_size("col")
    devices = [(d, c) for d in range(parts) for c in range(cols_count)]

    def moved(x, step, flip):
        route = [
            (d * cols_count + c, (d + step) * cols_count + (c ^ flip))
            for d, c in devices
            if 0 <= d + step < parts
        ]
        return lax.ppermute(x, AXES, route)

    p_flat = p_vals.reshape(ROWS, KP * BC)
    a_flat = a_vals.reshape(ROWS, KA * BW)

    own_pack = pl.pallas_call(
        pack_own_kernel,
        out_shape=jax.ShapeDtypeStruct((ROWS + 192, 256), BF16),
        in_specs=[whole_vmem()],
        out_specs=whole_vmem(),
        compiler_params=params(),
    )(p_flat)
    lists = lax.dynamic_slice_in_dim(halo_rows, part, 1, 0).reshape(2 * NS)
    halo_shape = jax.ShapeDtypeStruct((NS * W + 96, 256), BF16)
    down_pack, up_pack = pl.pallas_call(
        pack_halo_kernel,
        out_shape=[halo_shape, halo_shape],
        in_specs=[smem(), whole_vmem()],
        out_specs=[whole_vmem(), whole_vmem()],
        scratch_shapes=[pltpu.VMEM((NB, W, KP * BC), F32)],
        compiler_params=params(),
    )(lists, p_flat)

    def gathered(x):
        near = moved(x, 0, 2)
        return (x, moved(x, 0, 1), near, moved(near, 0, 1))

    own_sources = gathered(own_pack)
    low_sources = gathered(moved(up_pack, 1, 0))
    up_sources = gathered(moved(down_pack, -1, 0))

    lower, upper = jnp.maximum(part - 1, 0), jnp.minimum(part + 1, parts - 1)
    is_first = (part == 0).astype(jnp.int32)
    is_last = (part == parts - 1).astype(jnp.int32)
    place = jnp.stack([col.astype(jnp.int32), is_first, is_last])
    slot = jnp.arange(KA, dtype=jnp.int32)[None, :]
    cols = jnp.where(slot < 5, a_cols - part * NB, a_cols).reshape(NB * KA)

    def aggs_at(which):
        rows = lax.dynamic_slice_in_dim(p_aggs, which * NB, NB, 0) - which * NAG
        return rows

    own_aggs = aggs_at(part)
    low_aggs = aggs_at(lower).reshape(NB * KP)
    up_aggs = aggs_at(upper).reshape(NB * KP)
    low_list = lax.dynamic_slice(halo_rows, (lower, 1, 0), (1, 1, NS)).reshape(NS)
    up_list = lax.dynamic_slice(halo_rows, (upper, 0, 0), (1, 1, NS)).reshape(NS)

    order = jnp.stack([jnp.bitwise_xor(col, f) + NAG * e for f in (3, 1, 2, 0) for e in (0, 1)])
    live = jnp.arange(NB, dtype=jnp.int32) < live_rows[0]
    mask = (own_aggs.T[None, :, :] == order[:, None, None]) & live[None, None, :]
    mask = jnp.repeat(mask.reshape(8 * KP, NB).astype(F32), W, axis=1)
    spread = pl.pallas_call(
        spread_kernel,
        out_shape=jax.ShapeDtypeStruct((8 * BC, ROWS), BF16),
        in_specs=[whole_vmem(), whole_vmem()],
        out_specs=whole_vmem(),
        compiler_params=params(),
        cost_estimate=pl.CostEstimate(flops=10**9, bytes_accessed=4 * 10**6, transcendentals=0),
    )(p_flat, mask)

    a_low = lax.slice_in_dim(a_flat, 480, 736, axis=1)
    a_up = lax.slice_in_dim(a_flat, 608, 864, axis=1)
    own_shape = jax.ShapeDtypeStruct((ROWS, 512), F32)
    own_below, own_above = pl.pallas_call(
        own_kernel,
        out_shape=[own_shape, own_shape],
        in_specs=[smem()] * 3 + [anywhere()] * 4 + [whole_vmem()] * 3,
        out_specs=[whole_vmem(), whole_vmem()],
        scratch_shapes=[
            pltpu.VMEM((4, ROWS + 192, 256), BF16),
            pltpu.VMEM((NB, BW, 1024), BF16),
            pltpu.SemaphoreType.DMA((4,)),
        ],
        compiler_params=params(),
        cost_estimate=pl.CostEstimate(flops=4 * 10**9, bytes_accessed=14 * 10**6, transcendentals=0),
    )(place, cols, own_aggs.reshape(NB * KP), *own_sources, a_flat, a_low, a_up)

    def halo_terms(upper_side, rows_list, aggs, sources, a_part, own):
        return pl.pallas_call(
            make_halo_kernel(upper_side),
            out_shape=[
                jax.ShapeDtypeStruct((4 * BC, 8 * BC), BF16),
                jax.ShapeDtypeStruct((4 * BC, 8 * BC), F32),
            ],
            in_specs=[smem()] * 4 + [anywhere()] * 4 + [whole_vmem()] * 3,
            out_specs=[whole_vmem(), whole_vmem()],
            scratch_shapes=[
                pltpu.VMEM((4, NS * W + 96, 256), BF16),
                pltpu.VMEM((NS, BW, 1024), BF16),
                pltpu.VMEM((ROWS, 1024), BF16),
                pltpu.SemaphoreType.DMA((4,)),
            ],
            compiler_params=params(),
            cost_estimate=pl.CostEstimate(
                flops=5 * 10**9, bytes_accessed=14 * 10**6, transcendentals=0
            ),
        )(place, cols, rows_list, aggs, *sources, a_part, own, spread)

    def summed(send, keep):
        came = moved(send, 0, 1)
        both = keep + came.astype(F32)
        far = moved(both[: 2 * BC].astype(BF16), 0, 2)
        mine = both[2 * BC :] + far.astype(F32)
        return mine[:BC], moved(mine[BC:].astype(BF16), 1, 0)

    low_own, low_next = summed(*halo_terms(False, low_list, low_aggs, low_sources, a_low, own_below))
    up_own, up_next = summed(*halo_terms(True, up_list, up_aggs, up_sources, a_up, own_above))
    band = NAG * BC
    own = jnp.concatenate([low_own, up_own], axis=1)
    came = jnp.concatenate([low_next, up_next], axis=1).astype(F32)
    result = jnp.pad(own, ((0, 0), (band, 0))) + jnp.pad(came, ((0, 0), (0, band)))
    return result.astype(BF16)


def solution(mesh):
    in_specs = (P("dom", "col", None), P("dom", "col", None), P("dom", None), P(), P(), P("dom"))
    out_specs = P(("dom", "col"), None)
    return jax.shard_map(local, mesh=mesh, in_specs=in_specs, out_specs=out_specs, check_vma=False)
```

time: 952 us -> 157 us (0.16)
  the two profiles are of different devices: /device:TPU:16 before, /device:TPU:30 now
where the time goes in v1:
time: 157 us; the launch traced here: 156 us
  Pallas kernels  86.1 us (55%)
  waiting for transfers between devices  41.1 us (26%)
  starting transfers between devices  13.9 us (9%)
  local copies, waits for them, and re-layouts  11.9 us (8%)
  other arithmetic  2.49 us (2%)
    pallas_call x2, Pallas kernels, halo_terms(): pl.pallas_call(make_halo_kernel(upper_side), out_shape=[jax.ShapeDtypeStr...  42.6 us
    ppermute x17, waiting for transfers between devices, moved(): return lax.ppermute(x, AXES, route)  41.1 us
    pallas_call x1, Pallas kernels, local(): pl.pallas_call(own_kernel, out_shape=[own_shape, own_shape], in_specs=[sm...  33.9 us
    ppermute x17, starting transfers between devices, moved(): return lax.ppermute(x, AXES, route)  13.9 us
    pallas_call x1, Pallas kernels, local(): pl.pallas_call(spread_kernel, out_shape=jax.ShapeDtypeStruct((8 * BC, ROW...  4.43 us
  transfers between devices with their start and end apart: 17, of which 7 were waited for; matrix products, arithmetic and copies ran while one was open for 8% of the time, Pallas kernels for 54%

profile of v1, /device:TPU:30, one launch (start us, length us, event | category | flops | bytes accessed | tf_op | source)
XLA Modules:
  0.0 156.3 jit_solution(8347867851551655841)
XLA Ops:
  0.0 2.3 %shard_map.65.s0 = bf16[1728,256]{1,0:T(8,128)(2,1)} custom-call(bf16[1536,288]{1,0:T(8,128)(2,1)} %bitcast.19), custom_call_target="tpu_custom_call" | custom-call | tf_op jit(solution)/shard_map/pallas_call | solution.py:255
  2.3 0.5 collective-permute-start.5
  2.9 0.0 collective-permute-start.4
  2.9 0.7 constant_dynamic-slice_fusion.1
  3.5 0.6 reshape.47.lists_ref
  4.1 2.9 %shard_map.64 = (bf16[864,256]{1,0:T(8,128)(2,1)}, bf16[864,256]{1,0:T(8,128)(2,1)}) custom-call(s32[64]{0:T(128)} %reshape.47.lists_ref, bf16[1536,288]{1,0:T(8,128)(2,1)} %bitcast.20), custom_call_target="tpu_custom_call" | custom-call | tf_op jit(solution)/shard_map/pallas_call | solution.py:264
  7.0 1.3 collective-permute-start
  8.3 5.3 %collective-permute-start.9 = (bf16[864,256]{1,0:T(8,128)(2,1)}, bf16[864,256]{1,0:T(8,128)(2,1)}, u32[]{:S(2)}, u32[]{:S(2)}) collective-permute-start(bf16[864,256]{1,0:T(8,128)(2,1)} %get-tuple-element.17), channel_id=1, source_target_pairs={{4,0},{5,1},{6,2},{7,3},{8,4},{9,5},{10,6},{11,7},{12,8},{13,9},{1... | collective-permute-start | bytes 1327112 | tf_op jit(solution)/shard_map/ppermute | solution.py:250
  13.6 0.6 dynamic-slice_subtract_fusion.2
  14.3 0.1 stack.56
  14.3 0.1 eq.30
  14.4 0.1 eq.31
  15.2 0.1 and_convert_fusion
  15.3 8.8 %collective-permute-done.5.s2 = bf16[1728,256]{1,0:T(8,128)(2,1)} collective-permute-done((bf16[1728,256]{1,0:T(8,128)(2,1)}, bf16[1728,256]{1,0:T(8,128)(2,1)}, u32[]{:S(2)}, u32[]{:S(2)}) %collective-permute-start.5) | collective-permute-done | bytes 884768 | tf_op jit(solution)/shard_map/ppermute | solution.py:250
  24.1 0.1 subtract_select_fusion
  24.1 0.1 copy.9
  24.2 0.7 reshape.50.aggs_ref
  25.0 0.1 copy.7
  25.1 0.7 reshape.44.cols_ref
  25.8 0.3 broadcast_in_dim.16
  26.0 1.1 reshape.51.mask_ref
  27.1 0.8 copy.8
  27.9 0.6 reshape.46.aggs_ref
  28.5 0.1 copy.10
  28.6 0.7 reshape.53.aggs_ref
  29.3 0.6 pad_add_fusion.place_ref
  29.9 1.3 fusion.5
  31.1 0.0 collective-permute-done.s0
  31.2 0.5 collective-permute-start.2
  31.7 1.5 collective-permute-start.11
  33.2 2.0 %fusion.7 = (bf16[1536,256]{1,0:T(8,128)(2,1)}, bf16[1536,256]{1,0:T(8,128)(2,1)}) fusion(bf16[1536,864]{1,0:T(8,128)(2,1)S(1)} %bitcast.23), kind=kLoop, calls=%fused_computation.29 | loop fusion | bytes 3145728 | tf_op jit(solution)/shard_map/slice | solution.py:311
  35.1 0.0 collective-permute-start.1
  35.1 9.2 %collective-permute-done.2.s2 = bf16[864,256]{1,0:T(8,128)(2,1)S(1)} collective-permute-done((bf16[864,256]{1,0:T(8,128)(2,1)}, bf16[864,256]{1,0:T(8,128)(2,1)S(1)}, u32[]{:S(2)}, u32[]{:S(2)}) %collective-permute-start.2) | collective-permute-done | bytes 442400 | tf_op jit(solution)/shard_map/ppermute | solution.py:250
  44.3 4.4 %shard_map.67.spread_ref = bf16[768,1536]{1,0:T(8,128)(2,1)} custom-call(bf16[1536,288]{1,0:T(8,128)(2,1)} %bitcast.21, f32[24,1536]{1,0:T(8,128)} %reshape.51.mask_ref), custom_call_target="tpu_custom_call" | custom-call | flops 1000000000 | bytes 4000000 | tf_op jit(solution)/shard_map/pallas_call | solution.py:302
  48.8 0.0 collective-permute-done.4.s1
  48.8 0.3 collective-permute-start.10
  49.1 4.3 %collective-permute-done.11.s2 = bf16[864,256]{1,0:T(8,128)(2,1)S(1)} collective-permute-done((bf16[864,256]{1,0:T(8,128)(2,1)}, bf16[864,256]{1,0:T(8,128)(2,1)S(1)}, u32[]{:S(2)}, u32[]{:S(2)}) %collective-permute-start.11) | collective-permute-done | bytes 442400 | tf_op jit(solution)/shard_map/ppermute | solution.py:250
  53.4 0.0 collective-permute-start.12
  53.4 0.0 collective-permute-done.6.s3
  53.4 33.9 %shard_map.66 = (f32[1536,512]{1,0:T(8,128)}, f32[1536,512]{1,0:T(8,128)}) custom-call(s32[3]{0:T(128)} %pad_add_fusion.place_ref, s32[576]{0:T(1024)} %reshape.44.cols_ref, s32[192]{0:T(256)} %reshape.50.aggs_ref, bf16[1728,256]{1,0:T(8,128)(2,1)} %shard_map.65.s0, bf16[1728,256]{1,0:T(8,128)(2,1)} %collective-permute-done.4.s1, ...), custom_call_target="tpu_custom_call" | custom-call | flops 4000000000 | bytes 14000000 | tf_op jit(solution)/shard_map/pallas_call | solution.py:314
  87.4 0.0 collective-permute-done.1.s1
  87.4 0.0 collective-permute-done.3.s3
  87.4 0.7 copy-done.9
  88.2 0.2 copy-done.10
  88.3 20.7 %shard_map.68 = (bf16[384,768]{1,0:T(8,128)(2,1)}, f32[384,768]{1,0:T(8,128)}) custom-call(s32[3]{0:T(128)} %pad_add_fusion.place_ref, s32[576]{0:T(1024)} %reshape.44.cols_ref, s32[32]{0:T(128)} %get-tuple-element.26.list_ref, s32[192]{0:T(256)} %reshape.46.aggs_ref, bf16[864,256]{1,0:T(8,128)(2,1)} %collective-permute-done.s0, bf16[864,256]{1,0:T(8,128)(2,1)} %copy-done.9, ...), custom_call_target="tpu_custom_call" | custom-call | flops 5000000000 | bytes 14000000 | tf_op jit(solution)/shard_map/pallas_call | solution.py:329
  109.0 0.4 collective-permute-start.7
  109.4 0.0 collective-permute-done.10.s1
  109.5 0.8 copy-done.7
  110.2 0.1 copy-done.8
  110.4 21.9 %shard_map.69 = (bf16[384,768]{1,0:T(8,128)(2,1)}, f32[384,768]{1,0:T(8,128)}) custom-call(s32[3]{0:T(128)} %pad_add_fusion.place_ref, s32[576]{0:T(1024)} %reshape.44.cols_ref, s32[32]{0:T(128)} %get-tuple-element.27.list_ref, s32[192]{0:T(256)} %reshape.53.aggs_ref, bf16[864,256]{1,0:T(8,128)(2,1)} %collective-permute-done.9.s0, ...), custom_call_target="tpu_custom_call" | custom-call | flops 5000000000 | bytes 14000000 | tf_op jit(solution)/shard_map/pallas_call | solution.py:329
  132.3 0.2 collective-permute-start.13
  132.5 0.1 convert_add_fusion.1
  132.6 0.6 collective-permute-start.8
  133.2 1.3 collective-permute-done.13
  134.5 0.1 convert_add_fusion
  134.7 0.6 collective-permute-start.14
  135.3 7.3 %collective-permute-done.8 = bf16[192,768]{1,0:T(8,128)(2,1)S(1)} collective-permute-done((bf16[192,768]{1,0:T(8,128)(2,1)S(1)}, bf16[192,768]{1,0:T(8,128)(2,1)S(1)}, u32[]{:S(2)}, u32[]{:S(2)}) %collective-permute-start.8) | collective-permute-done | bytes 294944 | tf_op jit(solution)/shard_map/ppermute | solution.py:250
  142.5 0.1 slice_add_fusion.1
  142.6 1.3 collective-permute-start.15
  143.9 4.4 %collective-permute-done.14 = bf16[192,768]{1,0:T(8,128)(2,1)S(1)} collective-permute-done((bf16[192,768]{1,0:T(8,128)(2,1)S(1)}, bf16[192,768]{1,0:T(8,128)(2,1)S(1)}, u32[]{:S(2)}, u32[]{:S(2)}) %collective-permute-start.14) | collective-permute-done | bytes 294944 | tf_op jit(solution)/shard_map/ppermute | solution.py:250
  148.3 0.1 slice_add_fusion
  148.4 1.3 collective-permute-start.16
  149.7 5.8 %collective-permute-done.16 = bf16[96,768]{1,0:T(8,128)(2,1)S(1)} collective-permute-done((bf16[96,768]{1,0:T(8,128)(2,1)S(1)}, bf16[96,768]{1,0:T(8,128)(2,1)S(1)}, u32[]{:S(2)}, u32[]{:S(2)}) %collective-permute-start.16) | collective-permute-done | bytes 147488 | tf_op jit(solution)/shard_map/ppermute | solution.py:250
  155.6 0.8 fusion.3
  (34 shorter events, 0.2 us)
Async XLA Ops:
  0.0 13.6 %copy-start.4 = (s32[512,3]{0,1:T(4,128)S(1)}, s32[512,3]{0,1:T(4,128)}, u32[]{:S(2)}) copy-start(s32[512,3]{0,1:T(4,128)} %param.9) | copy-start | bytes 18436
  2.3 21.7 %copy-start.3 = (s32[64,9]{0,1:T(8,128)S(1)}, s32[64,9]{0,1:T(8,128)}, u32[]{:S(2)}) copy-start(s32[64,9]{0,1:T(8,128)} %param.8) | copy-start | bytes 6916
  2.3 21.7 %collective-permute-start.5 = (bf16[1728,256]{1,0:T(8,128)(2,1)}, bf16[1728,256]{1,0:T(8,128)(2,1)}, u32[]{:S(2)}, u32[]{:S(2)}) collective-permute-start(bf16[1728,256]{1,0:T(8,128)(2,1)} %shard_map.65.s0), channel_id=1, source_target_pairs={{0,2},{1,3},{2,0},{3,1},{4,6},{5,7},{6,4},{7,5},{8,10},{9,11},{10,... | collective-permute-start | bytes 2654216 | tf_op jit(solution)/shard_map/ppermute | solution.py:250
  2.9 45.9 %collective-permute-start.4 = (bf16[1728,256]{1,0:T(8,128)(2,1)}, bf16[1728,256]{1,0:T(8,128)(2,1)}, u32[]{:S(2)}, u32[]{:S(2)}) collective-permute-start(bf16[1728,256]{1,0:T(8,128)(2,1)} %shard_map.65.s0), channel_id=1, source_target_pairs={{0,1},{1,0},{2,3},{3,2},{4,5},{5,4},{6,7},{7,6},{8,9},{9,8},{10,11... | collective-permute-start | bytes 2654216 | tf_op jit(solution)/shard_map/ppermute | solution.py:250
  4.1 29.1 %copy-start.2 = (bf16[64,24,864]{2,1,0:T(8,128)(2,1)S(1)}, bf16[64,24,864]{2,1,0:T(8,128)(2,1)}, u32[]{:S(2)}) copy-start(bf16[64,24,864]{2,1,0:T(8,128)(2,1)} %param.6) | copy-start | bytes 7962628
  7.0 24.2 %collective-permute-start = (bf16[864,256]{1,0:T(8,128)(2,1)}, bf16[864,256]{1,0:T(8,128)(2,1)}, u32[]{:S(2)}, u32[]{:S(2)}) collective-permute-start(bf16[864,256]{1,0:T(8,128)(2,1)} %get-tuple-element.13), channel_id=1, source_target_pairs={{0,4},{1,5},{2,6},{3,7},{4,8},{5,9},{6,10},{7,11},{8,12},{9,13},{1... | collective-permute-start | bytes 1327112 | tf_op jit(solution)/shard_map/ppermute | solution.py:250
  8.3 23.4 %collective-permute-start.9 = (bf16[864,256]{1,0:T(8,128)(2,1)}, bf16[864,256]{1,0:T(8,128)(2,1)}, u32[]{:S(2)}, u32[]{:S(2)}) collective-permute-start(bf16[864,256]{1,0:T(8,128)(2,1)} %get-tuple-element.17), channel_id=1, source_target_pairs={{4,0},{5,1},{6,2},{7,3},{8,4},{9,5},{10,6},{11,7},{12,8},{13,9},{1... | collective-permute-start | bytes 1327112 | tf_op jit(solution)/shard_map/ppermute | solution.py:250
  24.0 29.4 %collective-permute-start.6 = (bf16[1728,256]{1,0:T(8,128)(2,1)}, bf16[1728,256]{1,0:T(8,128)(2,1)}, u32[]{:S(2)}, u32[]{:S(2)}) collective-permute-start(bf16[1728,256]{1,0:T(8,128)(2,1)} %collective-permute-done.5.s2), channel_id=1, source_target_pairs={{0,1},{1,0},{2,3},{3,2},{4,5},{5,4},{6,7},{7,6},{8,9},{9,8},{10,11... | collective-permute-start | bytes 2654216 | tf_op jit(solution)/shard_map/ppermute | solution.py:250
  31.2 13.2 %collective-permute-start.2 = (bf16[864,256]{1,0:T(8,128)(2,1)}, bf16[864,256]{1,0:T(8,128)(2,1)S(1)}, u32[]{:S(2)}, u32[]{:S(2)}) collective-permute-start(bf16[864,256]{1,0:T(8,128)(2,1)} %collective-permute-done.s0), channel_id=1, source_target_pairs={{0,2},{1,3},{2,0},{3,1},{4,6},{5,7},{6,4},{7,5},{8,10},{9,11},{10,... | collective-permute-start | bytes 1327112 | tf_op jit(solution)/shard_map/ppermute | solution.py:250
  31.7 21.8 %collective-permute-start.11 = (bf16[864,256]{1,0:T(8,128)(2,1)}, bf16[864,256]{1,0:T(8,128)(2,1)S(1)}, u32[]{:S(2)}, u32[]{:S(2)}) collective-permute-start(bf16[864,256]{1,0:T(8,128)(2,1)} %collective-permute-done.9.s0), channel_id=1, source_target_pairs={{0,2},{1,3},{2,0},{3,1},{4,6},{5,7},{6,4},{7,5},{8,10},{9,11},{10,... | collective-permute-start | bytes 1327112 | tf_op jit(solution)/shard_map/ppermute | solution.py:250
  35.1 52.2 %collective-permute-start.1 = (bf16[864,256]{1,0:T(8,128)(2,1)}, bf16[864,256]{1,0:T(8,128)(2,1)S(1)}, u32[]{:S(2)}, u32[]{:S(2)}) collective-permute-start(bf16[864,256]{1,0:T(8,128)(2,1)} %collective-permute-done.s0), channel_id=1, source_target_pairs={{0,1},{1,0},{2,3},{3,2},{4,5},{5,4},{6,7},{7,6},{8,9},{9,8},{10,11... | collective-permute-start | bytes 1327112 | tf_op jit(solution)/shard_map/ppermute | solution.py:250
  44.3 4.4 %copy-start.6 = (bf16[864,256]{1,0:T(8,128)(2,1)}, bf16[864,256]{1,0:T(8,128)(2,1)S(1)}, u32[]{:S(2)}) copy-start(bf16[864,256]{1,0:T(8,128)(2,1)S(1)} %collective-permute-done.2.s2) | copy-start | bytes 1327108
  44.3 43.1 %collective-permute-start.3 = (bf16[864,256]{1,0:T(8,128)(2,1)S(1)}, bf16[864,256]{1,0:T(8,128)(2,1)S(1)}, u32[]{:S(2)}, u32[]{:S(2)}) collective-permute-start(bf16[864,256]{1,0:T(8,128)(2,1)S(1)} %collective-permute-done.2.s2), channel_id=1, source_target_pairs={{0,1},{1,0},{2,3},{3,2},{4,5},{5,4},{6,7},{7,6},{8,9},{9,8},{10,11... | collective-permute-start | bytes 1327112 | tf_op jit(solution)/shard_map/ppermute | solution.py:250
  48.8 60.7 %collective-permute-start.10 = (bf16[864,256]{1,0:T(8,128)(2,1)}, bf16[864,256]{1,0:T(8,128)(2,1)S(1)}, u32[]{:S(2)}, u32[]{:S(2)}) collective-permute-start(bf16[864,256]{1,0:T(8,128)(2,1)} %collective-permute-done.9.s0), channel_id=1, source_target_pairs={{0,1},{1,0},{2,3},{3,2},{4,5},{5,4},{6,7},{7,6},{8,9},{9,8},{10,11... | collective-permute-start | bytes 1327112 | tf_op jit(solution)/shard_map/ppermute | solution.py:250
  53.4 33.9 %copy-start.5 = (bf16[864,256]{1,0:T(8,128)(2,1)}, bf16[864,256]{1,0:T(8,128)(2,1)S(1)}, u32[]{:S(2)}) copy-start(bf16[864,256]{1,0:T(8,128)(2,1)S(1)} %collective-permute-done.11.s2) | copy-start | bytes 1327108
  53.4 56.0 %collective-permute-start.12 = (bf16[864,256]{1,0:T(8,128)(2,1)S(1)}, bf16[864,256]{1,0:T(8,128)(2,1)S(1)}, u32[]{:S(2)}, u32[]{:S(2)}) collective-permute-start(bf16[864,256]{1,0:T(8,128)(2,1)S(1)} %collective-permute-done.11.s2), channel_id=1, source_target_pairs={{0,1},{1,0},{2,3},{3,2},{4,5},{5,4},{6,7},{7,6},{8,9},{9,8},{10,11... | collective-permute-start | bytes 1327112 | tf_op jit(solution)/shard_map/ppermute | solution.py:250
  87.4 0.8 copy-start.9
  87.4 0.9 copy-start.10
  109.0 23.5 %collective-permute-start.7 = (bf16[384,768]{1,0:T(8,128)(2,1)}, bf16[384,768]{1,0:T(8,128)(2,1)S(1)}, u32[]{:S(2)}, u32[]{:S(2)}) collective-permute-start(bf16[384,768]{1,0:T(8,128)(2,1)} %get-tuple-element.16), channel_id=1, source_target_pairs={{0,1},{1,0},{2,3},{3,2},{4,5},{5,4},{6,7},{7,6},{8,9},{9,8},{10,11... | collective-permute-start | bytes 1769480 | tf_op jit(solution)/shard_map/ppermute | solution.py:250
  109.4 0.8 copy-start.7
  109.5 0.9 copy-start.8
  110.4 22.1 %copy-start = (f32[384,768]{1,0:T(8,128)S(1)}, f32[384,768]{1,0:T(8,128)}, u32[]{:S(2)}) copy-start(f32[384,768]{1,0:T(8,128)} %get-tuple-element.15) | copy-start | bytes 3538948
  132.3 2.3 %collective-permute-start.13 = (bf16[384,768]{1,0:T(8,128)(2,1)}, bf16[384,768]{1,0:T(8,128)(2,1)S(1)}, u32[]{:S(2)}, u32[]{:S(2)}) collective-permute-start(bf16[384,768]{1,0:T(8,128)(2,1)} %get-tuple-element.20), channel_id=1, source_target_pairs={{0,1},{1,0},{2,3},{3,2},{4,5},{5,4},{6,7},{7,6},{8,9},{9,8},{10,11... | collective-permute-start | bytes 1769480 | tf_op jit(solution)/shard_map/ppermute | solution.py:250
  132.5 2.0 %copy-start.1 = (f32[384,768]{1,0:T(8,128)S(1)}, f32[384,768]{1,0:T(8,128)}, u32[]{:S(2)}) copy-start(f32[384,768]{1,0:T(8,128)} %get-tuple-element.19) | copy-start | bytes 3538948
  132.6 9.9 %collective-permute-start.8 = (bf16[192,768]{1,0:T(8,128)(2,1)S(1)}, bf16[192,768]{1,0:T(8,128)(2,1)S(1)}, u32[]{:S(2)}, u32[]{:S(2)}) collective-permute-start(bf16[192,768]{1,0:T(8,128)(2,1)S(1)} %slice.61), channel_id=1, source_target_pairs={{0,2},{1,3},{2,0},{3,1},{4,6},{5,7},{6,4},{7,5},{8,10},{9,11},{10,... | collective-permute-start | bytes 884744 | tf_op jit(solution)/shard_map/ppermute | solution.py:250
  134.7 13.6 %collective-permute-start.14 = (bf16[192,768]{1,0:T(8,128)(2,1)S(1)}, bf16[192,768]{1,0:T(8,128)(2,1)S(1)}, u32[]{:S(2)}, u32[]{:S(2)}) collective-permute-start(bf16[192,768]{1,0:T(8,128)(2,1)S(1)} %slice.60), channel_id=1, source_target_pairs={{0,2},{1,3},{2,0},{3,1},{4,6},{5,7},{6,4},{7,5},{8,10},{9,11},{10,... | collective-permute-start | bytes 884744 | tf_op jit(solution)/shard_map/ppermute | solution.py:250
  142.6 7.1 %collective-permute-start.15 = (bf16[96,768]{1,0:T(8,128)(2,1)S(1)}, bf16[96,768]{1,0:T(8,128)(2,1)S(1)}, u32[]{:S(2)}, u32[]{:S(2)}) collective-permute-start(bf16[96,768]{1,0:T(8,128)(2,1)S(1)} %slice.63), channel_id=1, source_target_pairs={{0,4},{1,5},{2,6},{3,7},{4,8},{5,9},{6,10},{7,11},{8,12},{9,13},{1... | collective-permute-start | bytes 442376 | tf_op jit(solution)/shard_map/ppermute | solution.py:250
  148.4 7.2 %collective-permute-start.16 = (bf16[96,768]{1,0:T(8,128)(2,1)S(1)}, bf16[96,768]{1,0:T(8,128)(2,1)S(1)}, u32[]{:S(2)}, u32[]{:S(2)}) collective-permute-start(bf16[96,768]{1,0:T(8,128)(2,1)S(1)} %slice.62), channel_id=1, source_target_pairs={{0,4},{1,5},{2,6},{3,7},{4,8},{5,9},{6,10},{7,11},{8,12},{9,13},{1... | collective-permute-start | bytes 442376 | tf_op jit(solution)/shard_map/ppermute | solution.py:250

commit v2 on v0

v2 whole, which is shorter than its diff:
```python
import jax
import jax.numpy as jnp
from jax import lax
from jax.experimental import pallas as pl
from jax.experimental.pallas import tpu as pltpu
from jax.sharding import PartitionSpec as P

BW = 96
BC = 96
KA = 9
KP = 3
NAG = 4
NB = 64
NS = 32
W = 24
ROWS = NB * W
PACK = NS * W + 96
UN = 4
STEPS = NB // UN
AXES = ("dom", "col")
VMEM_LIMIT = 56 * 1024 * 1024
F32, BF16, I32 = jnp.float32, jnp.bfloat16, jnp.int32


def params():
    return pltpu.CompilerParams(vmem_limit_bytes=VMEM_LIMIT)


def cost(microseconds):
    flops = int(microseconds * 1.1e9)
    return pl.CostEstimate(flops=flops, bytes_accessed=10**6, transcendentals=0)


def in_vmem():
    return pl.BlockSpec(memory_space=pltpu.VMEM)


def in_smem():
    return pl.BlockSpec(memory_space=pltpu.SMEM)


def anywhere():
    return pl.BlockSpec(memory_space=pl.ANY)


def window_start(part, parts):
    return jnp.clip((part - 1) * NB, 0, (parts - 3) * NB)


def fill_order(part, halo_ref, order_ref, inverse):
    def step(r, taken):
        here = halo_ref[part, 0, jnp.minimum(taken, NS - 1)]
        is_listed = jnp.logical_and(taken < NS, here == r).astype(I32)
        at = jnp.where(is_listed == 1, taken, NS + r - taken)
        if inverse:
            order_ref[r] = at
        else:
            order_ref[at] = r
        return taken + is_listed

    lax.fori_loop(0, NB, step, jnp.int32(0))


def pack_kernel(place_ref, halo_ref, p_ref, listed_ref, others_ref, up_ref, wide_ref, order_ref):
    part = place_ref[0]
    fill_order(part, halo_ref, order_ref, False)

    def widen(t, carry):
        pair = p_ref[pl.ds(pl.multiple_of(t * 48, 48), 48), :].astype(F32)
        wide_ref[2 * t] = pair[0:24]
        wide_ref[2 * t + 1] = pair[24:48]
        return carry

    lax.fori_loop(0, NB // 2, widen, 0, unroll=4)
    picks = (
        (listed_ref, lambda n: order_ref[n]),
        (others_ref, lambda n: order_ref[NS + n]),
        (up_ref, lambda n: halo_ref[part, 1, n]),
    )
    for out_ref, row_of in picks:
        for g in range(NS // 16):
            tails = []
            for q in range(8):
                t = 8 * g + q
                two = [wide_ref[row_of(2 * t)], wide_ref[row_of(2 * t + 1)]]
                pair = jnp.concatenate(two, axis=0).astype(BF16)
                out_ref[48 * t : 48 * t + 48, :] = pair[:, 0:256]
                tails.append(pair[:, 256:288])
            start = NS * W + 48 * g
            out_ref[start : start + 48, :] = jnp.concatenate(tails, axis=1)


def split96(tiles, lane):
    x0, x1, x2 = tiles
    second = jnp.where(lane < 32, pltpu.roll(x0, 32, 1), pltpu.roll(x1, 32, 1))
    third = jnp.where(lane < 64, pltpu.roll(x1, 64, 1), pltpu.roll(x2, 64, 1))
    return x0, second, third, pltpu.roll(x2, 96, 1)


def prepare_kernel(place_ref, aggs_ref, live_ref, p_ref, a_ref, spread_ref, blocks_ref, wide_ref, *, parts):
    part, col = place_ref[0], place_ref[1]
    own = part * NB - window_start(part, parts)
    lane = lax.broadcasted_iota(I32, (48, 128), 1)
    wide_ref[...] = jnp.zeros_like(wide_ref)

    def pair(t, carry):
        rows = pl.ds(pl.multiple_of(t * 48, 48), 48)
        for g in range(2):
            tiles = [a_ref[rows, 384 * g + 128 * x : 384 * g + 128 * x + 128].astype(F32) for x in range(3)]
            for k, block in enumerate(split96(tiles, lane)):
                blocks_ref[4 * g + k, rows, :] = block.astype(BF16)
        blocks_ref[8, rows, 0:96] = a_ref[rows, 768:864]
        p = p_ref[rows, :].astype(F32)
        x0, x1 = p[:, 0:128], p[:, 128:256]
        tail = jnp.concatenate([p[:, 256:288], jnp.zeros((48, 96), F32)], axis=1)
        blocks = split96((x0, x1, tail), lane)[:3]
        for odd in range(2):
            r = 2 * t + odd
            live = (r < live_ref[0]).astype(F32)
            for m in range(KP):
                block = aggs_ref[own + r, m] - part * NAG
                after = block // NAG
                turn = jnp.bitwise_xor(block - NAG * after, col)
                at = 2 * (3 - (2 * (turn % 2) + turn // 2)) + after
                value = jnp.where(lane < 96, blocks[m], 0.0)[24 * odd : 24 * odd + 24] * live
                wide_ref[at, pl.ds(pl.multiple_of(r * W, 8), W), :] = value
        return carry

    lax.fori_loop(0, NB // 2, pair, 0, unroll=2)
    eye = (
        lax.broadcasted_iota(I32, (BC, 128), 0) == lax.broadcasted_iota(I32, (BC, 128), 1)
    ).astype(F32).astype(BF16)
    for b in range(8):
        for n in range(3):
            flipped = lax.dot_general(
                eye,
                wide_ref[b, 512 * n : 512 * n + 512, :].astype(BF16),
                (((1,), (1,)), ((), ())),
                preferred_element_type=F32,
            )
            spread_ref[BC * b : BC * b + BC, 512 * n : 512 * n + 512] = flipped.astype(BF16)


def unpack(sources, prolong, first):
    lane = lax.broadcasted_iota(I32, (48, 128), 1)

    def group(g, carry):
        tails = []
        for v in range(4):
            rows = pl.ds(pl.multiple_of(NS * W + g * 48, 48), 48)
            tails.append([sources[v, rows, 128 * h : 128 * h + 128].astype(F32) for h in range(2)])
        for q in range(8):
            t = 8 * g + q
            parts = [[], [], []]
            for v in range(4):
                rows = pl.ds(pl.multiple_of(t * 48, 48), 48)
                x0 = sources[v, rows, 0:128].astype(F32)
                x1 = sources[v, rows, 128:256].astype(F32)
                tail, shift = tails[v][q // 4], (64 - 32 * (q % 4)) % 128
                if shift:
                    tail = pltpu.roll(tail, shift, 1)
                parts[0].append(x0)
                parts[1].append(jnp.where(lane < 32, pltpu.roll(x0, 32, 1), pltpu.roll(x1, 32, 1)))
                parts[2].append(jnp.where(lane < 64, pltpu.roll(x1, 64, 1), tail))
            for j in range(KP):
                for odd in range(2):
                    rows = [x[24 * odd : 24 * odd + 24] for x in parts[j]]
                    block = jnp.concatenate(rows, axis=0).astype(BF16)
                    prolong[first + 2 * t + odd, :, 128 * j : 128 * j + 128] = block
        return carry

    lax.fori_loop(0, NS // 16, group, 0)


def fetches(refs, scratch, sems, col):
    return [
        pltpu.make_async_copy(ref, scratch.at[jnp.bitwise_xor(col, s)], sems.at[s])
        for s, ref in enumerate(refs)
    ]


def add_products(step, slots, a_ref, first_slot, prolong, row_of, blocks_of, sums):
    for slot in slots:
        for u in range(UN):
            i = UN * step + u
            odd = u % 2
            start = pl.multiple_of(step * (UN * W) + 48 * (u // 2) + 16 * odd, 16)
            at = row_of(i, slot)
            got = jnp.dot(
                a_ref[slot - first_slot, pl.ds(start, 32), 0:BW], prolong[at[0]], preferred_element_type=F32
            )[8 * odd : 8 * odd + 24]
            where = blocks_of(at[1])
            held = [sums[u][step, c] for c in where]
            for j in range(KP):
                sums[u][step, where[j]] = held[j] + got[:, 128 * j : 128 * j + 128]


def own_kernel(place_ref, halo_ref, aggs_ref, cols_ref, *refs, parts):
    listed, others, a_hbm, out_hbm = refs[0:4], refs[4:8], refs[8], refs[9]
    sources, prolong, a_ref, s0, s1, s2, s3, order_ref, in_sems, a_sem, out_sems = refs[10:]
    sums = (s0, s1, s2, s3)
    part, col = place_ref[0], place_ref[1]
    own = part * NB - window_start(part, parts)
    base = part * NAG
    copies = [
        fetches(listed, sources.at[0], in_sems.at[0], col),
        fetches(others, sources.at[1], in_sems.at[1], col),
    ]
    a_copy = pltpu.make_async_copy(a_hbm, a_ref, a_sem)
    for copy in copies[0] + copies[1]:
        copy.start()
    a_copy.start()
    fill_order(part, halo_ref, order_ref, True)
    for each in sums:
        each[...] = jnp.zeros_like(each)
    for half in range(2):
        for copy in copies[half]:
            copy.wait()
        unpack(sources.at[half], prolong, NS * half)
    a_copy.wait()

    def row_of(i, slot):
        row = cols_ref[i, slot]
        if slot < 5:
            row = row - part * NB
        return order_ref[row], row

    def blocks_of(row):
        return [aggs_ref[own + row, j] - base for j in range(KP)]

    def run(slots, first, count):
        def step(n, carry):
            add_products(first + n, slots, a_ref, 0, prolong, row_of, blocks_of, sums)
            return carry

        lax.fori_loop(0, count, step, 0)

    @pl.when(part == 0)
    def _():
        run((5, 6), 0, STEPS)

    @pl.when(part == parts - 1)
    def _():
        run((7, 8), 0, STEPS)

    leaving = []
    for chunk in range(4):
        run((0, 1, 2, 3, 4), 4 * chunk, 4)
        for u in range(UN):
            copy = pltpu.make_async_copy(
                sums[u].at[4 * chunk : 4 * chunk + 4],
                out_hbm.at[u, 4 * chunk : 4 * chunk + 4],
                out_sems.at[chunk, u],
            )
            copy.start()
            leaving.append(copy)
    for copy in leaving:
        copy.wait()


def halo_kernel(place_ref, halo_ref, aggs_ref, cols_ref, *refs, parts, upper):
    packed, a_hbm, own_hbm, spread_hbm, send_ref, keep_ref = refs[0:4], *refs[4:9]
    sources, prolong, a_ref, s0, s1, s2, s3, spread, coupled, in_sems, own_sems, sems = refs[9:]
    sums = (s0, s1, s2, s3)
    part, col = place_ref[0], place_ref[1]
    first_slot = 7 if upper else 5
    other = jnp.minimum(part + 1, parts - 1) if upper else jnp.maximum(part - 1, 0)
    rows_at = other * NB - window_start(part, parts)
    own_at, new_at = (0, NAG) if upper else (NAG, 0)
    copies = fetches(packed, sources, in_sems, col)
    a_copy = pltpu.make_async_copy(a_hbm.at[first_slot : first_slot + 2], a_ref, sems.at[0])
    spread_copy = pltpu.make_async_copy(spread_hbm, spread, sems.at[1])
    own_copies = [
        pltpu.make_async_copy(
            own_hbm.at[u, :, (NAG if upper else 0) : (NAG if upper else 0) + NAG],
            sums[u].at[:, own_at : own_at + NAG],
            own_sems.at[u],
        )
        for u in range(UN)
    ]
    for copy in copies + [a_copy] + own_copies + [spread_copy]:
        copy.start()
    for each in sums:
        each[:, new_at : new_at + NAG] = jnp.zeros((STEPS, NAG, W, 128), F32)
    for copy in copies:
        copy.wait()
    unpack(sources, prolong, 0)
    for copy in [a_copy] + own_copies:
        copy.wait()
    lane = lax.broadcasted_iota(I32, (48, 128), 1)

    def row_of(i, slot):
        at = cols_ref[i, slot]
        return at, rows_at + halo_ref[other, 0 if upper else 1, at]

    def blocks_of(row):
        return [aggs_ref[row, j] - other * NAG for j in range(KP)]

    def step(n, carry):
        add_products(n, (first_slot, first_slot + 1), a_ref, first_slot, prolong, row_of, blocks_of, sums)
        for two in range(2):
            rows = pl.ds(pl.multiple_of(n * (UN * W) + 48 * two, 48), 48)
            for half in range(2):
                y0, y1, y2, y3 = [
                    jnp.concatenate([sums[2 * two][n, c], sums[2 * two + 1][n, c]], axis=0)
                    for c in range(4 * half, 4 * half + 4)
                ]
                y1, y2, y3 = pltpu.roll(y1, 96, 1), pltpu.roll(y2, 64, 1), pltpu.roll(y3, 32, 1)
                tiles = [
                    jnp.where(lane < 96, y0, y1),
                    jnp.where(lane < 64, y1, y2),
                    jnp.where(lane < 32, y2, y3),
                ]
                for x in range(3):
                    at = 384 * half + 128 * x
                    coupled[rows, at : at + 128] = tiles[x].astype(BF16)
        return carry

    lax.fori_loop(0, STEPS, step, 0)
    spread_copy.wait()
    for n in range(3):
        at = slice(256 * n, 256 * n + 256)
        for half, out_ref in ((0, send_ref), (1, keep_ref)):
            got = jnp.dot(
                spread[384 * half : 384 * half + 384, :], coupled[:, at], preferred_element_type=F32
            )
            out_ref[:, at] = got.astype(out_ref.dtype)


def local(a_vals, p_vals, a_cols, p_aggs, halo_rows, live_rows):
    part = lax.axis_index("dom")
    parts = lax.axis_size("dom")
    col = lax.axis_index("col")
    cols_count = lax.axis_size("col")
    devices = [(d, c) for d in range(parts) for c in range(cols_count)]

    def moved(x, step, flip):
        route = [
            (d * cols_count + c, (d + step) * cols_count + (c ^ flip))
            for d, c in devices
            if 0 <= d + step < parts
        ]
        return lax.ppermute(x, AXES, route)

    place = jnp.stack([part, col]).astype(I32)
    p_flat = p_vals.reshape(ROWS, KP * BC)
    a_flat = a_vals.reshape(ROWS, KA * BW)
    packed = jax.ShapeDtypeStruct((PACK, 256), BF16)
    listed, others, upward = pl.pallas_call(
        pack_kernel,
        out_shape=[packed] * 3,
        in_specs=[in_smem(), in_smem(), in_vmem()],
        out_specs=[in_vmem()] * 3,
        scratch_shapes=[pltpu.VMEM((NB, W, KP * BC), F32), pltpu.SMEM((NB,), I32)],
        compiler_params=params(),
        cost_estimate=cost(4),
    )(place, halo_rows, p_flat)

    near_listed = moved(listed, 0, 2)
    near_others = moved(others, 0, 2)
    low = moved(upward, 1, 0)
    up = moved(listed, -1, 0)
    up_far = moved(near_listed, -1, 0)
    low_far = moved(low, 0, 2)

    def both_cores(x, far):
        return (x, moved(x, 0, 1), far, moved(far, 0, 1))

    aggs = lax.dynamic_slice_in_dim(p_aggs, window_start(part, parts), 3 * NB, 0)
    spread, blocks = pl.pallas_call(
        lambda *refs: prepare_kernel(*refs, parts=parts),
        out_shape=[
            jax.ShapeDtypeStruct((8 * BC, ROWS), BF16),
            jax.ShapeDtypeStruct((KA, ROWS, 128), BF16),
        ],
        in_specs=[in_smem()] * 3 + [in_vmem()] * 2,
        out_specs=[in_vmem(), in_vmem()],
        scratch_shapes=[pltpu.VMEM((8, ROWS, 128), F32)],
        compiler_params=params(),
        cost_estimate=cost(9),
    )(place, aggs, live_rows, p_flat, a_flat)

    sums_scratch = [pltpu.VMEM((STEPS, 8, W, 128), F32)] * UN
    own = pl.pallas_call(
        lambda *refs: own_kernel(*refs, parts=parts),
        out_shape=jax.ShapeDtypeStruct((UN, STEPS, 8, W, 128), F32),
        in_specs=[in_smem()] * 4 + [anywhere()] * 9,
        out_specs=anywhere(),
        scratch_shapes=[
            pltpu.VMEM((2, 4, PACK, 256), BF16),
            pltpu.VMEM((NB, BW, KP * 128), BF16),
            pltpu.VMEM((KA, ROWS, 128), BF16),
            *sums_scratch,
            pltpu.SMEM((NB,), I32),
            pltpu.SemaphoreType.DMA((2, 4)),
            pltpu.SemaphoreType.DMA,
            pltpu.SemaphoreType.DMA((4, UN)),
        ],
        compiler_params=params(),
        cost_estimate=cost(10),
    )(place, halo_rows, aggs, a_cols, *both_cores(listed, near_listed), *both_cores(others, near_others), blocks)

    def halo_terms(upper, sources):
        return pl.pallas_call(
            lambda *refs: halo_kernel(*refs, parts=parts, upper=upper),
            out_shape=[
                jax.ShapeDtypeStruct((4 * BC, 8 * BC), BF16),
                jax.ShapeDtypeStruct((4 * BC, 8 * BC), F32),
            ],
            in_specs=[in_smem()] * 4 + [anywhere()] * 7,
            out_specs=[in_vmem(), in_vmem()],
            scratch_shapes=[
                pltpu.VMEM((4, PACK, 256), BF16),
                pltpu.VMEM((NS, BW, KP * 128), BF16),
                pltpu.VMEM((2, ROWS, 128), BF16),
                *sums_scratch,
                pltpu.VMEM((8 * BC, ROWS), BF16),
                pltpu.VMEM((ROWS, 8 * BC), BF16),
                pltpu.SemaphoreType.DMA((4,)),
                pltpu.SemaphoreType.DMA((UN,)),
                pltpu.SemaphoreType.DMA((2,)),
            ],
            compiler_params=params(),
            cost_estimate=cost(8),
        )(place, halo_rows, aggs, a_cols, *sources, blocks, own, spread)

    def summed(send, keep):
        both = keep + moved(send, 0, 1).astype(F32)
        away = both.astype(BF16)
        far_own = moved(away[0:BC], 0, 2)
        far_next = moved(away[BC : 2 * BC], 1, 2)
        near_next = moved(away[3 * BC :], 1, 0)
        mine = both[2 * BC : 3 * BC] + far_own.astype(F32)
        return mine, far_next.astype(F32) + near_next.astype(F32)

    low_own, low_next = summed(*halo_terms(False, both_cores(low, low_far)))
    up_own, up_next = summed(*halo_terms(True, both_cores(up, up_far)))
    band = NAG * BC
    mine = jnp.concatenate([low_own, up_own], axis=1)
    came = jnp.concatenate([low_next, up_next], axis=1)
    result = jnp.pad(mine, ((0, 0), (band, 0))) + jnp.pad(came, ((0, 0), (0, band)))
    return result.astype(BF16)


def solution(mesh):
    in_specs = (P("dom", "col", None), P("dom", "col", None), P("dom", None), P(), P(), P("dom"))
    out_specs = P(("dom", "col"), None)
    return jax.shard_map(local, mesh=mesh, in_specs=in_specs, out_specs=out_specs, check_vma=False)
```

time: 952 us -> 118 us (0.12)
  matrix products: 448 us -> 0 us
  waiting for transfers between devices: 290 us -> 18 us
  local copies, waits for them, and re-layouts: 182 us -> 4.11 us
  Pallas kernels: 0 us -> 56.9 us
  starting transfers between devices: 10.1 us -> 35.1 us
  between operations: 14.7 us -> 0.97 us
    dot_general x26 -> x0, matrix products: 448 us -> none  [the longest x8 340 us: add_rows(): jnp.einsum('imj,imbx->jbx', k_piece, term, precision=HIGH)]
    ppermute x3 -> x22, waiting for transfers between devices: 206 us -> 18 us  [moved(): return lax.ppermute(x, AXES, route)]
    gather x17 -> x0, local copies, waits for them, and re-layouts: 80.4 us -> none  [the longest x9 75.5 us: local(): fetched = jnp.take(extended, slab_row[:, slot], axis=0)]
    pallas_call x0 -> x5, Pallas kernels: none -> 56.9 us  [the longest x2 29.8 us: halo_terms(): pl.pallas_call(lambda *refs: halo_kernel(*refs, parts=parts, upper=upper)...]
    reduce_scatter x1 -> x0, waiting for transfers between devices: 48.1 us -> none  [local(): lax.psum_scatter(partial_value.reshape(2, band, 4 * band), 'col', scatter...]
    reshape x2 -> x0, local copies, waits for them, and re-layouts: 36.1 us -> none  [the longest x1 32.3 us: local(): stacked = jnp.stack(products, axis=2).reshape(NB, slice_rows, KA * KP, BC)]
    all_gather x1 -> x0, waiting for transfers between devices: 35.5 us -> none  [local(): p_full = lax.all_gather(p_vals, 'col', axis=1, tiled=True)]
    another operation x1 -> x0, local copies, waits for them, and re-layouts: 30.4 us -> none  [local(): stacked = jnp.stack(products, axis=2).reshape(NB, slice_rows, KA * KP, BC)]
  transfers between devices with their start and end apart: 5 -> 22, of which waited for: 4 -> 6; matrix products, arithmetic and copies ran while one was open for 2% -> 2% of each run, Pallas kernels for 0% -> 45%
where the time goes in v2:
time: 118 us; the launch traced here: 117 us
  Pallas kernels  56.9 us (48%)
  starting transfers between devices  35.1 us (30%)
  waiting for transfers between devices  18 us (15%)
  local copies, waits for them, and re-layouts  4.11 us (3%)
  other arithmetic  1.85 us (2%)
    ppermute x22, starting transfers between devices, moved(): return lax.ppermute(x, AXES, route)  35.1 us
    pallas_call x2, Pallas kernels, halo_terms(): pl.pallas_call(lambda *refs: halo_kernel(*refs, parts=parts, upper=upper)...  29.8 us
    ppermute x22, waiting for transfers between devices, moved(): return lax.ppermute(x, AXES, route)  18 us
    pallas_call x1, Pallas kernels, local(): pl.pallas_call(lambda *refs: own_kernel(*refs, parts=parts), out_shape=ja...  14.9 us
    pallas_call x1, Pallas kernels, local(): pl.pallas_call(lambda *refs: prepare_kernel(*refs, parts=parts), out_shap...  8.47 us
    unnamed x34, local copies, waits for them, and re-layouts  3.97 us
    pallas_call x1, Pallas kernels, local(): pl.pallas_call(pack_kernel, out_shape=[packed] * 3, in_specs=[in_smem(),...  3.8 us
  transfers between devices with their start and end apart: 22, of which 6 were waited for; matrix products, arithmetic and copies ran while one was open for 2% of the time, Pallas kernels for 45%

profile of v2, /device:TPU:16, one launch (start us, length us, event | category | flops | bytes accessed | tf_op | source)
XLA Modules:
  0.0 117.0 jit_solution(9703256093205219554)
XLA Ops:
  0.0 0.6 pad_add_fusion.place_ref.refs_0_
  0.7 3.8 %shard_map.64 = (bf16[864,256]{1,0:T(8,128)(2,1)}, bf16[864,256]{1,0:T(8,128)(2,1)}, bf16[864,256]{1,0:T(8,128)(2,1)}) custom-call(s32[2]{0:T(128)} %pad_add_fusion.place_ref.refs_0_, s32[8,2,32]{2,1,0:T(2,128)} %refs_1_.5, bf16[1536,288]{1,0:T(8,128)(2,1)} %bitcast.5), custom_call_target="tpu_custom_call" | custom-call | flops 4400000000 | bytes 1000000 | tf_op jit(solution)/shard_map/pallas_call | solution.py:349
  4.5 1.5 %collective-permute-start.5 = (bf16[864,256]{1,0:T(8,128)(2,1)}, bf16[864,256]{1,0:T(8,128)(2,1)S(1)}, u32[]{:S(2)}, u32[]{:S(2)}) collective-permute-start(bf16[864,256]{1,0:T(8,128)(2,1)} %get-tuple-element.16.refs_4_), channel_id=1, source_target_pairs={{0,2},{1,3},{2,0},{3,1},{4,6},{5,7},{6,4},{7,5},{8,10},{9,11},{10,... | collective-permute-start | bytes 1327112 | tf_op jit(solution)/shard_map/ppermute | solution.py:343
  6.0 0.5 collective-permute-start.8
  6.5 0.0 collective-permute-start.4
  6.5 0.5 collective-permute-start.7
  7.0 3.4 %collective-permute-start = (bf16[864,256]{1,0:T(8,128)(2,1)}, bf16[864,256]{1,0:T(8,128)(2,1)S(1)}, u32[]{:S(2)}, u32[]{:S(2)}) collective-permute-start(bf16[864,256]{1,0:T(8,128)(2,1)} %get-tuple-element.14), channel_id=1, source_target_pairs={{0,4},{1,5},{2,6},{3,7},{4,8},{5,9},{6,10},{7,11},{8,12},{9,13},{1... | collective-permute-start | bytes 1327112 | tf_op jit(solution)/shard_map/ppermute | solution.py:343
  10.4 0.1 constant_dynamic-slice_fusion
  10.5 0.8 copy.11.refs_1_.refs_2_
  11.9 5.8 %collective-permute-done.5.refs_6_ = bf16[864,256]{1,0:T(8,128)(2,1)S(1)} collective-permute-done((bf16[864,256]{1,0:T(8,128)(2,1)}, bf16[864,256]{1,0:T(8,128)(2,1)S(1)}, u32[]{:S(2)}, u32[]{:S(2)}) %collective-permute-start.5) | collective-permute-done | bytes 442400 | tf_op jit(solution)/shard_map/ppermute | solution.py:343
  17.7 3.3 %collective-permute-start.12 = (bf16[864,256]{1,0:T(8,128)(2,1)}, bf16[864,256]{1,0:T(8,128)(2,1)S(1)}, u32[]{:S(2)}, u32[]{:S(2)}) collective-permute-start(bf16[864,256]{1,0:T(8,128)(2,1)} %get-tuple-element.16.refs_4_), channel_id=1, source_target_pairs={{4,0},{5,1},{6,2},{7,3},{8,4},{9,5},{10,6},{11,7},{12,8},{13,9},{1... | collective-permute-start | bytes 1327112 | tf_op jit(solution)/shard_map/ppermute | solution.py:343
  21.0 5.0 %collective-permute-done.8.refs_10_ = bf16[864,256]{1,0:T(8,128)(2,1)S(1)} collective-permute-done((bf16[864,256]{1,0:T(8,128)(2,1)}, bf16[864,256]{1,0:T(8,128)(2,1)S(1)}, u32[]{:S(2)}, u32[]{:S(2)}) %collective-permute-start.8) | collective-permute-done | bytes 442400 | tf_op jit(solution)/shard_map/ppermute | solution.py:343
  26.1 0.0 collective-permute-start.6
  26.1 0.0 collective-permute-done.4.refs_5_
  26.1 3.3 %collective-permute-start.14 = (bf16[864,256]{1,0:T(8,128)(2,1)S(1)}, bf16[864,256]{1,0:T(8,128)(2,1)S(1)}, u32[]{:S(2)}, u32[]{:S(2)}) collective-permute-start(bf16[864,256]{1,0:T(8,128)(2,1)S(1)} %collective-permute-done.5.refs_6_), channel_id=1, source_target_pairs={{4,0},{5,1},{6,2},{7,3},{8,4},{9,5},{10,6},{11,7},{12,8},{13,9},{1... | collective-permute-start | bytes 1327112 | tf_op jit(solution)/shard_map/ppermute | solution.py:343
  29.4 0.0 collective-permute-done.7.refs_9_
  29.4 0.3 collective-permute-start.9
  29.7 0.0 collective-permute-done.refs_4_
  29.7 1.5 %collective-permute-start.2 = (bf16[864,256]{1,0:T(8,128)(2,1)S(1)}, bf16[864,256]{1,0:T(8,128)(2,1)}, u32[]{:S(2)}, u32[]{:S(2)}) collective-permute-start(bf16[864,256]{1,0:T(8,128)(2,1)S(1)} %collective-permute-done.refs_4_), channel_id=1, source_target_pairs={{0,2},{1,3},{2,0},{3,1},{4,6},{5,7},{6,4},{7,5},{8,10},{9,11},{10,... | collective-permute-start | bytes 1327112 | tf_op jit(solution)/shard_map/ppermute | solution.py:343
  31.2 8.5 %shard_map.65 = (bf16[768,1536]{1,0:T(8,128)(2,1)}, bf16[9,1536,128]{2,1,0:T(8,128)(2,1)}) custom-call(s32[2]{0:T(128)} %pad_add_fusion.place_ref.refs_0_, s32[192,3]{1,0:T(8,128)} %copy.11.refs_1_.refs_2_, s32[1]{0:T(128)S(6)} %copy.12.refs_2_, bf16[1536,288]{1,0:T(8,128)(2,1)} %bitcast.6, bf16[1536,864]{1,0:T(8,128)(2,1)} %bitcast.4), custom_call_target="tpu_custom_call" | custom-call | flops 9900000256 | bytes 1000000 | tf_op jit(solution)/shard_map/pallas_call | solution.py:370
  39.7 0.0 copy-done.4
  39.7 0.7 copy.9.refs_3_
  40.4 0.0 collective-permute-done.12.refs_4_
  40.4 0.1 collective-permute-start.1
  40.5 0.0 collective-permute-done.6.refs_7_
  40.5 0.5 collective-permute-start.13
  41.0 1.2 %collective-permute-done.2.refs_6_ = bf16[864,256]{1,0:T(8,128)(2,1)} collective-permute-done((bf16[864,256]{1,0:T(8,128)(2,1)S(1)}, bf16[864,256]{1,0:T(8,128)(2,1)}, u32[]{:S(2)}, u32[]{:S(2)}) %collective-permute-start.2) | collective-permute-done | bytes 442400 | tf_op jit(solution)/shard_map/ppermute | solution.py:343
  42.1 0.0 collective-permute-start.3
  42.2 0.0 collective-permute-done.14.refs_6_
  42.2 0.5 collective-permute-start.15
  42.7 0.0 collective-permute-done.9.refs_11_
  42.7 0.0 copy-done.11
  42.7 14.9 %shard_map.66.refs_9_ = f32[4,16,8,24,128]{4,3,2,1,0:T(8,128)} custom-call(s32[2]{0:T(128)} %pad_add_fusion.place_ref.refs_0_, s32[8,2,32]{2,1,0:T(2,128)} %refs_1_.5, s32[192,3]{1,0:T(8,128)} %copy.11.refs_1_.refs_2_, s32[64,9]{1,0:T(8,128)} %copy.9.refs_3_, bf16[864,256]{1,0:T(8,128)(2,1)} %get-tuple-element.16.refs_4_, bf16[864,256]{1,0:T(8,128)(2,1)} %copy-done.7, ...), custom_call_target="tpu_custom_call" | custom-call | flops 11000000512 | bytes 1000000 | tf_op jit(solution)/shard_map/pallas_call | solution.py:384
  57.6 0.0 copy-done.8
  57.6 0.0 copy-done.10
  57.6 0.0 collective-permute-done.1.refs_5_
  57.6 0.0 collective-permute-done.3.refs_7_
  57.6 0.7 copy-done.14
  58.4 0.1 copy-done.15
  58.5 14.9 %shard_map.67 = (bf16[384,768]{1,0:T(8,128)(2,1)}, f32[384,768]{1,0:T(8,128)}) custom-call(s32[2]{0:T(128)} %pad_add_fusion.place_ref.refs_0_, s32[8,2,32]{2,1,0:T(2,128)} %refs_1_.5, s32[192,3]{1,0:T(8,128)} %copy.11.refs_1_.refs_2_, s32[64,9]{1,0:T(8,128)} %copy.9.refs_3_, bf16[864,256]{1,0:T(8,128)(2,1)} %copy-done.5, bf16[864,256]{1,0:T(8,128)(2,1)} %copy-done.14, ...), custom_call_target="tpu_custom_call" | custom-call | flops 8800000000 | bytes 1000000 | tf_op jit(solution)/shard_map/pallas_call | solution.py:404
  73.4 0.1 collective-permute-start.10
  73.5 0.0 collective-permute-done.13.refs_5_
  73.5 0.0 collective-permute-done.15.refs_7_
  73.6 0.8 copy-done.12
  74.3 0.8 copy-done.13
  75.1 14.9 %shard_map.68 = (bf16[384,768]{1,0:T(8,128)(2,1)}, f32[384,768]{1,0:T(8,128)}) custom-call(s32[2]{0:T(128)} %pad_add_fusion.place_ref.refs_0_, s32[8,2,32]{2,1,0:T(2,128)} %refs_1_.5, s32[192,3]{1,0:T(8,128)} %copy.11.refs_1_.refs_2_, s32[64,9]{1,0:T(8,128)} %copy.9.refs_3_, bf16[864,256]{1,0:T(8,128)(2,1)} %copy-done.8, bf16[864,256]{1,0:T(8,128)(2,1)} %copy-done.12, ...), custom_call_target="tpu_custom_call" | custom-call | flops 8800000000 | bytes 1000000 | tf_op jit(solution)/shard_map/pallas_call | solution.py:404
  90.0 0.5 collective-permute-start.16
  90.5 0.0 collective-permute-done.10
  90.5 0.1 fusion.2
  90.7 1.6 %collective-permute-start.11 = (bf16[96,768]{1,0:T(8,128)(2,1)S(1)}, bf16[96,768]{1,0:T(8,128)(2,1)S(1)}, u32[]{:S(2)}, u32[]{:S(2)}) collective-permute-start(bf16[96,768]{1,0:T(8,128)(2,1)S(1)} %get-tuple-element.27), channel_id=1, source_target_pairs={{0,2},{1,3},{2,0},{3,1},{4,6},{5,7},{6,4},{7,5},{8,10},{9,11},{10,... | collective-permute-start | bytes 442376 | tf_op jit(solution)/shard_map/ppermute | solution.py:343
  92.3 0.1 collective-permute-done.16
  92.4 0.2 fusion.3
  92.6 1.6 %collective-permute-start.17 = (bf16[96,768]{1,0:T(8,128)(2,1)S(1)}, bf16[96,768]{1,0:T(8,128)(2,1)S(1)}, u32[]{:S(2)}, u32[]{:S(2)}) collective-permute-start(bf16[96,768]{1,0:T(8,128)(2,1)S(1)} %get-tuple-element.30), channel_id=1, source_target_pairs={{0,2},{1,3},{2,0},{3,1},{4,6},{5,7},{6,4},{7,5},{8,10},{9,11},{10,... | collective-permute-start | bytes 442376 | tf_op jit(solution)/shard_map/ppermute | solution.py:343
  94.2 2.5 %collective-permute-start.18 = (bf16[96,768]{1,0:T(8,128)(2,1)S(1)}, bf16[96,768]{1,0:T(8,128)(2,1)S(1)}, u32[]{:S(2)}, u32[]{:S(2)}) collective-permute-start(bf16[96,768]{1,0:T(8,128)(2,1)S(1)} %get-tuple-element.29), channel_id=1, source_target_pairs={{0,6},{1,7},{2,4},{3,5},{4,10},{5,11},{6,8},{7,9},{8,14},{9,15},{1... | collective-permute-start | bytes 442376 | tf_op jit(solution)/shard_map/ppermute | solution.py:343
  96.7 4.3 %collective-permute-start.19 = (bf16[96,768]{1,0:T(8,128)(2,1)S(1)}, bf16[96,768]{1,0:T(8,128)(2,1)S(1)}, u32[]{:S(2)}, u32[]{:S(2)}) collective-permute-start(bf16[96,768]{1,0:T(8,128)(2,1)S(1)} %get-tuple-element.28), channel_id=1, source_target_pairs={{0,4},{1,5},{2,6},{3,7},{4,8},{5,9},{6,10},{7,11},{8,12},{9,13},{1... | collective-permute-start | bytes 442376 | tf_op jit(solution)/shard_map/ppermute | solution.py:343
  101.0 7.2 %collective-permute-start.20 = (bf16[96,768]{1,0:T(8,128)(2,1)S(1)}, bf16[96,768]{1,0:T(8,128)(2,1)S(1)}, u32[]{:S(2)}, u32[]{:S(2)}) collective-permute-start(bf16[96,768]{1,0:T(8,128)(2,1)S(1)} %get-tuple-element.32), channel_id=1, source_target_pairs={{0,6},{1,7},{2,4},{3,5},{4,10},{5,11},{6,8},{7,9},{8,14},{9,15},{1... | collective-permute-start | bytes 442376 | tf_op jit(solution)/shard_map/ppermute | solution.py:343
  108.2 0.0 collective-permute-done.11
  108.2 1.9 %collective-permute-start.21 = (bf16[96,768]{1,0:T(8,128)(2,1)S(1)}, bf16[96,768]{1,0:T(8,128)(2,1)S(1)}, u32[]{:S(2)}, u32[]{:S(2)}) collective-permute-start(bf16[96,768]{1,0:T(8,128)(2,1)S(1)} %get-tuple-element.31), channel_id=1, source_target_pairs={{0,4},{1,5},{2,6},{3,7},{4,8},{5,9},{6,10},{7,11},{8,12},{9,13},{1... | collective-permute-start | bytes 442376 | tf_op jit(solution)/shard_map/ppermute | solution.py:343
  110.2 0.0 collective-permute-done.17
  110.3 0.0 collective-permute-done.18
  110.3 0.0 collective-permute-done.19
  110.3 2.0 %collective-permute-done.20 = bf16[96,768]{1,0:T(8,128)(2,1)S(1)} collective-permute-done((bf16[96,768]{1,0:T(8,128)(2,1)S(1)}, bf16[96,768]{1,0:T(8,128)(2,1)S(1)}, u32[]{:S(2)}, u32[]{:S(2)}) %collective-permute-start.20) | collective-permute-done | bytes 147488 | tf_op jit(solution)/shard_map/ppermute | solution.py:343
  112.3 3.9 %collective-permute-done.21 = bf16[96,768]{1,0:T(8,128)(2,1)S(1)} collective-permute-done((bf16[96,768]{1,0:T(8,128)(2,1)S(1)}, bf16[96,768]{1,0:T(8,128)(2,1)S(1)}, u32[]{:S(2)}, u32[]{:S(2)}) %collective-permute-start.21) | collective-permute-done | bytes 147488 | tf_op jit(solution)/shard_map/ppermute | solution.py:343
  116.2 0.8 fusion.1
  (30 shorter events, 0.2 us)
Async XLA Ops:
  0.0 10.4 %copy-start = (s32[512,3]{0,1:T(4,128)S(1)}, s32[512,3]{0,1:T(4,128)}, u32[]{:S(2)}) copy-start(s32[512,3]{0,1:T(4,128)} %param.9) | copy-start | bytes 18436
  4.5 13.3 %collective-permute-start.5 = (bf16[864,256]{1,0:T(8,128)(2,1)}, bf16[864,256]{1,0:T(8,128)(2,1)S(1)}, u32[]{:S(2)}, u32[]{:S(2)}) collective-permute-start(bf16[864,256]{1,0:T(8,128)(2,1)} %get-tuple-element.16.refs_4_), channel_id=1, source_target_pairs={{0,2},{1,3},{2,0},{3,1},{4,6},{5,7},{6,4},{7,5},{8,10},{9,11},{10,... | collective-permute-start | bytes 1327112 | tf_op jit(solution)/shard_map/ppermute | solution.py:343
  6.0 20.1 %collective-permute-start.8 = (bf16[864,256]{1,0:T(8,128)(2,1)}, bf16[864,256]{1,0:T(8,128)(2,1)S(1)}, u32[]{:S(2)}, u32[]{:S(2)}) collective-permute-start(bf16[864,256]{1,0:T(8,128)(2,1)} %get-tuple-element.17.refs_8_), channel_id=1, source_target_pairs={{0,2},{1,3},{2,0},{3,1},{4,6},{5,7},{6,4},{7,5},{8,10},{9,11},{10,... | collective-permute-start | bytes 1327112 | tf_op jit(solution)/shard_map/ppermute | solution.py:343
  6.5 19.6 %collective-permute-start.4 = (bf16[864,256]{1,0:T(8,128)(2,1)}, bf16[864,256]{1,0:T(8,128)(2,1)S(1)}, u32[]{:S(2)}, u32[]{:S(2)}) collective-permute-start(bf16[864,256]{1,0:T(8,128)(2,1)} %get-tuple-element.16.refs_4_), channel_id=1, source_target_pairs={{0,1},{1,0},{2,3},{3,2},{4,5},{5,4},{6,7},{7,6},{8,9},{9,8},{10,11... | collective-permute-start | bytes 1327112 | tf_op jit(solution)/shard_map/ppermute | solution.py:343
  6.5 22.9 %collective-permute-start.7 = (bf16[864,256]{1,0:T(8,128)(2,1)}, bf16[864,256]{1,0:T(8,128)(2,1)S(1)}, u32[]{:S(2)}, u32[]{:S(2)}) collective-permute-start(bf16[864,256]{1,0:T(8,128)(2,1)} %get-tuple-element.17.refs_8_), channel_id=1, source_target_pairs={{0,1},{1,0},{2,3},{3,2},{4,5},{5,4},{6,7},{7,6},{8,9},{9,8},{10,11... | collective-permute-start | bytes 1327112 | tf_op jit(solution)/shard_map/ppermute | solution.py:343
  7.0 22.7 %collective-permute-start = (bf16[864,256]{1,0:T(8,128)(2,1)}, bf16[864,256]{1,0:T(8,128)(2,1)S(1)}, u32[]{:S(2)}, u32[]{:S(2)}) collective-permute-start(bf16[864,256]{1,0:T(8,128)(2,1)} %get-tuple-element.14), channel_id=1, source_target_pairs={{0,4},{1,5},{2,6},{3,7},{4,8},{5,9},{6,10},{7,11},{8,12},{9,13},{1... | collective-permute-start | bytes 1327112 | tf_op jit(solution)/shard_map/ppermute | solution.py:343
  17.7 21.9 %copy-start.4 = (bf16[864,256]{1,0:T(8,128)(2,1)}, bf16[864,256]{1,0:T(8,128)(2,1)S(1)}, u32[]{:S(2)}) copy-start(bf16[864,256]{1,0:T(8,128)(2,1)S(1)} %collective-permute-done.5.refs_6_) | copy-start | bytes 1327108
  17.7 22.7 %collective-permute-start.12 = (bf16[864,256]{1,0:T(8,128)(2,1)}, bf16[864,256]{1,0:T(8,128)(2,1)S(1)}, u32[]{:S(2)}, u32[]{:S(2)}) collective-permute-start(bf16[864,256]{1,0:T(8,128)(2,1)} %get-tuple-element.16.refs_4_), channel_id=1, source_target_pairs={{4,0},{5,1},{6,2},{7,3},{8,4},{9,5},{10,6},{11,7},{12,8},{13,9},{1... | collective-permute-start | bytes 1327112 | tf_op jit(solution)/shard_map/ppermute | solution.py:343
  26.1 13.6 %copy-start.6 = (bf16[864,256]{1,0:T(8,128)(2,1)}, bf16[864,256]{1,0:T(8,128)(2,1)S(1)}, u32[]{:S(2)}) copy-start(bf16[864,256]{1,0:T(8,128)(2,1)S(1)} %collective-permute-done.8.refs_10_) | copy-start | bytes 1327108
  26.1 14.4 %collective-permute-start.6 = (bf16[864,256]{1,0:T(8,128)(2,1)S(1)}, bf16[864,256]{1,0:T(8,128)(2,1)S(1)}, u32[]{:S(2)}, u32[]{:S(2)}) collective-permute-start(bf16[864,256]{1,0:T(8,128)(2,1)S(1)} %collective-permute-done.5.refs_6_), channel_id=1, source_target_pairs={{0,1},{1,0},{2,3},{3,2},{4,5},{5,4},{6,7},{7,6},{8,9},{9,8},{10,11... | collective-permute-start | bytes 1327112 | tf_op jit(solution)/shard_map/ppermute | solution.py:343
  26.1 13.6 %copy-start.7 = (bf16[864,256]{1,0:T(8,128)(2,1)}, bf16[864,256]{1,0:T(8,128)(2,1)S(1)}, u32[]{:S(2)}) copy-start(bf16[864,256]{1,0:T(8,128)(2,1)S(1)} %collective-permute-done.4.refs_5_) | copy-start | bytes 1327108
  26.1 16.1 %collective-permute-start.14 = (bf16[864,256]{1,0:T(8,128)(2,1)S(1)}, bf16[864,256]{1,0:T(8,128)(2,1)S(1)}, u32[]{:S(2)}, u32[]{:S(2)}) collective-permute-start(bf16[864,256]{1,0:T(8,128)(2,1)S(1)} %collective-permute-done.5.refs_6_), channel_id=1, source_target_pairs={{4,0},{5,1},{6,2},{7,3},{8,4},{9,5},{10,6},{11,7},{12,8},{13,9},{1... | collective-permute-start | bytes 1327112 | tf_op jit(solution)/shard_map/ppermute | solution.py:343
  29.4 10.3 %copy-start.9 = (bf16[864,256]{1,0:T(8,128)(2,1)}, bf16[864,256]{1,0:T(8,128)(2,1)S(1)}, u32[]{:S(2)}) copy-start(bf16[864,256]{1,0:T(8,128)(2,1)S(1)} %collective-permute-done.7.refs_9_) | copy-start | bytes 1327108
  29.4 13.3 %collective-permute-start.9 = (bf16[864,256]{1,0:T(8,128)(2,1)S(1)}, bf16[864,256]{1,0:T(8,128)(2,1)}, u32[]{:S(2)}, u32[]{:S(2)}) collective-permute-start(bf16[864,256]{1,0:T(8,128)(2,1)S(1)} %collective-permute-done.8.refs_10_), channel_id=1, source_target_pairs={{0,1},{1,0},{2,3},{3,2},{4,5},{5,4},{6,7},{7,6},{8,9},{9,8},{10,11... | collective-permute-start | bytes 1327112 | tf_op jit(solution)/shard_map/ppermute | solution.py:343
  29.7 10.7 %copy-start.5 = (bf16[864,256]{1,0:T(8,128)(2,1)}, bf16[864,256]{1,0:T(8,128)(2,1)S(1)}, u32[]{:S(2)}) copy-start(bf16[864,256]{1,0:T(8,128)(2,1)S(1)} %collective-permute-done.refs_4_) | copy-start | bytes 1327108
  29.7 12.5 %collective-permute-start.2 = (bf16[864,256]{1,0:T(8,128)(2,1)S(1)}, bf16[864,256]{1,0:T(8,128)(2,1)}, u32[]{:S(2)}, u32[]{:S(2)}) collective-permute-start(bf16[864,256]{1,0:T(8,128)(2,1)S(1)} %collective-permute-done.refs_4_), channel_id=1, source_target_pairs={{0,2},{1,3},{2,0},{3,1},{4,6},{5,7},{6,4},{7,5},{8,10},{9,11},{10,... | collective-permute-start | bytes 1327112 | tf_op jit(solution)/shard_map/ppermute | solution.py:343
  31.2 8.5 %copy-start.3 = (s32[64,9]{0,1:T(8,128)S(1)}, s32[64,9]{0,1:T(8,128)}, u32[]{:S(2)}) copy-start(s32[64,9]{0,1:T(8,128)} %param.8) | copy-start | bytes 6916
  40.4 17.2 %copy-start.8 = (bf16[864,256]{1,0:T(8,128)(2,1)}, bf16[864,256]{1,0:T(8,128)(2,1)S(1)}, u32[]{:S(2)}) copy-start(bf16[864,256]{1,0:T(8,128)(2,1)S(1)} %collective-permute-done.12.refs_4_) | copy-start | bytes 1327108
  40.4 17.2 %collective-permute-start.1 = (bf16[864,256]{1,0:T(8,128)(2,1)S(1)}, bf16[864,256]{1,0:T(8,128)(2,1)S(1)}, u32[]{:S(2)}, u32[]{:S(2)}) collective-permute-start(bf16[864,256]{1,0:T(8,128)(2,1)S(1)} %collective-permute-done.refs_4_), channel_id=1, source_target_pairs={{0,1},{1,0},{2,3},{3,2},{4,5},{5,4},{6,7},{7,6},{8,9},{9,8},{10,11... | collective-permute-start | bytes 1327112 | tf_op jit(solution)/shard_map/ppermute | solution.py:343
  40.5 2.2 %copy-start.11 = (bf16[864,256]{1,0:T(8,128)(2,1)}, bf16[864,256]{1,0:T(8,128)(2,1)S(1)}, u32[]{:S(2)}) copy-start(bf16[864,256]{1,0:T(8,128)(2,1)S(1)} %collective-permute-done.6.refs_7_) | copy-start | bytes 1327108
  40.5 33.1 %collective-permute-start.13 = (bf16[864,256]{1,0:T(8,128)(2,1)S(1)}, bf16[864,256]{1,0:T(8,128)(2,1)S(1)}, u32[]{:S(2)}, u32[]{:S(2)}) collective-permute-start(bf16[864,256]{1,0:T(8,128)(2,1)S(1)} %collective-permute-done.12.refs_4_), channel_id=1, source_target_pairs={{0,1},{1,0},{2,3},{3,2},{4,5},{5,4},{6,7},{7,6},{8,9},{9,8},{10,11... | collective-permute-start | bytes 1327112 | tf_op jit(solution)/shard_map/ppermute | solution.py:343
  42.1 15.4 %collective-permute-start.3 = (bf16[864,256]{1,0:T(8,128)(2,1)}, bf16[864,256]{1,0:T(8,128)(2,1)S(1)}, u32[]{:S(2)}, u32[]{:S(2)}) collective-permute-start(bf16[864,256]{1,0:T(8,128)(2,1)} %collective-permute-done.2.refs_6_), channel_id=1, source_target_pairs={{0,1},{1,0},{2,3},{3,2},{4,5},{5,4},{6,7},{7,6},{8,9},{9,8},{10,11... | collective-permute-start | bytes 1327112 | tf_op jit(solution)/shard_map/ppermute | solution.py:343
  42.2 15.4 %copy-start.10 = (bf16[864,256]{1,0:T(8,128)(2,1)}, bf16[864,256]{1,0:T(8,128)(2,1)S(1)}, u32[]{:S(2)}) copy-start(bf16[864,256]{1,0:T(8,128)(2,1)S(1)} %collective-permute-done.14.refs_6_) | copy-start | bytes 1327108
  42.2 31.4 %collective-permute-start.15 = (bf16[864,256]{1,0:T(8,128)(2,1)S(1)}, bf16[864,256]{1,0:T(8,128)(2,1)S(1)}, u32[]{:S(2)}, u32[]{:S(2)}) collective-permute-start(bf16[864,256]{1,0:T(8,128)(2,1)S(1)} %collective-permute-done.14.refs_6_), channel_id=1, source_target_pairs={{0,1},{1,0},{2,3},{3,2},{4,5},{5,4},{6,7},{7,6},{8,9},{9,8},{10,11... | collective-permute-start | bytes 1327112 | tf_op jit(solution)/shard_map/ppermute | solution.py:343
  57.6 0.8 copy-start.14
  57.6 0.9 copy-start.15
  73.4 17.1 %copy-start.2 = (f32[384,768]{1,0:T(8,128)S(1)}, f32[384,768]{1,0:T(8,128)}, u32[]{:S(2)}) copy-start(f32[384,768]{1,0:T(8,128)} %get-tuple-element.19) | copy-start | bytes 3538948
  73.4 17.1 %collective-permute-start.10 = (bf16[384,768]{1,0:T(8,128)(2,1)}, bf16[384,768]{1,0:T(8,128)(2,1)S(1)}, u32[]{:S(2)}, u32[]{:S(2)}) collective-permute-start(bf16[384,768]{1,0:T(8,128)(2,1)} %get-tuple-element.20), channel_id=1, source_target_pairs={{0,1},{1,0},{2,3},{3,2},{4,5},{5,4},{6,7},{7,6},{8,9},{9,8},{10,11... | collective-permute-start | bytes 1769480 | tf_op jit(solution)/shard_map/ppermute | solution.py:343
  73.5 0.8 copy-start.12
  74.3 0.8 copy-start.13
  90.0 2.3 %collective-permute-start.16 = (bf16[384,768]{1,0:T(8,128)(2,1)}, bf16[384,768]{1,0:T(8,128)(2,1)S(1)}, u32[]{:S(2)}, u32[]{:S(2)}) collective-permute-start(bf16[384,768]{1,0:T(8,128)(2,1)} %get-tuple-element.22), channel_id=1, source_target_pairs={{0,1},{1,0},{2,3},{3,2},{4,5},{5,4},{6,7},{7,6},{8,9},{9,8},{10,11... | collective-permute-start | bytes 1769480 | tf_op jit(solution)/shard_map/ppermute | solution.py:343
  90.5 1.8 %copy-start.1 = (f32[384,768]{1,0:T(8,128)S(1)}, f32[384,768]{1,0:T(8,128)}, u32[]{:S(2)}) copy-start(f32[384,768]{1,0:T(8,128)} %get-tuple-element.21) | copy-start | bytes 3538948
  90.7 17.5 %collective-permute-start.11 = (bf16[96,768]{1,0:T(8,128)(2,1)S(1)}, bf16[96,768]{1,0:T(8,128)(2,1)S(1)}, u32[]{:S(2)}, u32[]{:S(2)}) collective-permute-start(bf16[96,768]{1,0:T(8,128)(2,1)S(1)} %get-tuple-element.27), channel_id=1, source_target_pairs={{0,2},{1,3},{2,0},{3,1},{4,6},{5,7},{6,4},{7,5},{8,10},{9,11},{10,... | collective-permute-start | bytes 442376 | tf_op jit(solution)/shard_map/ppermute | solution.py:343
  92.6 17.7 %collective-permute-start.17 = (bf16[96,768]{1,0:T(8,128)(2,1)S(1)}, bf16[96,768]{1,0:T(8,128)(2,1)S(1)}, u32[]{:S(2)}, u32[]{:S(2)}) collective-permute-start(bf16[96,768]{1,0:T(8,128)(2,1)S(1)} %get-tuple-element.30), channel_id=1, source_target_pairs={{0,2},{1,3},{2,0},{3,1},{4,6},{5,7},{6,4},{7,5},{8,10},{9,11},{10,... | collective-permute-start | bytes 442376 | tf_op jit(solution)/shard_map/ppermute | solution.py:343
  94.2 16.1 %collective-permute-start.18 = (bf16[96,768]{1,0:T(8,128)(2,1)S(1)}, bf16[96,768]{1,0:T(8,128)(2,1)S(1)}, u32[]{:S(2)}, u32[]{:S(2)}) collective-permute-start(bf16[96,768]{1,0:T(8,128)(2,1)S(1)} %get-tuple-element.29), channel_id=1, source_target_pairs={{0,6},{1,7},{2,4},{3,5},{4,10},{5,11},{6,8},{7,9},{8,14},{9,15},{1... | collective-permute-start | bytes 442376 | tf_op jit(solution)/shard_map/ppermute | solution.py:343
  96.7 13.6 %collective-permute-start.19 = (bf16[96,768]{1,0:T(8,128)(2,1)S(1)}, bf16[96,768]{1,0:T(8,128)(2,1)S(1)}, u32[]{:S(2)}, u32[]{:S(2)}) collective-permute-start(bf16[96,768]{1,0:T(8,128)(2,1)S(1)} %get-tuple-element.28), channel_id=1, source_target_pairs={{0,4},{1,5},{2,6},{3,7},{4,8},{5,9},{6,10},{7,11},{8,12},{9,13},{1... | collective-permute-start | bytes 442376 | tf_op jit(solution)/shard_map/ppermute | solution.py:343
  101.0 11.3 %collective-permute-start.20 = (bf16[96,768]{1,0:T(8,128)(2,1)S(1)}, bf16[96,768]{1,0:T(8,128)(2,1)S(1)}, u32[]{:S(2)}, u32[]{:S(2)}) collective-permute-start(bf16[96,768]{1,0:T(8,128)(2,1)S(1)} %get-tuple-element.32), channel_id=1, source_target_pairs={{0,6},{1,7},{2,4},{3,5},{4,10},{5,11},{6,8},{7,9},{8,14},{9,15},{1... | collective-permute-start | bytes 442376 | tf_op jit(solution)/shard_map/ppermute | solution.py:343
  108.2 7.9 %collective-permute-start.21 = (bf16[96,768]{1,0:T(8,128)(2,1)S(1)}, bf16[96,768]{1,0:T(8,128)(2,1)S(1)}, u32[]{:S(2)}, u32[]{:S(2)}) collective-permute-start(bf16[96,768]{1,0:T(8,128)(2,1)S(1)} %get-tuple-element.31), channel_id=1, source_target_pairs={{0,4},{1,5},{2,6},{3,7},{4,8},{5,9},{6,10},{7,11},{8,12},{9,13},{1... | collective-permute-start | bytes 442376 | tf_op jit(solution)/shard_map/ppermute | solution.py:343

commit v3 on v2

v3 whole, which is shorter than its diff:
```python
import jax
import jax.numpy as jnp
from jax import lax
from jax.experimental import pallas as pl
from jax.experimental.pallas import tpu as pltpu
from jax.sharding import PartitionSpec as P

BW = 96
BC = 96
KA = 9
KP = 3
NAG = 4
NB = 64
NS = 32
W = 24
ROWS = NB * W
UN = 4
STEPS = NB // UN
AXES = ("dom", "col")
VMEM_LIMIT = 16 * 1024 * 1024
F32, BF16, I32 = jnp.float32, jnp.bfloat16, jnp.int32


def params():
    return pltpu.CompilerParams(vmem_limit_bytes=VMEM_LIMIT)


def cost(microseconds):
    flops = int(microseconds * 1.1e9)
    return pl.CostEstimate(flops=flops, bytes_accessed=10**6, transcendentals=0)


def in_vmem():
    return pl.BlockSpec(memory_space=pltpu.VMEM)


def in_smem():
    return pl.BlockSpec(memory_space=pltpu.SMEM)


def window_start(part, parts):
    return jnp.clip((part - 1) * NB, 0, (parts - 3) * NB)


def packed(count):
    return jax.ShapeDtypeStruct((count * W + count * W // 8, 256), BF16)


def pack_own_kernel(p_ref, out_ref):
    out_ref[0:ROWS, :] = p_ref[:, 0:256]
    for g in range(NB // 16):
        tails = [p_ref[48 * (8 * g + q) : 48 * (8 * g + q) + 48, 256:288] for q in range(8)]
        out_ref[ROWS + 48 * g : ROWS + 48 * g + 48, :] = jnp.concatenate(tails, axis=1)


def pack_rows(wide_ref, row_of, out_ref):
    for g in range(NS // 16):
        tails = []
        for q in range(8):
            t = 8 * g + q
            two = [wide_ref[row_of(2 * t + odd)] for odd in range(2)]
            pair = jnp.concatenate(two, axis=0).astype(BF16)
            out_ref[48 * t : 48 * t + 48, :] = pair[:, 0:256]
            tails.append(pair[:, 256:288])
        start = NS * W + 48 * g
        out_ref[start : start + 48, :] = jnp.concatenate(tails, axis=1)


def pack_halo_kernel(place_ref, halo_ref, p_ref, down_ref, up_ref, wide_ref):
    part = place_ref[0]

    def widen(t, carry):
        pair = p_ref[pl.ds(pl.multiple_of(t * 48, 48), 48), :].astype(F32)
        wide_ref[2 * t] = pair[0:24]
        wide_ref[2 * t + 1] = pair[24:48]
        return carry

    lax.fori_loop(0, NB // 2, widen, 0, unroll=4)
    pack_rows(wide_ref, lambda n: halo_ref[part, 1, n], up_ref)
    pack_rows(wide_ref, lambda n: halo_ref[part, 0, n], down_ref)


def select_kernel(place_ref, halo_ref, packed_ref, down_ref, wide_ref):
    part = place_ref[0]

    def widen(g, carry):
        tail = packed_ref[pl.ds(pl.multiple_of(ROWS + g * 48, 48), 48), :].astype(F32)
        for q in range(8):
            t = 8 * g + q
            pair = packed_ref[pl.ds(pl.multiple_of(t * 48, 48), 48), :].astype(F32)
            for odd in range(2):
                rows = slice(24 * odd, 24 * odd + 24)
                wide_ref[2 * t + odd, :, 0:256] = pair[rows]
                wide_ref[2 * t + odd, :, 256:288] = tail[rows, 32 * q : 32 * q + 32]
        return carry

    lax.fori_loop(0, NB // 16, widen, 0)
    pack_rows(wide_ref, lambda n: halo_ref[part, 0, n], down_ref)


def prepare_kernel(place_ref, aggs_ref, live_ref, p_ref, a_ref, spread_ref, blocks_ref, wide_ref, *, parts):
    part, col = place_ref[0], place_ref[1]
    own = part * NB - window_start(part, parts)
    lane = lax.broadcasted_iota(I32, (48, 128), 1)
    wide_ref[...] = jnp.zeros_like(wide_ref)
    to = lax.broadcasted_iota(I32, (256, 128), 1)
    come = W * jnp.bitwise_xor(to // W, col) + to % W
    at = lax.broadcasted_iota(I32, (256, 128), 0)

    def one_hot(shift):
        return jnp.logical_and(at == come + shift, to < BW).astype(F32).astype(BF16)

    for k in range(KA):
        start = BW * k // 128 * 128
        stop = min(start + 256, KA * BW)
        pick = one_hot(BW * k - start)[0 : stop - start]
        for n in range(3):
            rows = slice(512 * n, 512 * n + 512)
            got = jnp.dot(a_ref[rows, start:stop], pick, preferred_element_type=F32)
            blocks_ref[k, rows, :] = got.astype(BF16)

    def pair(t, carry):
        rows = pl.ds(pl.multiple_of(t * 48, 48), 48)
        p = p_ref[rows, :].astype(F32)
        x0, x1 = p[:, 0:128], p[:, 128:256]
        tail = jnp.concatenate([p[:, 256:288], jnp.zeros((48, 96), F32)], axis=1)
        blocks = (
            x0,
            jnp.where(lane < 32, pltpu.roll(x0, 32, 1), pltpu.roll(x1, 32, 1)),
            jnp.where(lane < 64, pltpu.roll(x1, 64, 1), pltpu.roll(tail, 64, 1)),
        )
        for odd in range(2):
            r = 2 * t + odd
            live = (r < live_ref[0]).astype(F32)
            for m in range(KP):
                block = aggs_ref[KP * (own + r) + m] - part * NAG
                after = block // NAG
                turn = jnp.bitwise_xor(block - NAG * after, col)
                place = 2 * (3 - (2 * (turn % 2) + turn // 2)) + after
                value = jnp.where(lane < 96, blocks[m], 0.0)[24 * odd : 24 * odd + 24] * live
                wide_ref[place, pl.ds(pl.multiple_of(r * W, 8), W), :] = value
        return carry

    lax.fori_loop(0, NB // 2, pair, 0, unroll=2)
    eye = (
        lax.broadcasted_iota(I32, (BC, 128), 0) == lax.broadcasted_iota(I32, (BC, 128), 1)
    ).astype(F32).astype(BF16)
    for b in range(8):
        for n in range(3):
            flipped = lax.dot_general(
                eye,
                wide_ref[b, 512 * n : 512 * n + 512, :].astype(BF16),
                (((1,), (1,)), ((), ())),
                preferred_element_type=F32,
            )
            spread_ref[BC * b : BC * b + BC, 512 * n : 512 * n + 512] = flipped.astype(BF16)


def unpack(count, sources, prolong):
    lane = lax.broadcasted_iota(I32, (48, 128), 1)

    def group(g, carry):
        tails = []
        for source in sources:
            rows = pl.ds(pl.multiple_of(count * W + g * 48, 48), 48)
            tails.append([source[rows, 128 * h : 128 * h + 128].astype(F32) for h in range(2)])
        for q in range(8):
            t = 8 * g + q
            parts = [[], [], []]
            for v, source in enumerate(sources):
                rows = pl.ds(pl.multiple_of(t * 48, 48), 48)
                x0 = source[rows, 0:128].astype(F32)
                x1 = source[rows, 128:256].astype(F32)
                tail, shift = tails[v][q // 4], (64 - 32 * (q % 4)) % 128
                if shift:
                    tail = pltpu.roll(tail, shift, 1)
                parts[0].append(x0)
                parts[1].append(jnp.where(lane < 32, pltpu.roll(x0, 32, 1), pltpu.roll(x1, 32, 1)))
                parts[2].append(jnp.where(lane < 64, pltpu.roll(x1, 64, 1), tail))
            for j in range(KP):
                for odd in range(2):
                    rows = [x[24 * odd : 24 * odd + 24] for x in parts[j]]
                    block = jnp.concatenate(rows, axis=0).astype(BF16)
                    prolong[2 * t + odd, :, 128 * j : 128 * j + 128] = block
        return carry

    lax.fori_loop(0, count // 16, group, 0)


def add_products(step, slots, a_ref, prolong, row_of, blocks_of, sums):
    for slot in slots:
        for u in range(UN):
            i = UN * step + u
            odd = u % 2
            start = pl.multiple_of(step * (UN * W) + 48 * (u // 2) + 16 * odd, 16)
            at = row_of(i, slot)
            got = jnp.dot(
                a_ref[slot, pl.ds(start, 32), 0:BW], prolong[at[0]], preferred_element_type=F32
            )[8 * odd : 8 * odd + 24]
            where = blocks_of(at[1])
            held = [sums[u][step, c] for c in where]
            for j in range(KP):
                sums[u][step, where[j]] = held[j] + got[:, 128 * j : 128 * j + 128]


def own_kernel(place_ref, aggs_ref, cols_ref, *refs, parts):
    sources, a_ref, sums, prolong = refs[0:4], refs[4], refs[5:9], refs[9]
    part = place_ref[0]
    own = part * NB - window_start(part, parts)
    base = part * NAG
    unpack(NB, sources, prolong)

    def row_of(i, slot):
        row = cols_ref[KA * i + slot]
        if slot < 5:
            row = row - part * NB
        return row, row

    def blocks_of(row):
        return [aggs_ref[KP * (own + row) + j] - base for j in range(KP)]

    def run(slots, fresh):
        def step(n, carry):
            if fresh:
                for each in sums:
                    each[n] = jnp.zeros((8, W, 128), F32)
            add_products(n, slots, a_ref, prolong, row_of, blocks_of, sums)
            return carry

        lax.fori_loop(0, STEPS, step, 0, unroll=2 if fresh else 1)

    run((0, 1, 2, 3, 4), True)

    @pl.when(part == 0)
    def _():
        run((5, 6), False)

    @pl.when(part == parts - 1)
    def _():
        run((7, 8), False)


def halo_kernel(place_ref, halo_ref, aggs_ref, cols_ref, *refs, parts, upper):
    sources, a_ref, own, spread, send_ref, keep_ref = refs[0:4], refs[4], refs[5:9], *refs[9:12]
    prolong, sums, coupled = refs[12], refs[13:17], refs[17]
    part = place_ref[0]
    slots = (7, 8) if upper else (5, 6)
    other = jnp.minimum(part + 1, parts - 1) if upper else jnp.maximum(part - 1, 0)
    rows_at = other * NB - window_start(part, parts)
    inside = part < parts - 1 if upper else part > 0

    @pl.when(inside)
    def _():
        unpack(NS, sources, prolong)

    lane = lax.broadcasted_iota(I32, (48, 128), 1)

    def row_of(i, slot):
        at = cols_ref[KA * i + slot]
        return at, rows_at + halo_ref[other, 0 if upper else 1, at]

    def blocks_of(row):
        return [aggs_ref[KP * row + j] - other * NAG for j in range(KP)]

    def sum_of(n, u, c):
        if upper:
            return sums[u][n, c] + own[u][n, NAG + c] if c < NAG else sums[u][n, c]
        return sums[u][n, c] + own[u][n, c - NAG] if c >= NAG else sums[u][n, c]

    def run(products):
        def step(n, carry):
            for each in sums:
                each[n] = jnp.zeros((8, W, 128), F32)
            if products:
                add_products(n, slots, a_ref, prolong, row_of, blocks_of, sums)
            for two in range(2):
                rows = pl.ds(pl.multiple_of(n * (UN * W) + 48 * two, 48), 48)
                for half in range(2):
                    y0, y1, y2, y3 = [
                        jnp.concatenate([sum_of(n, 2 * two, c), sum_of(n, 2 * two + 1, c)], axis=0)
                        for c in range(4 * half, 4 * half + 4)
                    ]
                    y1, y2, y3 = pltpu.roll(y1, 96, 1), pltpu.roll(y2, 64, 1), pltpu.roll(y3, 32, 1)
                    tiles = [
                        jnp.where(lane < 96, y0, y1),
                        jnp.where(lane < 64, y1, y2),
                        jnp.where(lane < 32, y2, y3),
                    ]
                    for x in range(3):
                        at = 384 * half + 128 * x
                        coupled[rows, at : at + 128] = tiles[x].astype(BF16)
            return carry

        lax.fori_loop(0, STEPS, step, 0, unroll=2 if products else 1)

    @pl.when(inside)
    def _():
        run(True)

    @pl.when(jnp.logical_not(inside))
    def _():
        run(False)

    for n in range(3):
        at = slice(256 * n, 256 * n + 256)
        for half, out_ref in ((0, send_ref), (1, keep_ref)):
            got = jnp.dot(
                spread[384 * half : 384 * half + 384, :], coupled[:, at], preferred_element_type=F32
            )
            out_ref[:, at] = got.astype(out_ref.dtype)


def local(a_vals, p_vals, a_cols, p_aggs, halo_rows, live_rows):
    part = lax.axis_index("dom")
    parts = lax.axis_size("dom")
    col = lax.axis_index("col")
    cols_count = lax.axis_size("col")
    devices = [(d, c) for d in range(parts) for c in range(cols_count)]

    def moved(x, step, flip):
        route = [
            (d * cols_count + c, (d + step) * cols_count + (c ^ flip))
            for d, c in devices
            if 0 <= d + step < parts
        ]
        return lax.ppermute(x, AXES, route)

    place = jnp.stack([part, col]).astype(I32)
    p_flat = p_vals.reshape(ROWS, KP * BC)
    a_flat = a_vals.reshape(ROWS, KA * BW)
    own_pack = pl.pallas_call(
        pack_own_kernel,
        out_shape=packed(NB),
        in_specs=[in_vmem()],
        out_specs=in_vmem(),
        compiler_params=params(),
        cost_estimate=cost(2),
    )(p_flat)
    near = moved(own_pack, 0, 2)
    down, upward = pl.pallas_call(
        pack_halo_kernel,
        out_shape=[packed(NS)] * 2,
        in_specs=[in_smem(), in_smem(), in_vmem()],
        out_specs=[in_vmem()] * 2,
        scratch_shapes=[pltpu.VMEM((NB, W, KP * BC), F32)],
        compiler_params=params(),
        cost_estimate=cost(3),
    )(place, halo_rows, p_flat)
    low = moved(upward, 1, 0)
    up = moved(down, -1, 0)

    def both_cores(x, far):
        return (x, moved(x, 0, 1), far, moved(far, 0, 1))

    aggs = lax.dynamic_slice_in_dim(p_aggs, window_start(part, parts), 3 * NB, 0).reshape(3 * NB * KP)
    cols = a_cols.reshape(NB * KA)
    spread, blocks = pl.pallas_call(
        lambda *refs: prepare_kernel(*refs, parts=parts),
        out_shape=[
            jax.ShapeDtypeStruct((8 * BC, ROWS), BF16),
            jax.ShapeDtypeStruct((KA, ROWS, 128), BF16),
        ],
        in_specs=[in_smem()] * 3 + [in_vmem()] * 2,
        out_specs=[in_vmem()] * 2,
        scratch_shapes=[pltpu.VMEM((8, ROWS, 128), F32)],
        compiler_params=params(),
        cost_estimate=cost(9),
    )(place, aggs, live_rows, p_flat, a_flat)
    near, low, spread, blocks = lax.optimization_barrier((near, low, spread, blocks))
    low_far = moved(low, 0, 2)
    up_far = moved(
        pl.pallas_call(
            select_kernel,
            out_shape=packed(NS),
            in_specs=[in_smem(), in_smem(), in_vmem()],
            out_specs=in_vmem(),
            scratch_shapes=[pltpu.VMEM((NB, W, KP * BC), F32)],
            compiler_params=params(),
            cost_estimate=cost(3),
        )(place, halo_rows, near),
        -1,
        0,
    )

    sums_type = jax.ShapeDtypeStruct((STEPS, 8, W, 128), F32)
    own = pl.pallas_call(
        lambda *refs: own_kernel(*refs, parts=parts),
        out_shape=[sums_type] * UN,
        in_specs=[in_smem()] * 3 + [in_vmem()] * 5,
        out_specs=[in_vmem()] * UN,
        scratch_shapes=[pltpu.VMEM((NB, BW, KP * 128), BF16)],
        compiler_params=params(),
        cost_estimate=cost(10),
    )(place, aggs, cols, *both_cores(own_pack, near), blocks)
    up_far, low_far, first_sums = lax.optimization_barrier((up_far, low_far, own[0]))
    own = (first_sums, *own[1:])

    def halo_terms(upper, sources):
        return pl.pallas_call(
            lambda *refs: halo_kernel(*refs, parts=parts, upper=upper),
            out_shape=[
                jax.ShapeDtypeStruct((4 * BC, 8 * BC), BF16),
                jax.ShapeDtypeStruct((4 * BC, 8 * BC), F32),
            ],
            in_specs=[in_smem()] * 4 + [in_vmem()] * (6 + UN),
            out_specs=[in_vmem(), in_vmem()],
            scratch_shapes=[
                pltpu.VMEM((NS, BW, KP * 128), BF16),
                *[pltpu.VMEM((STEPS, 8, W, 128), F32)] * UN,
                pltpu.VMEM((ROWS, 8 * BC), BF16),
            ],
            compiler_params=params(),
            cost_estimate=cost(8),
        )(place, halo_rows, aggs, cols, *sources, blocks, *own, spread)

    low_send, low_keep = halo_terms(False, both_cores(low, low_far))
    low_came = moved(low_send, 0, 1)
    up_send, up_keep = halo_terms(True, both_cores(up, up_far))
    low_came, up_send, up_keep = lax.optimization_barrier((low_came, up_send, up_keep))
    up_came = moved(up_send, 0, 1)
    low_both = low_keep + low_came.astype(F32)
    low_mine = low_both[2 * BC :] + moved(low_both[: 2 * BC].astype(BF16), 0, 2).astype(F32)
    up_both = up_keep + up_came.astype(F32)
    away = up_both.astype(BF16)
    far_own = moved(away[0:BC], 0, 2)
    far_next = moved(away[BC : 2 * BC], 1, 2)
    near_next = moved(jnp.concatenate([low_mine[BC:].astype(BF16), away[3 * BC :]], axis=0), 1, 0)
    low_own, low_next = low_mine[:BC], near_next[:BC].astype(F32)
    up_own = up_both[2 * BC : 3 * BC] + far_own.astype(F32)
    up_next = near_next[BC:].astype(F32) + far_next.astype(F32)
    band = NAG * BC
    mine = jnp.concatenate([low_own, up_own], axis=1)
    came = jnp.concatenate([low_next, up_next], axis=1)
    result = jnp.pad(mine, ((0, 0), (band, 0))) + jnp.pad(came, ((0, 0), (0, band)))
    return result.astype(BF16)


def solution(mesh):
    in_specs = (P("dom", "col", None), P("dom", "col", None), P("dom", None), P(), P(), P("dom"))
    out_specs = P(("dom", "col"), None)
    return jax.shard_map(local, mesh=mesh, in_specs=in_specs, out_specs=out_specs, check_vma=False)
```

time: 118 us -> 91.7 us (0.78)
  Pallas kernels: 56.9 us -> 34.9 us
  starting transfers between devices: 35.1 us -> 23.7 us
  waiting for transfers between devices: 18 us -> 22.2 us
  local copies, waits for them, and re-layouts: 4.11 us -> 7.7 us
    pallas_call x2, Pallas kernels: 29.8 us -> 14.2 us  [halo_terms(): pl.pallas_call(lambda *refs: halo_kernel(*refs, parts=parts, upper=upper)...]
    ppermute x22 -> x17, starting transfers between devices: 35.1 us -> 23.7 us  [moved(): return lax.ppermute(x, AXES, route)]
    pallas_call x2 -> x4, Pallas kernels: 18.7 us -> 13.6 us  [the longest x1 8.85 us: local(): pl.pallas_call(lambda *refs: own_kernel(*refs, parts=parts), out_shape=[s...]
    ppermute x22 -> x17, waiting for transfers between devices: 18 us -> 22.2 us  [moved(): return lax.ppermute(x, AXES, route)]
    unnamed x34 -> x25, local copies, waits for them, and re-layouts: 3.97 us -> 7.09 us
    pallas_call x1, Pallas kernels: 8.47 us -> 7.08 us  [local(): pl.pallas_call(lambda *refs: prepare_kernel(*refs, parts=parts), out_shap...]
  transfers between devices with their start and end apart: 22 -> 17, of which waited for: 6 -> 6; matrix products, arithmetic and copies ran while one was open for 2% -> 1% of each run, Pallas kernels for 45% -> 37%
where the time goes in v3:
time: 91.7 us; the launch traced here: 90.8 us
  Pallas kernels  34.9 us (38%)
  starting transfers between devices  23.7 us (26%)
  waiting for transfers between devices  22.2 us (24%)
  local copies, waits for them, and re-layouts  7.7 us (8%)
  other arithmetic  1.29 us (1%)
  between operations  0.97 us (1%)
    ppermute x17, starting transfers between devices, moved(): return lax.ppermute(x, AXES, route)  23.7 us
    ppermute x17, waiting for transfers between devices, moved(): return lax.ppermute(x, AXES, route)  22.2 us
    pallas_call x2, Pallas kernels, halo_terms(): pl.pallas_call(lambda *refs: halo_kernel(*refs, parts=parts, upper=upper)...  14.2 us
    pallas_call x1, Pallas kernels, local(): pl.pallas_call(lambda *refs: own_kernel(*refs, parts=parts), out_shape=[s...  8.85 us
    unnamed x25, local copies, waits for them, and re-layouts  7.09 us
    pallas_call x1, Pallas kernels, local(): pl.pallas_call(lambda *refs: prepare_kernel(*refs, parts=parts), out_shap...  7.08 us
    pallas_call x1, Pallas kernels, local(): pl.pallas_call(pack_halo_kernel, out_shape=[packed(NS)] * 2, in_specs=[in...  1.95 us
  transfers between devices with their start and end apart: 17, of which 6 were waited for; matrix products, arithmetic and copies ran while one was open for 1% of the time, Pallas kernels for 37%

profile of v3, /device:TPU:16, one launch (start us, length us, event | category | flops | bytes accessed | tf_op | source)
XLA Modules:
  0.0 90.8 jit_solution(1147668653111584447)
XLA Ops:
  0.0 0.0 copy-start
  0.0 1.3 %copy-done.2 = bf16[64,24,288]{2,1,0:T(8,128)(2,1)S(1)} copy-done((bf16[64,24,288]{2,1,0:T(8,128)(2,1)S(1)}, bf16[64,24,288]{2,1,0:T(8,128)(2,1)}, u32[]{:S(2)}) %copy-start.2) | copy-done | bytes 884760
  1.3 1.1 %shard_map.64.refs_3_ = bf16[1728,256]{1,0:T(8,128)(2,1)} custom-call(bf16[1536,288]{1,0:T(8,128)(2,1)S(1)} %bitcast.5), custom_call_target="tpu_custom_call" | custom-call | flops 2200000000 | bytes 1000000 | tf_op jit(solution)/shard_map/pallas_call | solution.py:331
  2.4 1.5 %collective-permute-start = (bf16[1728,256]{1,0:T(8,128)(2,1)}, bf16[1728,256]{1,0:T(8,128)(2,1)}, u32[]{:S(2)}, u32[]{:S(2)}) collective-permute-start(bf16[1728,256]{1,0:T(8,128)(2,1)} %shard_map.64.refs_3_), channel_id=1, source_target_pairs={{0,2},{1,3},{2,0},{3,1},{4,6},{5,7},{6,4},{7,5},{8,10},{9,11},{10,... | collective-permute-start | bytes 2654216 | tf_op jit(solution)/shard_map/ppermute | solution.py:326
  3.9 0.0 collective-permute-start.5
  3.9 0.1 pad_add_fusion.place_ref.refs_0_
  4.0 0.0 copy-done.5
  4.0 1.3 %copy-done.3 = bf16[64,24,288]{2,1,0:T(8,128)(2,1)S(1)} copy-done((bf16[64,24,288]{2,1,0:T(8,128)(2,1)S(1)}, bf16[64,24,288]{2,1,0:T(8,128)(2,1)}, u32[]{:S(2)}) %copy-start.3) | copy-done | bytes 884760
  5.3 2.0 %shard_map.65 = (bf16[864,256]{1,0:T(8,128)(2,1)}, bf16[864,256]{1,0:T(8,128)(2,1)}) custom-call(s32[2]{0:T(128)S(1)} %pad_add_fusion.place_ref.refs_0_, s32[8,2,32]{2,1,0:T(2,128)S(1)} %copy-done.5, bf16[1536,288]{1,0:T(8,128)(2,1)S(1)} %bitcast.6), custom_call_target="tpu_custom_call" | custom-call | flops 3300000000 | bytes 1000000 | tf_op jit(solution)/shard_map/pallas_call | solution.py:340
  7.2 3.4 %collective-permute-start.1 = (bf16[864,256]{1,0:T(8,128)(2,1)}, bf16[864,256]{1,0:T(8,128)(2,1)S(1)}, u32[]{:S(2)}, u32[]{:S(2)}) collective-permute-start(bf16[864,256]{1,0:T(8,128)(2,1)} %get-tuple-element.27), channel_id=1, source_target_pairs={{0,4},{1,5},{2,6},{3,7},{4,8},{5,9},{6,10},{7,11},{8,12},{9,13},{1... | collective-permute-start | bytes 1327112 | tf_op jit(solution)/shard_map/ppermute | solution.py:326
  10.6 0.0 copy-done
  10.6 0.1 constant_dynamic-slice_fusion
  10.7 0.1 copy.7
  10.8 0.2 reshape.12.refs_1_.refs_2_
  11.7 0.0 copy-done.1
  11.7 0.0 copy-start.4
  11.7 1.3 %copy-done.4 = bf16[64,24,288]{2,1,0:T(8,128)(2,1)S(1)} copy-done((bf16[64,24,288]{2,1,0:T(8,128)(2,1)S(1)}, bf16[64,24,288]{2,1,0:T(8,128)(2,1)}, u32[]{:S(2)}) %copy-start.4) | copy-done | bytes 884760
  13.0 7.1 %shard_map.66 = (bf16[768,1536]{1,0:T(8,128)(2,1)S(1)}, bf16[9,1536,128]{2,1,0:T(8,128)(2,1)S(1)}) custom-call(s32[2]{0:T(128)S(1)} %pad_add_fusion.place_ref.refs_0_, s32[576]{0:T(1024)S(1)} %reshape.12.refs_1_.refs_2_, s32[1]{0:T(128)S(6)} %copy.9.refs_2_, bf16[1536,288]{1,0:T(8,128)(2,1)S(1)} %bitcast.7, bf16[1536,864]{1,0:T(8,128)(2,1)S(1)} %bitcast.4), custom_call_target="tpu_custom_call" | custom-call | flops 9900000256 | bytes 1000000 | tf_op jit(solution)/shard_map/pallas_call | solution.py:357
  20.1 0.0 copy-start.6
  20.1 1.7 %copy-done.6 = bf16[9,1536,128]{2,1,0:T(8,128)(2,1)} copy-done((bf16[9,1536,128]{2,1,0:T(8,128)(2,1)}, bf16[9,1536,128]{2,1,0:T(8,128)(2,1)S(1)}, u32[]{:S(2)}) %copy-start.6) | copy-done | bytes 3538968
  21.8 1.4 %copy-done.8 = bf16[768,1536]{1,0:T(8,128)(2,1)} copy-done((bf16[768,1536]{1,0:T(8,128)(2,1)}, bf16[768,1536]{1,0:T(8,128)(2,1)S(1)}, u32[]{:S(2)}) %copy-start.8) | copy-done | bytes 2359320
  23.2 0.0 collective-permute-done.1.refs_4_
  23.2 0.9 collective-permute-done.packed_ref.refs_5_
  24.1 0.0 collective-permute-start.6
  24.1 3.3 %collective-permute-start.9 = (bf16[864,256]{1,0:T(8,128)(2,1)}, bf16[864,256]{1,0:T(8,128)(2,1)S(1)}, u32[]{:S(2)}, u32[]{:S(2)}) collective-permute-start(bf16[864,256]{1,0:T(8,128)(2,1)} %get-tuple-element.42), channel_id=1, source_target_pairs={{4,0},{5,1},{6,2},{7,3},{8,4},{9,5},{10,6},{11,7},{12,8},{13,9},{1... | collective-permute-start | bytes 1327112 | tf_op jit(solution)/shard_map/ppermute | solution.py:326
  27.4 0.0 copy-done.11
  27.4 0.1 copy.8
  27.5 0.1 reshape.13.refs_2_.refs_3_
  27.6 1.6 %collective-permute-start.4 = (bf16[864,256]{1,0:T(8,128)(2,1)S(1)}, bf16[864,256]{1,0:T(8,128)(2,1)S(1)}, u32[]{:S(2)}, u32[]{:S(2)}) collective-permute-start(bf16[864,256]{1,0:T(8,128)(2,1)S(1)} %collective-permute-done.1.refs_4_), channel_id=1, source_target_pairs={{0,2},{1,3},{2,0},{3,1},{4,6},{5,7},{6,4},{7,5},{8,10},{9,11},{10,... | collective-permute-start | bytes 1327112 | tf_op jit(solution)/shard_map/ppermute | solution.py:326
  29.2 0.0 collective-permute-start.2
  29.2 1.7 %shard_map.67 = bf16[864,256]{1,0:T(8,128)(2,1)S(1)} custom-call(s32[2]{0:T(128)S(1)} %pad_add_fusion.place_ref.refs_0_, s32[8,2,32]{2,1,0:T(2,128)S(1)} %copy-done.5, bf16[1728,256]{1,0:T(8,128)(2,1)} %collective-permute-done.packed_ref.refs_5_), custom_call_target="tpu_custom_call" | custom-call | flops 3300000000 | bytes 1000000 | tf_op jit(solution)/shard_map/pallas_call | solution.py:372
  31.0 0.0 collective-permute-done.5.refs_4_
  31.0 2.6 %collective-permute-start.3 = (bf16[864,256]{1,0:T(8,128)(2,1)S(1)}, bf16[864,256]{1,0:T(8,128)(2,1)S(1)}, u32[]{:S(2)}, u32[]{:S(2)}) collective-permute-start(bf16[864,256]{1,0:T(8,128)(2,1)S(1)} %shard_map.67), channel_id=1, source_target_pairs={{4,0},{5,1},{6,2},{7,3},{8,4},{9,5},{10,6},{11,7},{12,8},{13,9},{1... | collective-permute-start | bytes 1327112 | tf_op jit(solution)/shard_map/ppermute | solution.py:326
  33.5 0.0 collective-permute-done.6.refs_6_
  33.6 8.8 %shard_map.68 = (f32[16,8,24,128]{3,2,1,0:T(8,128)S(1)}, f32[16,8,24,128]{3,2,1,0:T(8,128)S(1)}, f32[16,8,24,128]{3,2,1,0:T(8,128)S(1)}, f32[16,8,24,128]{3,2,1,0:T(8,128)S(1)}) custom-call(s32[2]{0:T(128)S(1)} %pad_add_fusion.place_ref.refs_0_, s32[576]{0:T(1024)S(1)} %reshape.12.refs_1_.refs_2_, s32[576]{0:T(1024)S(1)} %reshape.13.refs_2_.refs_3_, ...), custom_call_target="tpu_custom_call" | custom-call | flops 11000000512 | bytes 1000000 | tf_op jit(solution)/shard_map/pallas_call | solution.py:386
  42.4 5.8 %collective-permute-done.3.refs_6_ = bf16[864,256]{1,0:T(8,128)(2,1)S(1)} collective-permute-done((bf16[864,256]{1,0:T(8,128)(2,1)S(1)}, bf16[864,256]{1,0:T(8,128)(2,1)S(1)}, u32[]{:S(2)}, u32[]{:S(2)}) %collective-permute-start.3) | collective-permute-done | bytes 442400 | tf_op jit(solution)/shard_map/ppermute | solution.py:326
  48.2 0.0 collective-permute-done.4.refs_6_
  48.2 0.0 collective-permute-start.7
  48.3 0.0 collective-permute-done.9.refs_4_
  48.3 0.5 collective-permute-start.10
  48.8 0.1 collective-permute-start.11
  48.8 0.0 collective-permute-done.2.refs_5_
  48.8 1.2 %collective-permute-done.7.refs_7_ = bf16[864,256]{1,0:T(8,128)(2,1)S(1)} collective-permute-done((bf16[864,256]{1,0:T(8,128)(2,1)S(1)}, bf16[864,256]{1,0:T(8,128)(2,1)S(1)}, u32[]{:S(2)}, u32[]{:S(2)}) %collective-permute-start.7) | collective-permute-done | bytes 442400 | tf_op jit(solution)/shard_map/ppermute | solution.py:326
  50.0 7.1 %shard_map.69 = (bf16[384,768]{1,0:T(8,128)(2,1)S(1)}, f32[384,768]{1,0:T(8,128)S(1)}) custom-call(s32[2]{0:T(128)S(1)} %pad_add_fusion.place_ref.refs_0_, s32[8,2,32]{2,1,0:T(2,128)S(1)} %copy-done.5, s32[576]{0:T(1024)S(1)} %reshape.12.refs_1_.refs_2_, s32[576]{0:T(1024)S(1)} %reshape.13.refs_2_.refs_3_, ...), custom_call_target="tpu_custom_call" | custom-call | flops 8800000000 | bytes 1000000 | tf_op jit(solution)/shard_map/pallas_call | solution.py:399
  57.2 0.2 collective-permute-start.8
  57.4 0.0 collective-permute-done.10.refs_5_
  57.4 0.0 collective-permute-done.11.refs_7_
  57.4 7.1 %shard_map.70 = (bf16[384,768]{1,0:T(8,128)(2,1)S(1)}, f32[384,768]{1,0:T(8,128)S(1)}) custom-call(s32[2]{0:T(128)S(1)} %pad_add_fusion.place_ref.refs_0_, s32[8,2,32]{2,1,0:T(2,128)S(1)} %copy-done.5, s32[576]{0:T(1024)S(1)} %reshape.12.refs_1_.refs_2_, s32[576]{0:T(1024)S(1)} %reshape.13.refs_2_.refs_3_, ...), custom_call_target="tpu_custom_call" | custom-call | flops 8800000000 | bytes 1000000 | tf_op jit(solution)/shard_map/pallas_call | solution.py:399
  64.5 0.0 collective-permute-done.8
  64.5 0.4 collective-permute-start.13
  65.0 0.1 convert_add_fusion.1
  65.1 1.6 %collective-permute-start.12 = (bf16[192,768]{1,0:T(8,128)(2,1)S(1)}, bf16[192,768]{1,0:T(8,128)(2,1)S(1)}, u32[]{:S(2)}, u32[]{:S(2)}) collective-permute-start(bf16[192,768]{1,0:T(8,128)(2,1)S(1)} %slice.58), channel_id=1, source_target_pairs={{0,2},{1,3},{2,0},{3,1},{4,6},{5,7},{6,4},{7,5},{8,10},{9,11},{10,... | collective-permute-start | bytes 884744 | tf_op jit(solution)/shard_map/ppermute | solution.py:326
  66.7 7.5 %collective-permute-done.12 = bf16[192,768]{1,0:T(8,128)(2,1)S(1)} collective-permute-done((bf16[192,768]{1,0:T(8,128)(2,1)S(1)}, bf16[192,768]{1,0:T(8,128)(2,1)S(1)}, u32[]{:S(2)}, u32[]{:S(2)}) %collective-permute-start.12) | collective-permute-done | bytes 294944 | tf_op jit(solution)/shard_map/ppermute | solution.py:326
  74.2 0.1 slice_add_fusion
  74.3 0.0 collective-permute-done.13
  74.3 0.2 fusion.2
  74.5 1.6 %collective-permute-start.14 = (bf16[96,768]{1,0:T(8,128)(2,1)S(1)}, bf16[96,768]{1,0:T(8,128)(2,1)S(1)}, u32[]{:S(2)}, u32[]{:S(2)}) collective-permute-start(bf16[96,768]{1,0:T(8,128)(2,1)S(1)} %get-tuple-element.51), channel_id=1, source_target_pairs={{0,2},{1,3},{2,0},{3,1},{4,6},{5,7},{6,4},{7,5},{8,10},{9,11},{10,... | collective-permute-start | bytes 442376 | tf_op jit(solution)/shard_map/ppermute | solution.py:326
  76.1 4.4 %collective-permute-start.15 = (bf16[192,768]{1,0:T(8,128)(2,1)S(1)}, bf16[192,768]{1,0:T(8,128)(2,1)S(1)}, u32[]{:S(2)}, u32[]{:S(2)}) collective-permute-start(bf16[192,768]{1,0:T(8,128)(2,1)S(1)} %pad_maximum_fusion), channel_id=1, source_target_pairs={{0,4},{1,5},{2,6},{3,7},{4,8},{5,9},{6,10},{7,11},{8,12},{9,13},{1... | collective-permute-start | bytes 884744 | tf_op jit(solution)/shard_map/ppermute | solution.py:326
  80.5 0.0 slice-start
  80.5 2.6 %collective-permute-start.16 = (bf16[96,768]{1,0:T(8,128)(2,1)S(1)}, bf16[96,768]{1,0:T(8,128)(2,1)S(1)}, u32[]{:S(2)}, u32[]{:S(2)}) collective-permute-start(bf16[96,768]{1,0:T(8,128)(2,1)S(1)} %get-tuple-element.52), channel_id=1, source_target_pairs={{0,6},{1,7},{2,4},{3,5},{4,10},{5,11},{6,8},{7,9},{8,14},{9,15},{1... | collective-permute-start | bytes 442376 | tf_op jit(solution)/shard_map/ppermute | solution.py:326
  83.1 0.0 collective-permute-done.14
  83.2 5.3 %collective-permute-done.15 = bf16[192,768]{1,0:T(8,128)(2,1)S(1)} collective-permute-done((bf16[192,768]{1,0:T(8,128)(2,1)S(1)}, bf16[192,768]{1,0:T(8,128)(2,1)S(1)}, u32[]{:S(2)}, u32[]{:S(2)}) %collective-permute-start.15) | collective-permute-done | bytes 294944 | tf_op jit(solution)/shard_map/ppermute | solution.py:326
  88.5 1.5 %collective-permute-done.16 = bf16[96,768]{1,0:T(8,128)(2,1)S(1)} collective-permute-done((bf16[96,768]{1,0:T(8,128)(2,1)S(1)}, bf16[96,768]{1,0:T(8,128)(2,1)S(1)}, u32[]{:S(2)}, u32[]{:S(2)}) %collective-permute-start.16) | collective-permute-done | bytes 147488 | tf_op jit(solution)/shard_map/ppermute | solution.py:326
  90.0 0.8 fusion.1
  (20 shorter events, 0.2 us)
Async XLA Ops:
  0.0 10.6 %copy-start = (s32[512,3]{0,1:T(4,128)S(1)}, s32[512,3]{0,1:T(4,128)}, u32[]{:S(2)}) copy-start(s32[512,3]{0,1:T(4,128)} %param.9) | copy-start | bytes 18436
  0.0 1.3 %copy-start.2 = (bf16[64,24,288]{2,1,0:T(8,128)(2,1)S(1)}, bf16[64,24,288]{2,1,0:T(8,128)(2,1)}, u32[]{:S(2)}) copy-start(bf16[64,24,288]{2,1,0:T(8,128)(2,1)} %param.7) | copy-start | bytes 2654212
  1.3 2.7 %copy-start.5 = (s32[8,2,32]{2,1,0:T(2,128)S(1)}, s32[8,2,32]{2,1,0:T(2,128)}, u32[]{:S(2)}) copy-start(s32[8,2,32]{2,1,0:T(2,128)} %refs_1_.3) | copy-start | bytes 6148
  2.4 21.7 %collective-permute-start = (bf16[1728,256]{1,0:T(8,128)(2,1)}, bf16[1728,256]{1,0:T(8,128)(2,1)}, u32[]{:S(2)}, u32[]{:S(2)}) collective-permute-start(bf16[1728,256]{1,0:T(8,128)(2,1)} %shard_map.64.refs_3_), channel_id=1, source_target_pairs={{0,2},{1,3},{2,0},{3,1},{4,6},{5,7},{6,4},{7,5},{8,10},{9,11},{10,... | collective-permute-start | bytes 2654216 | tf_op jit(solution)/shard_map/ppermute | solution.py:326
  3.9 27.1 %collective-permute-start.5 = (bf16[1728,256]{1,0:T(8,128)(2,1)}, bf16[1728,256]{1,0:T(8,128)(2,1)}, u32[]{:S(2)}, u32[]{:S(2)}) collective-permute-start(bf16[1728,256]{1,0:T(8,128)(2,1)} %shard_map.64.refs_3_), channel_id=1, source_target_pairs={{0,1},{1,0},{2,3},{3,2},{4,5},{5,4},{6,7},{7,6},{8,9},{9,8},{10,11... | collective-permute-start | bytes 2654216 | tf_op jit(solution)/shard_map/ppermute | solution.py:326
  4.0 1.3 %copy-start.3 = (bf16[64,24,288]{2,1,0:T(8,128)(2,1)S(1)}, bf16[64,24,288]{2,1,0:T(8,128)(2,1)}, u32[]{:S(2)}) copy-start(bf16[64,24,288]{2,1,0:T(8,128)(2,1)} %param.7) | copy-start | bytes 2654212
  5.3 6.4 %copy-start.1 = (bf16[64,24,864]{2,1,0:T(8,128)(2,1)S(1)}, bf16[64,24,864]{2,1,0:T(8,128)(2,1)}, u32[]{:S(2)}) copy-start(bf16[64,24,864]{2,1,0:T(8,128)(2,1)} %param.6) | copy-start | bytes 7962628
  7.2 16.0 %collective-permute-start.1 = (bf16[864,256]{1,0:T(8,128)(2,1)}, bf16[864,256]{1,0:T(8,128)(2,1)S(1)}, u32[]{:S(2)}, u32[]{:S(2)}) collective-permute-start(bf16[864,256]{1,0:T(8,128)(2,1)} %get-tuple-element.27), channel_id=1, source_target_pairs={{0,4},{1,5},{2,6},{3,7},{4,8},{5,9},{6,10},{7,11},{8,12},{9,13},{1... | collective-permute-start | bytes 1327112 | tf_op jit(solution)/shard_map/ppermute | solution.py:326
  11.7 1.3 %copy-start.4 = (bf16[64,24,288]{2,1,0:T(8,128)(2,1)S(1)}, bf16[64,24,288]{2,1,0:T(8,128)(2,1)}, u32[]{:S(2)}) copy-start(bf16[64,24,288]{2,1,0:T(8,128)(2,1)} %param.7) | copy-start | bytes 2654212
  13.0 14.4 %copy-start.11 = (s32[64,9]{0,1:T(8,128)S(1)}, s32[64,9]{0,1:T(8,128)}, u32[]{:S(2)}) copy-start(s32[64,9]{0,1:T(8,128)} %param.8) | copy-start | bytes 6916
  20.1 1.7 %copy-start.6 = (bf16[9,1536,128]{2,1,0:T(8,128)(2,1)}, bf16[9,1536,128]{2,1,0:T(8,128)(2,1)S(1)}, u32[]{:S(2)}) copy-start(bf16[9,1536,128]{2,1,0:T(8,128)(2,1)S(1)} %get-tuple-element.32.refs_7_.refs_8_) | copy-start | bytes 10616836
  21.8 1.4 %copy-start.8 = (bf16[768,1536]{1,0:T(8,128)(2,1)}, bf16[768,1536]{1,0:T(8,128)(2,1)S(1)}, u32[]{:S(2)}) copy-start(bf16[768,1536]{1,0:T(8,128)(2,1)S(1)} %get-tuple-element.39.refs_13_) | copy-start | bytes 7077892
  24.1 9.5 %collective-permute-start.6 = (bf16[1728,256]{1,0:T(8,128)(2,1)}, bf16[1728,256]{1,0:T(8,128)(2,1)S(1)}, u32[]{:S(2)}, u32[]{:S(2)}) collective-permute-start(bf16[1728,256]{1,0:T(8,128)(2,1)} %collective-permute-done.packed_ref.refs_5_), channel_id=1, source_target_pairs={{0,1},{1,0},{2,3},{3,2},{4,5},{5,4},{6,7},{7,6},{8,9},{9,8},{10,11... | collective-permute-start | bytes 2654216 | tf_op jit(solution)/shard_map/ppermute | solution.py:326
  24.1 24.2 %collective-permute-start.9 = (bf16[864,256]{1,0:T(8,128)(2,1)}, bf16[864,256]{1,0:T(8,128)(2,1)S(1)}, u32[]{:S(2)}, u32[]{:S(2)}) collective-permute-start(bf16[864,256]{1,0:T(8,128)(2,1)} %get-tuple-element.42), channel_id=1, source_target_pairs={{4,0},{5,1},{6,2},{7,3},{8,4},{9,5},{10,6},{11,7},{12,8},{13,9},{1... | collective-permute-start | bytes 1327112 | tf_op jit(solution)/shard_map/ppermute | solution.py:326
  27.6 5.9 %copy-start.7 = (bf16[9,1536,128]{2,1,0:T(8,128)(2,1)S(1)}, bf16[9,1536,128]{2,1,0:T(8,128)(2,1)}, u32[]{:S(2)}) copy-start(bf16[9,1536,128]{2,1,0:T(8,128)(2,1)} %copy-done.6) | copy-start | bytes 10616836
  27.6 20.6 %collective-permute-start.4 = (bf16[864,256]{1,0:T(8,128)(2,1)S(1)}, bf16[864,256]{1,0:T(8,128)(2,1)S(1)}, u32[]{:S(2)}, u32[]{:S(2)}) collective-permute-start(bf16[864,256]{1,0:T(8,128)(2,1)S(1)} %collective-permute-done.1.refs_4_), channel_id=1, source_target_pairs={{0,2},{1,3},{2,0},{3,1},{4,6},{5,7},{6,4},{7,5},{8,10},{9,11},{10,... | collective-permute-start | bytes 1327112 | tf_op jit(solution)/shard_map/ppermute | solution.py:326
  29.2 19.6 %collective-permute-start.2 = (bf16[864,256]{1,0:T(8,128)(2,1)S(1)}, bf16[864,256]{1,0:T(8,128)(2,1)S(1)}, u32[]{:S(2)}, u32[]{:S(2)}) collective-permute-start(bf16[864,256]{1,0:T(8,128)(2,1)S(1)} %collective-permute-done.1.refs_4_), channel_id=1, source_target_pairs={{0,1},{1,0},{2,3},{3,2},{4,5},{5,4},{6,7},{7,6},{8,9},{9,8},{10,11... | collective-permute-start | bytes 1327112 | tf_op jit(solution)/shard_map/ppermute | solution.py:326
  30.9 19.1 %copy-start.9 = (bf16[768,1536]{1,0:T(8,128)(2,1)S(1)}, bf16[768,1536]{1,0:T(8,128)(2,1)}, u32[]{:S(2)}) copy-start(bf16[768,1536]{1,0:T(8,128)(2,1)} %copy-done.8) | copy-start | bytes 7077892
  31.0 17.3 %collective-permute-start.3 = (bf16[864,256]{1,0:T(8,128)(2,1)S(1)}, bf16[864,256]{1,0:T(8,128)(2,1)S(1)}, u32[]{:S(2)}, u32[]{:S(2)}) collective-permute-start(bf16[864,256]{1,0:T(8,128)(2,1)S(1)} %shard_map.67), channel_id=1, source_target_pairs={{4,0},{5,1},{6,2},{7,3},{8,4},{9,5},{10,6},{11,7},{12,8},{13,9},{1... | collective-permute-start | bytes 1327112 | tf_op jit(solution)/shard_map/ppermute | solution.py:326
  48.2 1.8 %collective-permute-start.7 = (bf16[864,256]{1,0:T(8,128)(2,1)S(1)}, bf16[864,256]{1,0:T(8,128)(2,1)S(1)}, u32[]{:S(2)}, u32[]{:S(2)}) collective-permute-start(bf16[864,256]{1,0:T(8,128)(2,1)S(1)} %collective-permute-done.4.refs_6_), channel_id=1, source_target_pairs={{0,1},{1,0},{2,3},{3,2},{4,5},{5,4},{6,7},{7,6},{8,9},{9,8},{10,11... | collective-permute-start | bytes 1327112 | tf_op jit(solution)/shard_map/ppermute | solution.py:326
  48.3 9.1 %collective-permute-start.10 = (bf16[864,256]{1,0:T(8,128)(2,1)S(1)}, bf16[864,256]{1,0:T(8,128)(2,1)S(1)}, u32[]{:S(2)}, u32[]{:S(2)}) collective-permute-start(bf16[864,256]{1,0:T(8,128)(2,1)S(1)} %collective-permute-done.9.refs_4_), channel_id=1, source_target_pairs={{0,1},{1,0},{2,3},{3,2},{4,5},{5,4},{6,7},{7,6},{8,9},{9,8},{10,11... | collective-permute-start | bytes 1327112 | tf_op jit(solution)/shard_map/ppermute | solution.py:326
  48.8 8.6 %collective-permute-start.11 = (bf16[864,256]{1,0:T(8,128)(2,1)S(1)}, bf16[864,256]{1,0:T(8,128)(2,1)S(1)}, u32[]{:S(2)}, u32[]{:S(2)}) collective-permute-start(bf16[864,256]{1,0:T(8,128)(2,1)S(1)} %collective-permute-done.3.refs_6_), channel_id=1, source_target_pairs={{0,1},{1,0},{2,3},{3,2},{4,5},{5,4},{6,7},{7,6},{8,9},{9,8},{10,11... | collective-permute-start | bytes 1327112 | tf_op jit(solution)/shard_map/ppermute | solution.py:326
  57.2 7.3 %collective-permute-start.8 = (bf16[384,768]{1,0:T(8,128)(2,1)S(1)}, bf16[384,768]{1,0:T(8,128)(2,1)S(1)}, u32[]{:S(2)}, u32[]{:S(2)}) collective-permute-start(bf16[384,768]{1,0:T(8,128)(2,1)S(1)} %get-tuple-element.41), channel_id=1, source_target_pairs={{0,1},{1,0},{2,3},{3,2},{4,5},{5,4},{6,7},{7,6},{8,9},{9,8},{10,11... | collective-permute-start | bytes 1769480 | tf_op jit(solution)/shard_map/ppermute | solution.py:326
  64.5 9.8 %collective-permute-start.13 = (bf16[384,768]{1,0:T(8,128)(2,1)S(1)}, bf16[384,768]{1,0:T(8,128)(2,1)S(1)}, u32[]{:S(2)}, u32[]{:S(2)}) collective-permute-start(bf16[384,768]{1,0:T(8,128)(2,1)S(1)} %get-tuple-element.48), channel_id=1, source_target_pairs={{0,1},{1,0},{2,3},{3,2},{4,5},{5,4},{6,7},{7,6},{8,9},{9,8},{10,11... | collective-permute-start | bytes 1769480 | tf_op jit(solution)/shard_map/ppermute | solution.py:326
  65.1 9.1 %collective-permute-start.12 = (bf16[192,768]{1,0:T(8,128)(2,1)S(1)}, bf16[192,768]{1,0:T(8,128)(2,1)S(1)}, u32[]{:S(2)}, u32[]{:S(2)}) collective-permute-start(bf16[192,768]{1,0:T(8,128)(2,1)S(1)} %slice.58), channel_id=1, source_target_pairs={{0,2},{1,3},{2,0},{3,1},{4,6},{5,7},{6,4},{7,5},{8,10},{9,11},{10,... | collective-permute-start | bytes 884744 | tf_op jit(solution)/shard_map/ppermute | solution.py:326
  74.3 6.2 %copy-start.10 = (f32[192,768]{1,0:T(8,128)}, f32[192,768]{1,0:T(8,128)S(1)}, u32[]{:S(2)}) copy-start(f32[192,768]{1,0:T(8,128)S(1)} %slice_add_fusion) | copy-start | bytes 1769476
  74.5 8.6 %collective-permute-start.14 = (bf16[96,768]{1,0:T(8,128)(2,1)S(1)}, bf16[96,768]{1,0:T(8,128)(2,1)S(1)}, u32[]{:S(2)}, u32[]{:S(2)}) collective-permute-start(bf16[96,768]{1,0:T(8,128)(2,1)S(1)} %get-tuple-element.51), channel_id=1, source_target_pairs={{0,2},{1,3},{2,0},{3,1},{4,6},{5,7},{6,4},{7,5},{8,10},{9,11},{10,... | collective-permute-start | bytes 442376 | tf_op jit(solution)/shard_map/ppermute | solution.py:326
  76.1 12.3 %collective-permute-start.15 = (bf16[192,768]{1,0:T(8,128)(2,1)S(1)}, bf16[192,768]{1,0:T(8,128)(2,1)S(1)}, u32[]{:S(2)}, u32[]{:S(2)}) collective-permute-start(bf16[192,768]{1,0:T(8,128)(2,1)S(1)} %pad_maximum_fusion), channel_id=1, source_target_pairs={{0,4},{1,5},{2,6},{3,7},{4,8},{5,9},{6,10},{7,11},{8,12},{9,13},{1... | collective-permute-start | bytes 884744 | tf_op jit(solution)/shard_map/ppermute | solution.py:326
  80.5 9.5 %slice-start = ((f32[192,768]{1,0:T(8,128)}), f32[96,768]{1,0:T(8,128)S(1)}, s32[]{:S(2)}) async-start(f32[192,768]{1,0:T(8,128)} %copy-done.10), calls=%async_computation | async-start | bytes 589824 | tf_op jit(solution)/shard_map/slice | solution.py:428
  80.5 9.4 %collective-permute-start.16 = (bf16[96,768]{1,0:T(8,128)(2,1)S(1)}, bf16[96,768]{1,0:T(8,128)(2,1)S(1)}, u32[]{:S(2)}, u32[]{:S(2)}) collective-permute-start(bf16[96,768]{1,0:T(8,128)(2,1)S(1)} %get-tuple-element.52), channel_id=1, source_target_pairs={{0,6},{1,7},{2,4},{3,5},{4,10},{5,11},{6,8},{7,9},{8,14},{9,15},{1... | collective-permute-start | bytes 442376 | tf_op jit(solution)/shard_map/ppermute | solution.py:326

commit v4 on v3

--- a/solution.py
+++ b/solution.py
@@ -34,6 +34,10 @@
     return pl.BlockSpec(memory_space=pltpu.VMEM)
 
 
+def in_hbm():
+    return pl.BlockSpec(memory_space=pltpu.HBM)
+
+
 def in_smem():
     return pl.BlockSpec(memory_space=pltpu.SMEM)
 
@@ -66,35 +70,34 @@
         out_ref[start : start + 48, :] = jnp.concatenate(tails, axis=1)
 
 
+def packed_pairs(packed_ref, g):
+    tail_rows = pl.ds(pl.multiple_of(ROWS + g * 48, 48), 48)
+    tails = [packed_ref[tail_rows, 128 * h : 128 * h + 128].astype(F32) for h in range(2)]
+    for q in range(8):
+        rows = pl.ds(pl.multiple_of((8 * g + q) * 48, 48), 48)
+        x0, x1 = [packed_ref[rows, 128 * h : 128 * h + 128].astype(F32) for h in range(2)]
+        shift = (-32 * (q % 4)) % 128
+        tail = tails[q // 4]
+        yield q, x0, x1, pltpu.roll(tail, shift, 1) if shift else tail
+
+
+def widen(packed_ref, wide_ref):
+    def group(g, carry):
+        for q, x0, x1, tail in packed_pairs(packed_ref, g):
+            for odd in range(2):
+                r, rows = 2 * (8 * g + q) + odd, slice(24 * odd, 24 * odd + 24)
+                wide_ref[r, :, 0:128] = x0[rows]
+                wide_ref[r, :, 128:256] = x1[rows]
+                wide_ref[r, :, 256:288] = tail[rows, 0:32]
+        return carry
+
+    lax.fori_loop(0, NB // 16, group, 0)
+
+
 def pack_halo_kernel(place_ref, halo_ref, p_ref, down_ref, up_ref, wide_ref):
     part = place_ref[0]
-
-    def widen(t, carry):
-        pair = p_ref[pl.ds(pl.multiple_of(t * 48, 48), 48), :].astype(F32)
-        wide_ref[2 * t] = pair[0:24]
-        wide_ref[2 * t + 1] = pair[24:48]
-        return carry
-
-    lax.fori_loop(0, NB // 2, widen, 0, unroll=4)
+    widen(p_ref, wide_ref)
     pack_rows(wide_ref, lambda n: halo_ref[part, 1, n], up_ref)
-    pack_rows(wide_ref, lambda n: halo_ref[part, 0, n], down_ref)
-
-
-def select_kernel(place_ref, halo_ref, packed_ref, down_ref, wide_ref):
-    part = place_ref[0]
-
-    def widen(g, carry):
-        tail = packed_ref[pl.ds(pl.multiple_of(ROWS + g * 48, 48), 48), :].astype(F32)
-        for q in range(8):
-            t = 8 * g + q
-            pair = packed_ref[pl.ds(pl.multiple_of(t * 48, 48), 48), :].astype(F32)
-            for odd in range(2):
-                rows = slice(24 * odd, 24 * odd + 24)
-                wide_ref[2 * t + odd, :, 0:256] = pair[rows]
-                wide_ref[2 * t + odd, :, 256:288] = tail[rows, 32 * q : 32 * q + 32]
-        return carry
-
-    lax.fori_loop(0, NB // 16, widen, 0)
     pack_rows(wide_ref, lambda n: halo_ref[part, 0, n], down_ref)
 
 
@@ -119,29 +122,26 @@
             got = jnp.dot(a_ref[rows, start:stop], pick, preferred_element_type=F32)
             blocks_ref[k, rows, :] = got.astype(BF16)
 
-    def pair(t, carry):
-        rows = pl.ds(pl.multiple_of(t * 48, 48), 48)
-        p = p_ref[rows, :].astype(F32)
-        x0, x1 = p[:, 0:128], p[:, 128:256]
-        tail = jnp.concatenate([p[:, 256:288], jnp.zeros((48, 96), F32)], axis=1)
-        blocks = (
-            x0,
-            jnp.where(lane < 32, pltpu.roll(x0, 32, 1), pltpu.roll(x1, 32, 1)),
-            jnp.where(lane < 64, pltpu.roll(x1, 64, 1), pltpu.roll(tail, 64, 1)),
-        )
-        for odd in range(2):
-            r = 2 * t + odd
-            live = (r < live_ref[0]).astype(F32)
-            for m in range(KP):
-                block = aggs_ref[KP * (own + r) + m] - part * NAG
-                after = block // NAG
-                turn = jnp.bitwise_xor(block - NAG * after, col)
-                place = 2 * (3 - (2 * (turn % 2) + turn // 2)) + after
-                value = jnp.where(lane < 96, blocks[m], 0.0)[24 * odd : 24 * odd + 24] * live
-                wide_ref[place, pl.ds(pl.multiple_of(r * W, 8), W), :] = value
+    def group(g, carry):
+        for q, x0, x1, tail in packed_pairs(p_ref, g):
+            blocks = (
+                x0,
+                jnp.where(lane < 32, pltpu.roll(x0, 32, 1), pltpu.roll(x1, 32, 1)),
+                jnp.where(lane < 64, pltpu.roll(x1, 64, 1), pltpu.roll(tail, 64, 1)),
+            )
+            for odd in range(2):
+                r = 2 * (8 * g + q) + odd
+                live = (r < live_ref[0]).astype(F32)
+                for m in range(KP):
+                    block = aggs_ref[KP * (own + r) + m] - part * NAG
+                    after = block // NAG
+                    turn = jnp.bitwise_xor(block - NAG * after, col)
+                    place = 2 * (3 - (2 * (turn % 2) + turn // 2)) + after
+                    value = jnp.where(lane < 96, blocks[m], 0.0)[24 * odd : 24 * odd + 24] * live
+                    wide_ref[place, pl.ds(pl.multiple_of(r * W, 8), W), :] = value
         return carry
 
-    lax.fori_loop(0, NB // 2, pair, 0, unroll=2)
+    lax.fori_loop(0, NB // 16, group, 0)
     eye = (
         lax.broadcasted_iota(I32, (BC, 128), 0) == lax.broadcasted_iota(I32, (BC, 128), 1)
     ).astype(F32).astype(BF16)
@@ -187,7 +187,7 @@
     lax.fori_loop(0, count // 16, group, 0)
 
 
-def add_products(step, slots, a_ref, prolong, row_of, blocks_of, sums):
+def add_products(step, slots, a_ref, first_slot, prolong, row_of, blocks_of, sums):
     for slot in slots:
         for u in range(UN):
             i = UN * step + u
@@ -195,7 +195,7 @@
             start = pl.multiple_of(step * (UN * W) + 48 * (u // 2) + 16 * odd, 16)
             at = row_of(i, slot)
             got = jnp.dot(
-                a_ref[slot, pl.ds(start, 32), 0:BW], prolong[at[0]], preferred_element_type=F32
+                a_ref[slot - first_slot, pl.ds(start, 32), 0:BW], prolong[at[0]], preferred_element_type=F32
             )[8 * odd : 8 * odd + 24]
             where = blocks_of(at[1])
             held = [sums[u][step, c] for c in where]
@@ -204,11 +204,14 @@
 
 
 def own_kernel(place_ref, aggs_ref, cols_ref, *refs, parts):
-    sources, a_ref, sums, prolong = refs[0:4], refs[4], refs[5:9], refs[9]
     part = place_ref[0]
+    a_hbm, sums, (prolong, a_ref, sem) = refs[4], refs[5 : 5 + UN], refs[5 + UN :]
+    a_copy = pltpu.make_async_copy(a_hbm, a_ref, sem)
+    a_copy.start()
+    unpack(NB, refs[0:4], prolong)
+    a_copy.wait()
     own = part * NB - window_start(part, parts)
     base = part * NAG
-    unpack(NB, sources, prolong)
 
     def row_of(i, slot):
         row = cols_ref[KA * i + slot]
@@ -224,7 +227,7 @@
             if fresh:
                 for each in sums:
                     each[n] = jnp.zeros((8, W, 128), F32)
-            add_products(n, slots, a_ref, prolong, row_of, blocks_of, sums)
+            add_products(n, slots, a_ref, 0, prolong, row_of, blocks_of, sums)
             return carry
 
         lax.fori_loop(0, STEPS, step, 0, unroll=2 if fresh else 1)
@@ -241,17 +244,21 @@
 
 
 def halo_kernel(place_ref, halo_ref, aggs_ref, cols_ref, *refs, parts, upper):
-    sources, a_ref, own, spread, send_ref, keep_ref = refs[0:4], refs[4], refs[5:9], *refs[9:12]
-    prolong, sums, coupled = refs[12], refs[13:17], refs[17]
+    sources, a_hbm, own, coupled = refs[0:4], refs[4], refs[5:9], refs[9]
+    prolong, a_ref, sums, sem = refs[10], refs[11], refs[12:16], refs[16]
     part = place_ref[0]
     slots = (7, 8) if upper else (5, 6)
     other = jnp.minimum(part + 1, parts - 1) if upper else jnp.maximum(part - 1, 0)
     rows_at = other * NB - window_start(part, parts)
     inside = part < parts - 1 if upper else part > 0
+    a_copy = pltpu.make_async_copy(a_hbm.at[slots[0] : slots[0] + 2], a_ref, sem)
+    a_copy.start()
 
     @pl.when(inside)
     def _():
         unpack(NS, sources, prolong)
+
+    a_copy.wait()
 
     lane = lax.broadcasted_iota(I32, (48, 128), 1)
 
@@ -272,7 +279,7 @@
             for each in sums:
                 each[n] = jnp.zeros((8, W, 128), F32)
             if products:
-                add_products(n, slots, a_ref, prolong, row_of, blocks_of, sums)
+                add_products(n, slots, a_ref, slots[0], prolong, row_of, blocks_of, sums)
             for two in range(2):
                 rows = pl.ds(pl.multiple_of(n * (UN * W) + 48 * two, 48), 48)
                 for half in range(2):
@@ -301,13 +308,14 @@
     def _():
         run(False)
 
+
+def coarse_kernel(spread, coupled, out_ref, *, half):
     for n in range(3):
         at = slice(256 * n, 256 * n + 256)
-        for half, out_ref in ((0, send_ref), (1, keep_ref)):
-            got = jnp.dot(
-                spread[384 * half : 384 * half + 384, :], coupled[:, at], preferred_element_type=F32
-            )
-            out_ref[:, at] = got.astype(out_ref.dtype)
+        got = jnp.dot(
+            spread[384 * half : 384 * half + 384, :], coupled[:, at], preferred_element_type=F32
+        )
+        out_ref[:, at] = got.astype(out_ref.dtype)
 
 
 def local(a_vals, p_vals, a_cols, p_aggs, halo_rows, live_rows):
@@ -328,6 +336,7 @@
     place = jnp.stack([part, col]).astype(I32)
     p_flat = p_vals.reshape(ROWS, KP * BC)
     a_flat = a_vals.reshape(ROWS, KA * BW)
+    wide = pltpu.VMEM((NB, W, KP * BC), F32)
     own_pack = pl.pallas_call(
         pack_own_kernel,
         out_shape=packed(NB),
@@ -342,10 +351,10 @@
         out_shape=[packed(NS)] * 2,
         in_specs=[in_smem(), in_smem(), in_vmem()],
         out_specs=[in_vmem()] * 2,
-        scratch_shapes=[pltpu.VMEM((NB, W, KP * BC), F32)],
+        scratch_shapes=[wide],
         compiler_params=params(),
         cost_estimate=cost(3),
-    )(place, halo_rows, p_flat)
+    )(place, halo_rows, own_pack)
     low = moved(upward, 1, 0)
     up = moved(down, -1, 0)
 
@@ -365,68 +374,77 @@
         scratch_shapes=[pltpu.VMEM((8, ROWS, 128), F32)],
         compiler_params=params(),
         cost_estimate=cost(9),
-    )(place, aggs, live_rows, p_flat, a_flat)
-    near, low, spread, blocks = lax.optimization_barrier((near, low, spread, blocks))
+    )(place, aggs, live_rows, own_pack, a_flat)
+    near, low, spread = lax.optimization_barrier((near, low, spread))
     low_far = moved(low, 0, 2)
-    up_far = moved(
-        pl.pallas_call(
-            select_kernel,
-            out_shape=packed(NS),
-            in_specs=[in_smem(), in_smem(), in_vmem()],
-            out_specs=in_vmem(),
-            scratch_shapes=[pltpu.VMEM((NB, W, KP * BC), F32)],
-            compiler_params=params(),
-            cost_estimate=cost(3),
-        )(place, halo_rows, near),
-        -1,
-        0,
-    )
 
     sums_type = jax.ShapeDtypeStruct((STEPS, 8, W, 128), F32)
     own = pl.pallas_call(
         lambda *refs: own_kernel(*refs, parts=parts),
         out_shape=[sums_type] * UN,
-        in_specs=[in_smem()] * 3 + [in_vmem()] * 5,
+        in_specs=[in_smem()] * 3 + [in_vmem()] * 4 + [in_hbm()],
         out_specs=[in_vmem()] * UN,
-        scratch_shapes=[pltpu.VMEM((NB, BW, KP * 128), BF16)],
+        scratch_shapes=[
+            pltpu.VMEM((NB, BW, KP * 128), BF16),
+            pltpu.VMEM((KA, ROWS, 128), BF16),
+            pltpu.SemaphoreType.DMA,
+        ],
         compiler_params=params(),
         cost_estimate=cost(10),
     )(place, aggs, cols, *both_cores(own_pack, near), blocks)
-    up_far, low_far, first_sums = lax.optimization_barrier((up_far, low_far, own[0]))
+    up, low_far, first_sums = lax.optimization_barrier((up, low_far, own[0]))
     own = (first_sums, *own[1:])
-
-    def halo_terms(upper, sources):
+    up_far = moved(up, 0, 2)
+
+    def coupled_of(upper, sources):
         return pl.pallas_call(
             lambda *refs: halo_kernel(*refs, parts=parts, upper=upper),
-            out_shape=[
-                jax.ShapeDtypeStruct((4 * BC, 8 * BC), BF16),
-                jax.ShapeDtypeStruct((4 * BC, 8 * BC), F32),
-            ],
-            in_specs=[in_smem()] * 4 + [in_vmem()] * (6 + UN),
-            out_specs=[in_vmem(), in_vmem()],
+            out_shape=jax.ShapeDtypeStruct((ROWS, 8 * BC), BF16),
+            in_specs=[in_smem()] * 4 + [in_vmem()] * 4 + [in_hbm()] + [in_vmem()] * UN,
+            out_specs=in_vmem(),
             scratch_shapes=[
                 pltpu.VMEM((NS, BW, KP * 128), BF16),
+                pltpu.VMEM((2, ROWS, 128), BF16),
                 *[pltpu.VMEM((STEPS, 8, W, 128), F32)] * UN,
-                pltpu.VMEM((ROWS, 8 * BC), BF16),
+                pltpu.SemaphoreType.DMA,
             ],
             compiler_params=params(),
-            cost_estimate=cost(8),
-        )(place, halo_rows, aggs, cols, *sources, blocks, *own, spread)
-
-    low_send, low_keep = halo_terms(False, both_cores(low, low_far))
-    low_came = moved(low_send, 0, 1)
-    up_send, up_keep = halo_terms(True, both_cores(up, up_far))
-    low_came, up_send, up_keep = lax.optimization_barrier((low_came, up_send, up_keep))
-    up_came = moved(up_send, 0, 1)
+            cost_estimate=cost(6),
+        )(place, halo_rows, aggs, cols, *sources, blocks, *own)
+
+    def coarse_of(coupled, half):
+        return pl.pallas_call(
+            lambda *refs: coarse_kernel(*refs, half=half),
+            out_shape=jax.ShapeDtypeStruct((4 * BC, 8 * BC), F32 if half else BF16),
+            in_specs=[in_vmem()] * 2,
+            out_specs=in_vmem(),
+            compiler_params=params(),
+            cost_estimate=cost(1.5),
+        )(spread, coupled)
+
+    low_coupled = coupled_of(False, both_cores(low, low_far))
+    low_coupled, up_far = lax.optimization_barrier((low_coupled, up_far))
+    low_came = moved(coarse_of(low_coupled, 0), 0, 1)
+    low_keep = coarse_of(low_coupled, 1)
+    up_sources = both_cores(up, up_far)
     low_both = low_keep + low_came.astype(F32)
-    low_mine = low_both[2 * BC :] + moved(low_both[: 2 * BC].astype(BF16), 0, 2).astype(F32)
+    low_away = low_both[: 2 * BC].astype(BF16)
+    up_coupled = coupled_of(True, up_sources)
+    low_away, up_coupled = lax.optimization_barrier((low_away, up_coupled))
+    low_far_next = moved(low_away[BC:], 0, 2)
+    low_next = (low_both[3 * BC :] + low_far_next.astype(F32)).astype(BF16)
+    up_came = moved(coarse_of(up_coupled, 0), 0, 1)
+    up_keep = coarse_of(up_coupled, 1)
+    low_next, up_keep = lax.optimization_barrier((low_next, up_keep))
     up_both = up_keep + up_came.astype(F32)
     away = up_both.astype(BF16)
-    far_own = moved(away[0:BC], 0, 2)
+    near_next = moved(jnp.concatenate([low_next, away[3 * BC :]], axis=0), 1, 0)
     far_next = moved(away[BC : 2 * BC], 1, 2)
-    near_next = moved(jnp.concatenate([low_mine[BC:].astype(BF16), away[3 * BC :]], axis=0), 1, 0)
-    low_own, low_next = low_mine[:BC], near_next[:BC].astype(F32)
-    up_own = up_both[2 * BC : 3 * BC] + far_own.astype(F32)
+    far_own = moved(jnp.concatenate([low_away[:BC], away[0:BC]], axis=0), 0, 2)
+    near_next, far_next, far_own = lax.optimization_barrier((near_next, far_next, far_own))
+    far_own = far_own.astype(F32)
+    low_own, low_next = low_both[2 * BC : 3 * BC] + far_own[:BC], near_next[:BC].astype(F32)
+    up_own = up_both[2 * BC : 3 * BC] + far_own[BC:]
     up_next = near_next[BC:].astype(F32) + far_next.astype(F32)
     band = NAG * BC
     mine = jnp.concatenate([low_own, up_own], axis=1)

time: 91.7 us -> 86.2 us (0.940)
  waiting for transfers between devices: 22.2 us -> 19.3 us
  starting transfers between devices: 23.7 us -> 21 us
    ppermute x17, waiting for transfers between devices: 22.2 us -> 19.3 us  [moved(): return lax.ppermute(x, AXES, route)]
    ppermute x17, starting transfers between devices: 23.7 us -> 21 us  [moved(): return lax.ppermute(x, AXES, route)]
    pallas_call x3 -> x6, Pallas kernels: 16 us -> 14.9 us  [the longest x2 10.6 us: coupled_of(): pl.pallas_call(lambda *refs: halo_kernel(*refs, parts=parts, upper=upper)...]
    unnamed x25 -> x21, local copies, waits for them, and re-layouts: 7.09 us -> 6.53 us
  transfers between devices with their start and end apart: 17 -> 17, of which waited for: 6 -> 6; matrix products, arithmetic and copies ran while one was open for 1% -> 1% of each run, Pallas kernels for 37% -> 39%
where the time goes in v4:
time: 86.2 us; the launch traced here: 85.4 us
  Pallas kernels  35.7 us (41%)
  starting transfers between devices  21 us (24%)
  waiting for transfers between devices  19.3 us (22%)
  local copies, waits for them, and re-layouts  7.15 us (8%)
  other arithmetic  1.37 us (2%)
  between operations  0.96 us (1%)
    ppermute x17, starting transfers between devices, moved(): return lax.ppermute(x, AXES, route)  21 us
    ppermute x17, waiting for transfers between devices, moved(): return lax.ppermute(x, AXES, route)  19.3 us
    pallas_call x2, Pallas kernels, coupled_of(): pl.pallas_call(lambda *refs: halo_kernel(*refs, parts=parts, upper=upper)...  10.6 us
    pallas_call x1, Pallas kernels, local(): pl.pallas_call(lambda *refs: own_kernel(*refs, parts=parts), out_shape=[s...  9.42 us
    pallas_call x1, Pallas kernels, local(): pl.pallas_call(lambda *refs: prepare_kernel(*refs, parts=parts), out_shap...  7.46 us
    unnamed x21, local copies, waits for them, and re-layouts  6.53 us
    pallas_call x4, Pallas kernels, coarse_of(): pl.pallas_call(lambda *refs: coarse_kernel(*refs, half=half), out_shape=j...  4.3 us
    pallas_call x1, Pallas kernels, local(): pl.pallas_call(pack_halo_kernel, out_shape=[packed(NS)] * 2, in_specs=[in...  2.83 us
  transfers between devices with their start and end apart: 17, of which 6 were waited for; matrix products, arithmetic and copies ran while one was open for 1% of the time, Pallas kernels for 39%

profile of v4, /device:TPU:16, one launch (start us, length us, event | category | flops | bytes accessed | tf_op | source)
XLA Modules:
  0.0 85.4 jit_solution(4169030350404303033)
XLA Ops:
  0.0 0.0 copy-start
  0.0 1.3 %copy-done.2 = bf16[64,24,288]{2,1,0:T(8,128)(2,1)S(1)} copy-done((bf16[64,24,288]{2,1,0:T(8,128)(2,1)S(1)}, bf16[64,24,288]{2,1,0:T(8,128)(2,1)}, u32[]{:S(2)}) %copy-start.2) | copy-done | bytes 884760
  1.3 1.1 %shard_map.64.p_ref.refs_3_ = bf16[1728,256]{1,0:T(8,128)(2,1)} custom-call(bf16[1536,288]{1,0:T(8,128)(2,1)S(1)} %bitcast.5), custom_call_target="tpu_custom_call" | custom-call | flops 2200000000 | bytes 1000000 | tf_op jit(solution)/shard_map/pallas_call | solution.py:340
  2.4 1.5 %collective-permute-start = (bf16[1728,256]{1,0:T(8,128)(2,1)}, bf16[1728,256]{1,0:T(8,128)(2,1)}, u32[]{:S(2)}, u32[]{:S(2)}) collective-permute-start(bf16[1728,256]{1,0:T(8,128)(2,1)} %shard_map.64.p_ref.refs_3_), channel_id=1, source_target_pairs={{0,2},{1,3},{2,0},{3,1},{4,6},{5,7},{6,4},{7,5},{8,10},{9,11},{10,... | collective-permute-start | bytes 2654216 | tf_op jit(solution)/shard_map/ppermute | solution.py:334
  3.9 0.0 collective-permute-start.5
  3.9 0.1 pad_add_fusion.place_ref.refs_0_
  4.0 0.0 copy-done.3
  4.0 2.8 %shard_map.65 = (bf16[864,256]{1,0:T(8,128)(2,1)}, bf16[864,256]{1,0:T(8,128)(2,1)}) custom-call(s32[2]{0:T(128)S(1)} %pad_add_fusion.place_ref.refs_0_, s32[8,2,32]{2,1,0:T(2,128)S(1)} %copy-done.3, bf16[1728,256]{1,0:T(8,128)(2,1)} %shard_map.64.p_ref.refs_3_), custom_call_target="tpu_custom_call" | custom-call | flops 3300000000 | bytes 1000000 | tf_op jit(solution)/shard_map/pallas_call | solution.py:349
  6.8 3.4 %collective-permute-start.1 = (bf16[864,256]{1,0:T(8,128)(2,1)}, bf16[864,256]{1,0:T(8,128)(2,1)S(1)}, u32[]{:S(2)}, u32[]{:S(2)}) collective-permute-start(bf16[864,256]{1,0:T(8,128)(2,1)} %get-tuple-element.28), channel_id=1, source_target_pairs={{0,4},{1,5},{2,6},{3,7},{4,8},{5,9},{6,10},{7,11},{8,12},{9,13},{1... | collective-permute-start | bytes 1327112 | tf_op jit(solution)/shard_map/ppermute | solution.py:334
  10.2 0.0 copy-done
  10.2 0.1 constant_dynamic-slice_fusion
  10.3 0.1 copy.7
  10.4 0.2 reshape.13.refs_1_.refs_2_
  11.3 0.0 copy-done.1
  11.3 0.0 copy-start.9
  11.3 7.5 %shard_map.66 = (bf16[768,1536]{1,0:T(8,128)(2,1)S(1)}, bf16[9,1536,128]{2,1,0:T(8,128)(2,1)S(1)}) custom-call(s32[2]{0:T(128)S(1)} %pad_add_fusion.place_ref.refs_0_, s32[576]{0:T(1024)S(1)} %reshape.13.refs_1_.refs_2_, s32[1]{0:T(128)S(6)} %copy.9.refs_2_, bf16[1728,256]{1,0:T(8,128)(2,1)} %shard_map.64.p_ref.refs_3_, bf16[1536,864]{1,0:T(8,128)(2,1)S(1)} %bitcast.4), custom_call_target="tpu_custom_call" | custom-call | flops 9900000256 | bytes 1000000 | tf_op jit(solution)/shard_map/pallas_call | solution.py:366
  18.8 1.4 %copy-done.4 = bf16[768,1536]{1,0:T(8,128)(2,1)} copy-done((bf16[768,1536]{1,0:T(8,128)(2,1)}, bf16[768,1536]{1,0:T(8,128)(2,1)S(1)}, u32[]{:S(2)}) %copy-start.4) | copy-done | bytes 2359320
  20.2 1.7 %copy-done.6 = bf16[9,1536,128]{2,1,0:T(8,128)(2,1)} copy-done((bf16[9,1536,128]{2,1,0:T(8,128)(2,1)}, bf16[9,1536,128]{2,1,0:T(8,128)(2,1)S(1)}, u32[]{:S(2)}) %copy-start.6) | copy-done | bytes 3538968
  21.9 0.5 collective-permute-done.1.refs_4_
  22.4 1.7 %collective-permute-done.refs_5_ = bf16[1728,256]{1,0:T(8,128)(2,1)} collective-permute-done((bf16[1728,256]{1,0:T(8,128)(2,1)}, bf16[1728,256]{1,0:T(8,128)(2,1)}, u32[]{:S(2)}, u32[]{:S(2)}) %collective-permute-start) | collective-permute-done | bytes 884768 | tf_op jit(solution)/shard_map/ppermute | solution.py:334
  24.1 0.0 collective-permute-start.6
  24.1 3.3 %collective-permute-start.3 = (bf16[864,256]{1,0:T(8,128)(2,1)}, bf16[864,256]{1,0:T(8,128)(2,1)S(1)}, u32[]{:S(2)}, u32[]{:S(2)}) collective-permute-start(bf16[864,256]{1,0:T(8,128)(2,1)} %get-tuple-element.32), channel_id=1, source_target_pairs={{4,0},{5,1},{6,2},{7,3},{8,4},{9,5},{10,6},{11,7},{12,8},{13,9},{1... | collective-permute-start | bytes 1327112 | tf_op jit(solution)/shard_map/ppermute | solution.py:334
  27.4 0.1 copy.8
  27.5 0.1 reshape.15.refs_2_.refs_3_
  27.6 0.3 collective-permute-start.2
  27.9 1.5 %collective-permute-start.4 = (bf16[864,256]{1,0:T(8,128)(2,1)S(1)}, bf16[864,256]{1,0:T(8,128)(2,1)S(1)}, u32[]{:S(2)}, u32[]{:S(2)}) collective-permute-start(bf16[864,256]{1,0:T(8,128)(2,1)S(1)} %collective-permute-done.1.refs_4_), channel_id=1, source_target_pairs={{0,2},{1,3},{2,0},{3,1},{4,6},{5,7},{6,4},{7,5},{8,10},{9,11},{10,... | collective-permute-start | bytes 1327112 | tf_op jit(solution)/shard_map/ppermute | solution.py:334
  29.4 0.0 collective-permute-done.5.refs_4_
  29.4 0.0 collective-permute-done.6.refs_6_
  29.4 2.0 %copy-done.7 = bf16[9,1536,128]{2,1,0:T(8,128)(2,1)S(1)} copy-done((bf16[9,1536,128]{2,1,0:T(8,128)(2,1)S(1)}, bf16[9,1536,128]{2,1,0:T(8,128)(2,1)}, u32[]{:S(2)}) %copy-start.7) | copy-done | bytes 3538968
  31.4 9.4 %shard_map.67 = (f32[16,8,24,128]{3,2,1,0:T(8,128)S(1)}, f32[16,8,24,128]{3,2,1,0:T(8,128)S(1)}, f32[16,8,24,128]{3,2,1,0:T(8,128)S(1)}, f32[16,8,24,128]{3,2,1,0:T(8,128)S(1)}) custom-call(s32[2]{0:T(128)S(1)} %pad_add_fusion.place_ref.refs_0_, s32[576]{0:T(1024)S(1)} %reshape.13.refs_1_.refs_2_, s32[576]{0:T(1024)S(1)} %reshape.15.refs_2_.refs_3_, ...), custom_call_target="tpu_custom_call" | custom-call | flops 11000000512 | bytes 1000000 | tf_op jit(solution)/shard_map/pallas_call | solution.py:382
  40.9 0.0 collective-permute-done.3.refs_4_
  40.9 0.0 collective-permute-done.4.refs_6_
  40.9 0.1 collective-permute-start.7
  41.0 0.8 collective-permute-start.8
  41.8 0.2 collective-permute-start.10
  42.0 0.0 collective-permute-done.2.refs_5_
  42.0 0.7 collective-permute-done.7.refs_7_
  42.7 0.0 copy-done.8
  42.7 5.2 %shard_map.68.refs_1_ = bf16[1536,768]{1,0:T(8,128)(2,1)S(1)} custom-call(s32[2]{0:T(128)S(1)} %pad_add_fusion.place_ref.refs_0_, s32[8,2,32]{2,1,0:T(2,128)S(1)} %copy-done.3, s32[576]{0:T(1024)S(1)} %reshape.13.refs_1_.refs_2_, s32[576]{0:T(1024)S(1)} %reshape.15.refs_2_.refs_3_, bf16[864,256]{1,0:T(8,128)(2,1)S(1)} %collective-permute-done.1.refs_4_, ...), custom_call_target="tpu_custom_call" | custom-call | flops 6600000000 | bytes 1000000 | tf_op jit(solution)/shard_map/pallas_call | solution.py:400
  48.0 5.6 %collective-permute-done.8.refs_6_ = bf16[864,256]{1,0:T(8,128)(2,1)S(1)} collective-permute-done((bf16[864,256]{1,0:T(8,128)(2,1)S(1)}, bf16[864,256]{1,0:T(8,128)(2,1)S(1)}, u32[]{:S(2)}, u32[]{:S(2)}) %collective-permute-start.8) | collective-permute-done | bytes 442400 | tf_op jit(solution)/shard_map/ppermute | solution.py:334
  53.5 0.0 collective-permute-start.11
  53.5 1.1 %shard_map.70 = bf16[384,768]{1,0:T(8,128)(2,1)S(1)} custom-call(bf16[768,1536]{1,0:T(8,128)(2,1)S(1)} %copy-done.5, bf16[1536,768]{1,0:T(8,128)(2,1)S(1)} %shard_map.68.refs_1_), custom_call_target="tpu_custom_call" | custom-call | flops 1650000000 | bytes 1000000 | tf_op jit(solution)/shard_map/pallas_call | solution.py:416
  54.6 0.6 collective-permute-start.9
  55.2 1.1 %shard_map.69 = f32[384,768]{1,0:T(8,128)S(1)} custom-call(bf16[768,1536]{1,0:T(8,128)(2,1)S(1)} %copy-done.5, bf16[1536,768]{1,0:T(8,128)(2,1)S(1)} %shard_map.68.refs_1_), custom_call_target="tpu_custom_call" | custom-call | flops 1650000000 | bytes 1000000 | tf_op jit(solution)/shard_map/pallas_call | solution.py:416
  56.3 0.0 collective-permute-done.10.refs_5_
  56.3 0.0 collective-permute-done.11.refs_7_
  56.3 5.4 %shard_map.71.refs_1_ = bf16[1536,768]{1,0:T(8,128)(2,1)S(1)} custom-call(s32[2]{0:T(128)S(1)} %pad_add_fusion.place_ref.refs_0_, s32[8,2,32]{2,1,0:T(2,128)S(1)} %copy-done.3, s32[576]{0:T(1024)S(1)} %reshape.13.refs_1_.refs_2_, s32[576]{0:T(1024)S(1)} %reshape.15.refs_2_.refs_3_, bf16[864,256]{1,0:T(8,128)(2,1)S(1)} %collective-permute-done.3.refs_4_, ...), custom_call_target="tpu_custom_call" | custom-call | flops 6600000000 | bytes 1000000 | tf_op jit(solution)/shard_map/pallas_call | solution.py:400
  61.7 0.0 collective-permute-done.9
  61.7 0.1 convert_add_fusion.1
  61.9 1.1 %shard_map.73 = bf16[384,768]{1,0:T(8,128)(2,1)S(1)} custom-call(bf16[768,1536]{1,0:T(8,128)(2,1)S(1)} %copy-done.5, bf16[1536,768]{1,0:T(8,128)(2,1)S(1)} %shard_map.71.refs_1_), custom_call_target="tpu_custom_call" | custom-call | flops 1650000000 | bytes 1000000 | tf_op jit(solution)/shard_map/pallas_call | solution.py:416
  62.9 0.1 collective-permute-start.13
  63.1 0.9 %collective-permute-start.12 = (bf16[96,768]{1,0:T(8,128)(2,1)S(1)}, bf16[96,768]{1,0:T(8,128)(2,1)S(1)}, u32[]{:S(2)}, u32[]{:S(2)}) collective-permute-start(bf16[96,768]{1,0:T(8,128)(2,1)S(1)} %get-tuple-element.59), channel_id=1, source_target_pairs={{0,2},{1,3},{2,0},{3,1},{4,6},{5,7},{6,4},{7,5},{8,10},{9,11},{10,... | collective-permute-start | bytes 442376 | tf_op jit(solution)/shard_map/ppermute | solution.py:334
  63.9 1.1 %shard_map.72 = f32[384,768]{1,0:T(8,128)S(1)} custom-call(bf16[768,1536]{1,0:T(8,128)(2,1)S(1)} %copy-done.5, bf16[1536,768]{1,0:T(8,128)(2,1)S(1)} %shard_map.71.refs_1_), custom_call_target="tpu_custom_call" | custom-call | flops 1650000000 | bytes 1000000 | tf_op jit(solution)/shard_map/pallas_call | solution.py:416
  65.0 4.3 %collective-permute-done.12 = bf16[96,768]{1,0:T(8,128)(2,1)S(1)} collective-permute-done((bf16[96,768]{1,0:T(8,128)(2,1)S(1)}, bf16[96,768]{1,0:T(8,128)(2,1)S(1)}, u32[]{:S(2)}, u32[]{:S(2)}) %collective-permute-start.12) | collective-permute-done | bytes 147488 | tf_op jit(solution)/shard_map/ppermute | solution.py:334
  69.4 0.0 collective-permute-done.13
  69.4 0.1 fusion.3
  69.6 2.6 %collective-permute-start.14 = (bf16[192,768]{1,0:T(8,128)(2,1)S(1)}, bf16[192,768]{1,0:T(8,128)(2,1)S(1)}, u32[]{:S(2)}, u32[]{:S(2)}) collective-permute-start(bf16[192,768]{1,0:T(8,128)(2,1)S(1)} %pad_maximum_fusion), channel_id=1, source_target_pairs={{0,4},{1,5},{2,6},{3,7},{4,8},{5,9},{6,10},{7,11},{8,12},{9,13},{1... | collective-permute-start | bytes 884744 | tf_op jit(solution)/shard_map/ppermute | solution.py:334
  72.2 1.1 %collective-permute-start.16 = (bf16[192,768]{1,0:T(8,128)(2,1)S(1)}, bf16[192,768]{1,0:T(8,128)(2,1)S(1)}, u32[]{:S(2)}, u32[]{:S(2)}) collective-permute-start(bf16[192,768]{1,0:T(8,128)(2,1)S(1)} %pad_maximum_fusion.1), channel_id=1, source_target_pairs={{0,2},{1,3},{2,0},{3,1},{4,6},{5,7},{6,4},{7,5},{8,10},{9,11},{10,... | collective-permute-start | bytes 884744 | tf_op jit(solution)/shard_map/ppermute | solution.py:334
  73.4 4.7 %collective-permute-start.15 = (bf16[96,768]{1,0:T(8,128)(2,1)S(1)}, bf16[96,768]{1,0:T(8,128)(2,1)S(1)}, u32[]{:S(2)}, u32[]{:S(2)}) collective-permute-start(bf16[96,768]{1,0:T(8,128)(2,1)S(1)} %get-tuple-element.56), channel_id=1, source_target_pairs={{0,6},{1,7},{2,4},{3,5},{4,10},{5,11},{6,8},{7,9},{8,14},{9,15},{1... | collective-permute-start | bytes 442376 | tf_op jit(solution)/shard_map/ppermute | solution.py:334
  78.0 6.4 %collective-permute-done.15 = bf16[96,768]{1,0:T(8,128)(2,1)S(1)} collective-permute-done((bf16[96,768]{1,0:T(8,128)(2,1)S(1)}, bf16[96,768]{1,0:T(8,128)(2,1)S(1)}, u32[]{:S(2)}, u32[]{:S(2)}) %collective-permute-start.15) | collective-permute-done | bytes 147488 | tf_op jit(solution)/shard_map/ppermute | solution.py:334
  84.5 0.0 collective-permute-done.14
  84.5 0.0 collective-permute-done.16
  84.5 0.1 slice_add_fusion.1
  84.6 0.8 fusion.1
  (18 shorter events, 0.2 us)
Async XLA Ops:
  0.0 10.2 %copy-start = (s32[512,3]{0,1:T(4,128)S(1)}, s32[512,3]{0,1:T(4,128)}, u32[]{:S(2)}) copy-start(s32[512,3]{0,1:T(4,128)} %param.9) | copy-start | bytes 18436
  0.0 1.3 %copy-start.2 = (bf16[64,24,288]{2,1,0:T(8,128)(2,1)S(1)}, bf16[64,24,288]{2,1,0:T(8,128)(2,1)}, u32[]{:S(2)}) copy-start(bf16[64,24,288]{2,1,0:T(8,128)(2,1)} %param.7) | copy-start | bytes 2654212
  1.3 2.7 %copy-start.3 = (s32[8,2,32]{2,1,0:T(2,128)S(1)}, s32[8,2,32]{2,1,0:T(2,128)}, u32[]{:S(2)}) copy-start(s32[8,2,32]{2,1,0:T(2,128)} %refs_1_.3) | copy-start | bytes 6148
  2.4 21.7 %collective-permute-start = (bf16[1728,256]{1,0:T(8,128)(2,1)}, bf16[1728,256]{1,0:T(8,128)(2,1)}, u32[]{:S(2)}, u32[]{:S(2)}) collective-permute-start(bf16[1728,256]{1,0:T(8,128)(2,1)} %shard_map.64.p_ref.refs_3_), channel_id=1, source_target_pairs={{0,2},{1,3},{2,0},{3,1},{4,6},{5,7},{6,4},{7,5},{8,10},{9,11},{10,... | collective-permute-start | bytes 2654216 | tf_op jit(solution)/shard_map/ppermute | solution.py:334
  3.9 25.5 %collective-permute-start.5 = (bf16[1728,256]{1,0:T(8,128)(2,1)}, bf16[1728,256]{1,0:T(8,128)(2,1)}, u32[]{:S(2)}, u32[]{:S(2)}) collective-permute-start(bf16[1728,256]{1,0:T(8,128)(2,1)} %shard_map.64.p_ref.refs_3_), channel_id=1, source_target_pairs={{0,1},{1,0},{2,3},{3,2},{4,5},{5,4},{6,7},{7,6},{8,9},{9,8},{10,11... | collective-permute-start | bytes 2654216 | tf_op jit(solution)/shard_map/ppermute | solution.py:334
  4.0 7.3 %copy-start.1 = (bf16[64,24,864]{2,1,0:T(8,128)(2,1)S(1)}, bf16[64,24,864]{2,1,0:T(8,128)(2,1)}, u32[]{:S(2)}) copy-start(bf16[64,24,864]{2,1,0:T(8,128)(2,1)} %param.6) | copy-start | bytes 7962628
  6.8 15.6 %collective-permute-start.1 = (bf16[864,256]{1,0:T(8,128)(2,1)}, bf16[864,256]{1,0:T(8,128)(2,1)S(1)}, u32[]{:S(2)}, u32[]{:S(2)}) collective-permute-start(bf16[864,256]{1,0:T(8,128)(2,1)} %get-tuple-element.28), channel_id=1, source_target_pairs={{0,4},{1,5},{2,6},{3,7},{4,8},{5,9},{6,10},{7,11},{8,12},{9,13},{1... | collective-permute-start | bytes 1327112 | tf_op jit(solution)/shard_map/ppermute | solution.py:334
  11.3 16.1 %copy-start.9 = (s32[64,9]{0,1:T(8,128)S(1)}, s32[64,9]{0,1:T(8,128)}, u32[]{:S(2)}) copy-start(s32[64,9]{0,1:T(8,128)} %param.8) | copy-start | bytes 6916
  18.8 1.4 %copy-start.4 = (bf16[768,1536]{1,0:T(8,128)(2,1)}, bf16[768,1536]{1,0:T(8,128)(2,1)S(1)}, u32[]{:S(2)}) copy-start(bf16[768,1536]{1,0:T(8,128)(2,1)S(1)} %get-tuple-element.30.refs_0_) | copy-start | bytes 7077892
  20.2 1.7 %copy-start.6 = (bf16[9,1536,128]{2,1,0:T(8,128)(2,1)}, bf16[9,1536,128]{2,1,0:T(8,128)(2,1)S(1)}, u32[]{:S(2)}) copy-start(bf16[9,1536,128]{2,1,0:T(8,128)(2,1)S(1)} %get-tuple-element.34.refs_7_.refs_8_) | copy-start | bytes 10616836
  24.1 5.3 %collective-permute-start.6 = (bf16[1728,256]{1,0:T(8,128)(2,1)}, bf16[1728,256]{1,0:T(8,128)(2,1)S(1)}, u32[]{:S(2)}, u32[]{:S(2)}) collective-permute-start(bf16[1728,256]{1,0:T(8,128)(2,1)} %collective-permute-done.refs_5_), channel_id=1, source_target_pairs={{0,1},{1,0},{2,3},{3,2},{4,5},{5,4},{6,7},{7,6},{8,9},{9,8},{10,11... | collective-permute-start | bytes 2654216 | tf_op jit(solution)/shard_map/ppermute | solution.py:334
  24.1 16.8 %collective-permute-start.3 = (bf16[864,256]{1,0:T(8,128)(2,1)}, bf16[864,256]{1,0:T(8,128)(2,1)S(1)}, u32[]{:S(2)}, u32[]{:S(2)}) collective-permute-start(bf16[864,256]{1,0:T(8,128)(2,1)} %get-tuple-element.32), channel_id=1, source_target_pairs={{4,0},{5,1},{6,2},{7,3},{8,4},{9,5},{10,6},{11,7},{12,8},{13,9},{1... | collective-permute-start | bytes 1327112 | tf_op jit(solution)/shard_map/ppermute | solution.py:334
  27.6 14.4 %collective-permute-start.2 = (bf16[864,256]{1,0:T(8,128)(2,1)S(1)}, bf16[864,256]{1,0:T(8,128)(2,1)S(1)}, u32[]{:S(2)}, u32[]{:S(2)}) collective-permute-start(bf16[864,256]{1,0:T(8,128)(2,1)S(1)} %collective-permute-done.1.refs_4_), channel_id=1, source_target_pairs={{0,1},{1,0},{2,3},{3,2},{4,5},{5,4},{6,7},{7,6},{8,9},{9,8},{10,11... | collective-permute-start | bytes 1327112 | tf_op jit(solution)/shard_map/ppermute | solution.py:334
  27.9 13.0 %collective-permute-start.4 = (bf16[864,256]{1,0:T(8,128)(2,1)S(1)}, bf16[864,256]{1,0:T(8,128)(2,1)S(1)}, u32[]{:S(2)}, u32[]{:S(2)}) collective-permute-start(bf16[864,256]{1,0:T(8,128)(2,1)S(1)} %collective-permute-done.1.refs_4_), channel_id=1, source_target_pairs={{0,2},{1,3},{2,0},{3,1},{4,6},{5,7},{6,4},{7,5},{8,10},{9,11},{10,... | collective-permute-start | bytes 1327112 | tf_op jit(solution)/shard_map/ppermute | solution.py:334
  29.4 2.0 %copy-start.7 = (bf16[9,1536,128]{2,1,0:T(8,128)(2,1)S(1)}, bf16[9,1536,128]{2,1,0:T(8,128)(2,1)}, u32[]{:S(2)}) copy-start(bf16[9,1536,128]{2,1,0:T(8,128)(2,1)} %copy-done.6) | copy-start | bytes 10616836
  31.4 11.3 %copy-start.8 = (bf16[9,1536,128]{2,1,0:T(8,128)(2,1)S(1)}, bf16[9,1536,128]{2,1,0:T(8,128)(2,1)}, u32[]{:S(2)}) copy-start(bf16[9,1536,128]{2,1,0:T(8,128)(2,1)} %copy-done.6) | copy-start | bytes 10616836
  40.9 1.9 %collective-permute-start.7 = (bf16[864,256]{1,0:T(8,128)(2,1)S(1)}, bf16[864,256]{1,0:T(8,128)(2,1)S(1)}, u32[]{:S(2)}, u32[]{:S(2)}) collective-permute-start(bf16[864,256]{1,0:T(8,128)(2,1)S(1)} %collective-permute-done.4.refs_6_), channel_id=1, source_target_pairs={{0,1},{1,0},{2,3},{3,2},{4,5},{5,4},{6,7},{7,6},{8,9},{9,8},{10,11... | collective-permute-start | bytes 1327112 | tf_op jit(solution)/shard_map/ppermute | solution.py:334
  41.0 12.6 %collective-permute-start.8 = (bf16[864,256]{1,0:T(8,128)(2,1)S(1)}, bf16[864,256]{1,0:T(8,128)(2,1)S(1)}, u32[]{:S(2)}, u32[]{:S(2)}) collective-permute-start(bf16[864,256]{1,0:T(8,128)(2,1)S(1)} %collective-permute-done.3.refs_4_), channel_id=1, source_target_pairs={{0,2},{1,3},{2,0},{3,1},{4,6},{5,7},{6,4},{7,5},{8,10},{9,11},{10,... | collective-permute-start | bytes 1327112 | tf_op jit(solution)/shard_map/ppermute | solution.py:334
  41.8 14.5 %collective-permute-start.10 = (bf16[864,256]{1,0:T(8,128)(2,1)S(1)}, bf16[864,256]{1,0:T(8,128)(2,1)S(1)}, u32[]{:S(2)}, u32[]{:S(2)}) collective-permute-start(bf16[864,256]{1,0:T(8,128)(2,1)S(1)} %collective-permute-done.3.refs_4_), channel_id=1, source_target_pairs={{0,1},{1,0},{2,3},{3,2},{4,5},{5,4},{6,7},{7,6},{8,9},{9,8},{10,11... | collective-permute-start | bytes 1327112 | tf_op jit(solution)/shard_map/ppermute | solution.py:334
  42.7 10.8 %copy-start.5 = (bf16[768,1536]{1,0:T(8,128)(2,1)S(1)}, bf16[768,1536]{1,0:T(8,128)(2,1)}, u32[]{:S(2)}) copy-start(bf16[768,1536]{1,0:T(8,128)(2,1)} %copy-done.4) | copy-start | bytes 7077892
  53.5 2.8 %collective-permute-start.11 = (bf16[864,256]{1,0:T(8,128)(2,1)S(1)}, bf16[864,256]{1,0:T(8,128)(2,1)S(1)}, u32[]{:S(2)}, u32[]{:S(2)}) collective-permute-start(bf16[864,256]{1,0:T(8,128)(2,1)S(1)} %collective-permute-done.8.refs_6_), channel_id=1, source_target_pairs={{0,1},{1,0},{2,3},{3,2},{4,5},{5,4},{6,7},{7,6},{8,9},{9,8},{10,11... | collective-permute-start | bytes 1327112 | tf_op jit(solution)/shard_map/ppermute | solution.py:334
  54.6 7.0 %collective-permute-start.9 = (bf16[384,768]{1,0:T(8,128)(2,1)S(1)}, bf16[384,768]{1,0:T(8,128)(2,1)S(1)}, u32[]{:S(2)}, u32[]{:S(2)}) collective-permute-start(bf16[384,768]{1,0:T(8,128)(2,1)S(1)} %shard_map.70), channel_id=1, source_target_pairs={{0,1},{1,0},{2,3},{3,2},{4,5},{5,4},{6,7},{7,6},{8,9},{9,8},{10,11... | collective-permute-start | bytes 1769480 | tf_op jit(solution)/shard_map/ppermute | solution.py:334
  62.9 6.5 %collective-permute-start.13 = (bf16[384,768]{1,0:T(8,128)(2,1)S(1)}, bf16[384,768]{1,0:T(8,128)(2,1)S(1)}, u32[]{:S(2)}, u32[]{:S(2)}) collective-permute-start(bf16[384,768]{1,0:T(8,128)(2,1)S(1)} %shard_map.73), channel_id=1, source_target_pairs={{0,1},{1,0},{2,3},{3,2},{4,5},{5,4},{6,7},{7,6},{8,9},{9,8},{10,11... | collective-permute-start | bytes 1769480 | tf_op jit(solution)/shard_map/ppermute | solution.py:334
  63.1 6.3 %collective-permute-start.12 = (bf16[96,768]{1,0:T(8,128)(2,1)S(1)}, bf16[96,768]{1,0:T(8,128)(2,1)S(1)}, u32[]{:S(2)}, u32[]{:S(2)}) collective-permute-start(bf16[96,768]{1,0:T(8,128)(2,1)S(1)} %get-tuple-element.59), channel_id=1, source_target_pairs={{0,2},{1,3},{2,0},{3,1},{4,6},{5,7},{6,4},{7,5},{8,10},{9,11},{10,... | collective-permute-start | bytes 442376 | tf_op jit(solution)/shard_map/ppermute | solution.py:334
  69.6 14.8 %collective-permute-start.14 = (bf16[192,768]{1,0:T(8,128)(2,1)S(1)}, bf16[192,768]{1,0:T(8,128)(2,1)S(1)}, u32[]{:S(2)}, u32[]{:S(2)}) collective-permute-start(bf16[192,768]{1,0:T(8,128)(2,1)S(1)} %pad_maximum_fusion), channel_id=1, source_target_pairs={{0,4},{1,5},{2,6},{3,7},{4,8},{5,9},{6,10},{7,11},{8,12},{9,13},{1... | collective-permute-start | bytes 884744 | tf_op jit(solution)/shard_map/ppermute | solution.py:334
  72.2 12.2 %collective-permute-start.16 = (bf16[192,768]{1,0:T(8,128)(2,1)S(1)}, bf16[192,768]{1,0:T(8,128)(2,1)S(1)}, u32[]{:S(2)}, u32[]{:S(2)}) collective-permute-start(bf16[192,768]{1,0:T(8,128)(2,1)S(1)} %pad_maximum_fusion.1), channel_id=1, source_target_pairs={{0,2},{1,3},{2,0},{3,1},{4,6},{5,7},{6,4},{7,5},{8,10},{9,11},{10,... | collective-permute-start | bytes 884744 | tf_op jit(solution)/shard_map/ppermute | solution.py:334
  73.4 11.1 %collective-permute-start.15 = (bf16[96,768]{1,0:T(8,128)(2,1)S(1)}, bf16[96,768]{1,0:T(8,128)(2,1)S(1)}, u32[]{:S(2)}, u32[]{:S(2)}) collective-permute-start(bf16[96,768]{1,0:T(8,128)(2,1)S(1)} %get-tuple-element.56), channel_id=1, source_target_pairs={{0,6},{1,7},{2,4},{3,5},{4,10},{5,11},{6,8},{7,9},{8,14},{9,15},{1... | collective-permute-start | bytes 442376 | tf_op jit(solution)/shard_map/ppermute | solution.py:334

commit v5 on v4

--- a/solution.py
+++ b/solution.py
@@ -203,15 +203,8 @@
                 sums[u][step, where[j]] = held[j] + got[:, 128 * j : 128 * j + 128]
 
 
-def own_kernel(place_ref, aggs_ref, cols_ref, *refs, parts):
-    part = place_ref[0]
-    a_hbm, sums, (prolong, a_ref, sem) = refs[4], refs[5 : 5 + UN], refs[5 + UN :]
-    a_copy = pltpu.make_async_copy(a_hbm, a_ref, sem)
-    a_copy.start()
-    unpack(NB, refs[0:4], prolong)
-    a_copy.wait()
+def own_rows(part, parts, cols_ref, aggs_ref):
     own = part * NB - window_start(part, parts)
-    base = part * NAG
 
     def row_of(i, slot):
         row = cols_ref[KA * i + slot]
@@ -220,82 +213,161 @@
         return row, row
 
     def blocks_of(row):
-        return [aggs_ref[KP * (own + row) + j] - base for j in range(KP)]
-
-    def run(slots, fresh):
+        return [aggs_ref[KP * (own + row) + j] - part * NAG for j in range(KP)]
+
+    return row_of, blocks_of
+
+
+def own_kernel(place_ref, aggs_ref, cols_ref, *refs, parts):
+    part = place_ref[0]
+    a_hbm, prolong, sums, (a_ref, sem) = refs[4], refs[5], refs[6 : 6 + UN], refs[6 + UN :]
+    a_copy = pltpu.make_async_copy(a_hbm, a_ref, sem)
+    a_copy.start()
+    unpack(NB, refs[0:4], prolong)
+    a_copy.wait()
+    row_of, blocks_of = own_rows(part, parts, cols_ref, aggs_ref)
+
+    def step(n, carry):
+        for each in sums:
+            each[n] = jnp.zeros((8, W, 128), F32)
+        add_products(n, range(5), a_ref, 0, prolong, row_of, blocks_of, sums)
+        return carry
+
+    lax.fori_loop(0, STEPS, step, 0, unroll=4)
+
+
+def halo_rows_of(part, parts, upper, halo_ref, cols_ref, aggs_ref):
+    other = jnp.minimum(part + 1, parts - 1) if upper else jnp.maximum(part - 1, 0)
+    rows_at = other * NB - window_start(part, parts)
+
+    def row_of(i, slot):
+        at = cols_ref[KA * i + slot]
+        return at, rows_at + halo_ref[other, 0 if upper else 1, at]
+
+    def blocks_of(row):
+        return [aggs_ref[KP * row + j] - other * NAG for j in range(KP)]
+
+    return row_of, blocks_of
+
+
+def couple(n, block_of, coupled):
+    lane = lax.broadcasted_iota(I32, (48, 128), 1)
+    for two in range(2):
+        rows = pl.ds(pl.multiple_of(n * (UN * W) + 48 * two, 48), 48)
+        for half in range(2):
+            y0, y1, y2, y3 = [
+                jnp.concatenate([block_of(2 * two, c), block_of(2 * two + 1, c)], axis=0)
+                for c in range(4 * half, 4 * half + 4)
+            ]
+            y1, y2, y3 = pltpu.roll(y1, 96, 1), pltpu.roll(y2, 64, 1), pltpu.roll(y3, 32, 1)
+            tiles = [
+                jnp.where(lane < 96, y0, y1),
+                jnp.where(lane < 64, y1, y2),
+                jnp.where(lane < 32, y2, y3),
+            ]
+            for x in range(3):
+                at = 384 * half + 128 * x
+                coupled[rows, at : at + 128] = tiles[x].astype(BF16)
+
+
+def lower_kernel(place_ref, halo_ref, aggs_ref, cols_ref, *refs, parts):
+    sources, a_hbm, own_hbm, own, coupled, above = refs[0:4], refs[4], refs[5], refs[6:10], refs[10], refs[11:15]
+    prolong, a_ref, sums, sem, own_sem = refs[15], refs[16], refs[17:21], refs[21], refs[22]
+    part = place_ref[0]
+    a_copy = pltpu.make_async_copy(a_hbm.at[5:9], a_ref, sem)
+    a_copy.start()
+    own_row, own_block = own_rows(part, parts, cols_ref, aggs_ref)
+    row_of, blocks_of = halo_rows_of(part, parts, False, halo_ref, cols_ref, aggs_ref)
+
+    def swapped(row):
+        return [jnp.bitwise_xor(c, NAG) for c in own_block(row)]
+
+    def clear(n):
+        for each in sums:
+            each[n] = jnp.zeros((8, W, 128), F32)
+
+    def fetch_own():
+        copy = pltpu.make_async_copy(own_hbm, prolong, own_sem)
+        copy.start()
+        copy.wait()
+
+    def finish(n):
+        couple(n, lambda u, c: sums[u][n, c] + own[u][n, c - NAG] if c >= NAG else sums[u][n, c], coupled)
+        for u in range(UN):
+            above[u][n] = own[u][n, NAG : 2 * NAG]
+
+    @pl.when(part == parts - 1)
+    def _():
+        fetch_own()
+        a_copy.wait()
+
         def step(n, carry):
-            if fresh:
-                for each in sums:
-                    each[n] = jnp.zeros((8, W, 128), F32)
-            add_products(n, slots, a_ref, 0, prolong, row_of, blocks_of, sums)
+            clear(n)
+            add_products(n, (7, 8), a_ref, 5, prolong, own_row, swapped, sums)
             return carry
 
-        lax.fori_loop(0, STEPS, step, 0, unroll=2 if fresh else 1)
-
-    run((0, 1, 2, 3, 4), True)
+        lax.fori_loop(0, STEPS, step, 0, unroll=2)
+        unpack(NS, sources, prolong)
+
+        def step(n, carry):
+            add_products(n, (5, 6), a_ref, 5, prolong, row_of, blocks_of, sums)
+            finish(n)
+            return carry
+
+        lax.fori_loop(0, STEPS, step, 0, unroll=2)
 
     @pl.when(part == 0)
     def _():
-        run((5, 6), False)
-
-    @pl.when(part == parts - 1)
+        fetch_own()
+        a_copy.wait()
+
+        def step(n, carry):
+            clear(n)
+            add_products(n, (5, 6), a_ref, 5, prolong, own_row, swapped, sums)
+            nothing = jnp.zeros((W, 128), F32)
+            couple(n, lambda u, c: sums[u][n, c] + own[u][n, c - NAG] if c >= NAG else nothing, coupled)
+            for u in range(UN):
+                above[u][n] = own[u][n, NAG : 2 * NAG] + sums[u][n, 0:NAG]
+            return carry
+
+        lax.fori_loop(0, STEPS, step, 0, unroll=2)
+
+    @pl.when(jnp.logical_and(part > 0, part < parts - 1))
     def _():
-        run((7, 8), False)
-
-
-def halo_kernel(place_ref, halo_ref, aggs_ref, cols_ref, *refs, parts, upper):
-    sources, a_hbm, own, coupled = refs[0:4], refs[4], refs[5:9], refs[9]
+        unpack(NS, sources, prolong)
+        a_copy.wait()
+
+        def step(n, carry):
+            clear(n)
+            add_products(n, (5, 6), a_ref, 5, prolong, row_of, blocks_of, sums)
+            finish(n)
+            return carry
+
+        lax.fori_loop(0, STEPS, step, 0, unroll=2)
+
+
+def upper_kernel(place_ref, halo_ref, aggs_ref, cols_ref, *refs, parts):
+    sources, a_hbm, above, coupled = refs[0:4], refs[4], refs[5:9], refs[9]
     prolong, a_ref, sums, sem = refs[10], refs[11], refs[12:16], refs[16]
     part = place_ref[0]
-    slots = (7, 8) if upper else (5, 6)
-    other = jnp.minimum(part + 1, parts - 1) if upper else jnp.maximum(part - 1, 0)
-    rows_at = other * NB - window_start(part, parts)
-    inside = part < parts - 1 if upper else part > 0
-    a_copy = pltpu.make_async_copy(a_hbm.at[slots[0] : slots[0] + 2], a_ref, sem)
+    a_copy = pltpu.make_async_copy(a_hbm.at[7:9], a_ref, sem)
     a_copy.start()
+    row_of, blocks_of = halo_rows_of(part, parts, True, halo_ref, cols_ref, aggs_ref)
+    inside = part < parts - 1
 
     @pl.when(inside)
     def _():
         unpack(NS, sources, prolong)
 
     a_copy.wait()
-
-    lane = lax.broadcasted_iota(I32, (48, 128), 1)
-
-    def row_of(i, slot):
-        at = cols_ref[KA * i + slot]
-        return at, rows_at + halo_ref[other, 0 if upper else 1, at]
-
-    def blocks_of(row):
-        return [aggs_ref[KP * row + j] - other * NAG for j in range(KP)]
-
-    def sum_of(n, u, c):
-        if upper:
-            return sums[u][n, c] + own[u][n, NAG + c] if c < NAG else sums[u][n, c]
-        return sums[u][n, c] + own[u][n, c - NAG] if c >= NAG else sums[u][n, c]
 
     def run(products):
         def step(n, carry):
             for each in sums:
                 each[n] = jnp.zeros((8, W, 128), F32)
             if products:
-                add_products(n, slots, a_ref, slots[0], prolong, row_of, blocks_of, sums)
-            for two in range(2):
-                rows = pl.ds(pl.multiple_of(n * (UN * W) + 48 * two, 48), 48)
-                for half in range(2):
-                    y0, y1, y2, y3 = [
-                        jnp.concatenate([sum_of(n, 2 * two, c), sum_of(n, 2 * two + 1, c)], axis=0)
-                        for c in range(4 * half, 4 * half + 4)
-                    ]
-                    y1, y2, y3 = pltpu.roll(y1, 96, 1), pltpu.roll(y2, 64, 1), pltpu.roll(y3, 32, 1)
-                    tiles = [
-                        jnp.where(lane < 96, y0, y1),
-                        jnp.where(lane < 64, y1, y2),
-                        jnp.where(lane < 32, y2, y3),
-                    ]
-                    for x in range(3):
-                        at = 384 * half + 128 * x
-                        coupled[rows, at : at + 128] = tiles[x].astype(BF16)
+                add_products(n, (7, 8), a_ref, 7, prolong, row_of, blocks_of, sums)
+            couple(n, lambda u, c: sums[u][n, c] + above[u][n, c] if c < NAG else sums[u][n, c], coupled)
             return carry
 
         lax.fori_loop(0, STEPS, step, 0, unroll=2 if products else 1)
@@ -379,63 +451,79 @@
     low_far = moved(low, 0, 2)
 
     sums_type = jax.ShapeDtypeStruct((STEPS, 8, W, 128), F32)
-    own = pl.pallas_call(
+    prolong_type = jax.ShapeDtypeStruct((NB, BW, KP * 128), BF16)
+    prolong, *own = pl.pallas_call(
         lambda *refs: own_kernel(*refs, parts=parts),
-        out_shape=[sums_type] * UN,
+        out_shape=[prolong_type] + [sums_type] * UN,
         in_specs=[in_smem()] * 3 + [in_vmem()] * 4 + [in_hbm()],
-        out_specs=[in_vmem()] * UN,
-        scratch_shapes=[
-            pltpu.VMEM((NB, BW, KP * 128), BF16),
-            pltpu.VMEM((KA, ROWS, 128), BF16),
-            pltpu.SemaphoreType.DMA,
-        ],
+        out_specs=[in_vmem()] * (1 + UN),
+        scratch_shapes=[pltpu.VMEM((KA, ROWS, 128), BF16), pltpu.SemaphoreType.DMA],
         compiler_params=params(),
         cost_estimate=cost(10),
     )(place, aggs, cols, *both_cores(own_pack, near), blocks)
     up, low_far, first_sums = lax.optimization_barrier((up, low_far, own[0]))
     own = (first_sums, *own[1:])
     up_far = moved(up, 0, 2)
-
-    def coupled_of(upper, sources):
+    coupled_type = jax.ShapeDtypeStruct((ROWS, 8 * BC), BF16)
+    above_type = jax.ShapeDtypeStruct((STEPS, NAG, W, 128), F32)
+    sums_scratch = [pltpu.VMEM((STEPS, 8, W, 128), F32)] * UN
+    low_coupled, *above = pl.pallas_call(
+        lambda *refs: lower_kernel(*refs, parts=parts),
+        out_shape=[coupled_type] + [above_type] * UN,
+        in_specs=[in_smem()] * 4 + [in_vmem()] * 4 + [in_hbm()] * 2 + [in_vmem()] * UN,
+        out_specs=[in_vmem()] * (1 + UN),
+        scratch_shapes=[
+            pltpu.VMEM((NB, BW, KP * 128), BF16),
+            pltpu.VMEM((4, ROWS, 128), BF16),
+            *sums_scratch,
+            pltpu.SemaphoreType.DMA,
+            pltpu.SemaphoreType.DMA,
+        ],
+        compiler_params=params(),
+        cost_estimate=cost(6),
+    )(place, halo_rows, aggs, cols, *both_cores(low, low_far), blocks, prolong, *own)
+
+    def upper_coupled(sources, above):
         return pl.pallas_call(
-            lambda *refs: halo_kernel(*refs, parts=parts, upper=upper),
-            out_shape=jax.ShapeDtypeStruct((ROWS, 8 * BC), BF16),
+            lambda *refs: upper_kernel(*refs, parts=parts),
+            out_shape=coupled_type,
             in_specs=[in_smem()] * 4 + [in_vmem()] * 4 + [in_hbm()] + [in_vmem()] * UN,
             out_specs=in_vmem(),
             scratch_shapes=[
                 pltpu.VMEM((NS, BW, KP * 128), BF16),
                 pltpu.VMEM((2, ROWS, 128), BF16),
-                *[pltpu.VMEM((STEPS, 8, W, 128), F32)] * UN,
+                *sums_scratch,
                 pltpu.SemaphoreType.DMA,
             ],
             compiler_params=params(),
             cost_estimate=cost(6),
-        )(place, halo_rows, aggs, cols, *sources, blocks, *own)
-
-    def coarse_of(coupled, half):
+        )(place, halo_rows, aggs, cols, *sources, blocks, *above)
+
+    def coarse_of(coupled, half, weight):
         return pl.pallas_call(
             lambda *refs: coarse_kernel(*refs, half=half),
             out_shape=jax.ShapeDtypeStruct((4 * BC, 8 * BC), F32 if half else BF16),
             in_specs=[in_vmem()] * 2,
             out_specs=in_vmem(),
             compiler_params=params(),
-            cost_estimate=cost(1.5),
+            cost_estimate=cost(weight),
         )(spread, coupled)
 
-    low_coupled = coupled_of(False, both_cores(low, low_far))
-    low_coupled, up_far = lax.optimization_barrier((low_coupled, up_far))
-    low_came = moved(coarse_of(low_coupled, 0), 0, 1)
-    low_keep = coarse_of(low_coupled, 1)
-    up_sources = both_cores(up, up_far)
+    low_came = moved(coarse_of(low_coupled, 0, 0.01), 0, 1)
+    low_keep = coarse_of(low_coupled, 1, 0.01)
+    low_keep, up_far = lax.optimization_barrier((low_keep, up_far))
+    *up_sources, last_source = both_cores(up, up_far)
+    low_came, last_source = lax.optimization_barrier((low_came, last_source))
+    up_sources = (*up_sources, last_source)
     low_both = low_keep + low_came.astype(F32)
     low_away = low_both[: 2 * BC].astype(BF16)
-    up_coupled = coupled_of(True, up_sources)
-    low_away, up_coupled = lax.optimization_barrier((low_away, up_coupled))
+    low_away, first_above = lax.optimization_barrier((low_away, above[0]))
     low_far_next = moved(low_away[BC:], 0, 2)
+    up_coupled = upper_coupled(up_sources, (first_above, *above[1:]))
+    low_far_next, up_coupled = lax.optimization_barrier((low_far_next, up_coupled))
     low_next = (low_both[3 * BC :] + low_far_next.astype(F32)).astype(BF16)
-    up_came = moved(coarse_of(up_coupled, 0), 0, 1)
-    up_keep = coarse_of(up_coupled, 1)
-    low_next, up_keep = lax.optimization_barrier((low_next, up_keep))
+    up_came = moved(coarse_of(up_coupled, 0, 1.5), 0, 1)
+    up_keep = coarse_of(up_coupled, 1, 1.5)
     up_both = up_keep + up_came.astype(F32)
     away = up_both.astype(BF16)
     near_next = moved(jnp.concatenate([low_next, away[3 * BC :]], axis=0), 1, 0)

time: 86.2 us -> 82.6 us (0.958)
  waiting for transfers between devices: 19.3 us -> 16 us
  Pallas kernels: 35.7 us -> 33.7 us
  starting transfers between devices: 21 us -> 22.3 us
    ppermute x17, waiting for transfers between devices: 19.3 us -> 16 us  [moved(): return lax.ppermute(x, AXES, route)]
    ppermute x17, starting transfers between devices: 21 us -> 22.3 us  [moved(): return lax.ppermute(x, AXES, route)]
    pallas_call x1, Pallas kernels: 1.09 us -> 0.15 us  [local(): pl.pallas_call(pack_own_kernel, out_shape=packed(NB), in_specs=[in_vmem()...]
    unnamed x21 -> x17, local copies, waits for them, and re-layouts: 6.53 us -> 6.9 us
  transfers between devices with their start and end apart: 17 -> 17, of which waited for: 6 -> 7; matrix products, arithmetic and copies ran while one was open for 1% -> 1% of each run, Pallas kernels for 39% -> 40%
where the time goes in v5:
time: 82.6 us; the launch traced here: 81.8 us
  Pallas kernels  33.7 us (41%)
  starting transfers between devices  22.3 us (27%)
  waiting for transfers between devices  16 us (19%)
  local copies, waits for them, and re-layouts  7.52 us (9%)
  other arithmetic  1.33 us (2%)
  between operations  0.94 us (1%)
    ppermute x17, starting transfers between devices, moved(): return lax.ppermute(x, AXES, route)  22.3 us
    ppermute x17, waiting for transfers between devices, moved(): return lax.ppermute(x, AXES, route)  16 us
    pallas_call x1, Pallas kernels, local(): pl.pallas_call(lambda *refs: own_kernel(*refs, parts=parts), out_shape=[p...  8.91 us
    unnamed x17, local copies, waits for them, and re-layouts  6.9 us
    pallas_call x1, Pallas kernels, local(): pl.pallas_call(lambda *refs: prepare_kernel(*refs, parts=parts), out_shap...  6.86 us
    pallas_call x1, Pallas kernels, upper_coupled(): pl.pallas_call(lambda *refs: upper_kernel(*refs, parts=parts), out_shape=...  5.67 us
    pallas_call x1, Pallas kernels, local(): pl.pallas_call(lambda *refs: lower_kernel(*refs, parts=parts), out_shape=...  5.66 us
    pallas_call x4, Pallas kernels, coarse_of(): pl.pallas_call(lambda *refs: coarse_kernel(*refs, half=half), out_shape=j...  4.3 us
  transfers between devices with their start and end apart: 17, of which 7 were waited for; matrix products, arithmetic and copies ran while one was open for 1% of the time, Pallas kernels for 40%

profile of v5, /device:TPU:16, one launch (start us, length us, event | category | flops | bytes accessed | tf_op | source)
XLA Modules:
  0.0 81.8 jit_solution(1721982087179016273)
XLA Ops:
  0.0 0.0 copy-start
  0.0 1.3 %copy-done.2 = bf16[64,24,288]{2,1,0:T(8,128)(2,1)S(1)} copy-done((bf16[64,24,288]{2,1,0:T(8,128)(2,1)S(1)}, bf16[64,24,288]{2,1,0:T(8,128)(2,1)}, u32[]{:S(2)}) %copy-start.2) | copy-done | bytes 884760
  1.3 0.1 shard_map.64.p_ref.refs_3_
  1.4 0.1 collective-permute-start.5
  1.5 1.6 %collective-permute-start = (bf16[1728,256]{1,0:T(8,128)(2,1)S(1)}, bf16[1728,256]{1,0:T(8,128)(2,1)}, u32[]{:S(2)}, u32[]{:S(2)}) collective-permute-start(bf16[1728,256]{1,0:T(8,128)(2,1)S(1)} %shard_map.64.p_ref.refs_3_), channel_id=1, source_target_pairs={{0,2},{1,3},{2,0},{3,1},{4,6},{5,7},{6,4},{7,5},{8,10},{9,11},{10,... | collective-permute-start | bytes 2654216 | tf_op jit(solution)/shard_map/ppermute | solution.py:406
  3.1 0.1 pad_add_fusion.place_ref.refs_0_
  3.2 0.0 copy-done.3
  3.2 2.2 %shard_map.65 = (bf16[864,256]{1,0:T(8,128)(2,1)}, bf16[864,256]{1,0:T(8,128)(2,1)}) custom-call(s32[2]{0:T(128)S(1)} %pad_add_fusion.place_ref.refs_0_, s32[8,2,32]{2,1,0:T(2,128)S(1)} %copy-done.3, bf16[1728,256]{1,0:T(8,128)(2,1)S(1)} %shard_map.64.p_ref.refs_3_), custom_call_target="tpu_custom_call" | custom-call | flops 3300000000 | bytes 1000000 | tf_op jit(solution)/shard_map/pallas_call | solution.py:421
  5.3 3.4 %collective-permute-start.1 = (bf16[864,256]{1,0:T(8,128)(2,1)}, bf16[864,256]{1,0:T(8,128)(2,1)}, u32[]{:S(2)}, u32[]{:S(2)}) collective-permute-start(bf16[864,256]{1,0:T(8,128)(2,1)} %get-tuple-element.36), channel_id=1, source_target_pairs={{0,4},{1,5},{2,6},{3,7},{4,8},{5,9},{6,10},{7,11},{8,12},{9,13},{1... | collective-permute-start | bytes 1327112 | tf_op jit(solution)/shard_map/ppermute | solution.py:406
  9.4 0.0 copy-done
  9.4 0.1 constant_dynamic-slice_fusion
  9.5 0.1 copy.7
  9.6 0.2 reshape.13.refs_1_.refs_2_
  9.8 0.0 copy-start.1
  9.8 1.8 %copy-done.1 = bf16[64,24,864]{2,1,0:T(8,128)(2,1)S(1)} copy-done((bf16[64,24,864]{2,1,0:T(8,128)(2,1)S(1)}, bf16[64,24,864]{2,1,0:T(8,128)(2,1)}, u32[]{:S(2)}) %copy-start.1) | copy-done | bytes 2654232
  11.6 6.9 %shard_map.66 = (bf16[768,1536]{1,0:T(8,128)(2,1)S(1)}, bf16[9,1536,128]{2,1,0:T(8,128)(2,1)S(1)}) custom-call(s32[2]{0:T(128)S(1)} %pad_add_fusion.place_ref.refs_0_, s32[576]{0:T(1024)S(1)} %reshape.13.refs_1_.refs_2_, s32[1]{0:T(128)S(6)} %copy.9.refs_2_, bf16[1728,256]{1,0:T(8,128)(2,1)S(1)} %shard_map.64.p_ref.refs_3_, bf16[1536,864]{1,0:T(8,128)(2,1)S(1)} %bitcast.4), custom_call_target="tpu_custom_call" | custom-call | flops 9900000256 | bytes 1000000 | tf_op jit(solution)/shard_map/pallas_call | solution.py:438
  18.5 0.0 copy-start.4
  18.5 1.7 %copy-done.4 = bf16[9,1536,128]{2,1,0:T(8,128)(2,1)} copy-done((bf16[9,1536,128]{2,1,0:T(8,128)(2,1)}, bf16[9,1536,128]{2,1,0:T(8,128)(2,1)S(1)}, u32[]{:S(2)}) %copy-start.4) | copy-done | bytes 3538968
  20.2 0.5 collective-permute-done.1.refs_4_
  20.7 3.0 %collective-permute-done.refs_5_ = bf16[1728,256]{1,0:T(8,128)(2,1)} collective-permute-done((bf16[1728,256]{1,0:T(8,128)(2,1)S(1)}, bf16[1728,256]{1,0:T(8,128)(2,1)}, u32[]{:S(2)}, u32[]{:S(2)}) %collective-permute-start) | collective-permute-done | bytes 884768 | tf_op jit(solution)/shard_map/ppermute | solution.py:406
  23.7 0.0 collective-permute-start.6
  23.7 3.3 %collective-permute-start.3 = (bf16[864,256]{1,0:T(8,128)(2,1)}, bf16[864,256]{1,0:T(8,128)(2,1)}, u32[]{:S(2)}, u32[]{:S(2)}) collective-permute-start(bf16[864,256]{1,0:T(8,128)(2,1)} %get-tuple-element.40), channel_id=1, source_target_pairs={{4,0},{5,1},{6,2},{7,3},{8,4},{9,5},{10,6},{11,7},{12,8},{13,9},{1... | collective-permute-start | bytes 1327112 | tf_op jit(solution)/shard_map/ppermute | solution.py:406
  27.0 0.0 copy-done.7
  27.0 0.1 copy.8
  27.1 0.1 reshape.15.refs_2_.refs_3_
  27.2 1.6 %collective-permute-start.4 = (bf16[864,256]{1,0:T(8,128)(2,1)}, bf16[864,256]{1,0:T(8,128)(2,1)S(1)}, u32[]{:S(2)}, u32[]{:S(2)}) collective-permute-start(bf16[864,256]{1,0:T(8,128)(2,1)} %collective-permute-done.1.refs_4_), channel_id=1, source_target_pairs={{0,2},{1,3},{2,0},{3,1},{4,6},{5,7},{6,4},{7,5},{8,10},{9,11},{10,... | collective-permute-start | bytes 1327112 | tf_op jit(solution)/shard_map/ppermute | solution.py:406
  28.8 0.0 collective-permute-start.2
  28.8 0.0 collective-permute-done.5.refs_4_
  28.8 0.0 collective-permute-done.6.refs_6_
  28.8 2.0 %copy-done.5 = bf16[9,1536,128]{2,1,0:T(8,128)(2,1)S(1)} copy-done((bf16[9,1536,128]{2,1,0:T(8,128)(2,1)S(1)}, bf16[9,1536,128]{2,1,0:T(8,128)(2,1)}, u32[]{:S(2)}) %copy-start.5) | copy-done | bytes 3538968
  30.8 8.9 %shard_map.67 = (bf16[64,96,384]{2,1,0:T(8,128)(2,1)S(1)}, f32[16,8,24,128]{3,2,1,0:T(8,128)S(1)}, f32[16,8,24,128]{3,2,1,0:T(8,128)S(1)}, f32[16,8,24,128]{3,2,1,0:T(8,128)S(1)}, f32[16,8,24,128]{3,2,1,0:T(8,128)S(1)}) custom-call(s32[2]{0:T(128)S(1)} %pad_add_fusion.place_ref.refs_0_, s32[576]{0:T(1024)S(1)} %reshape.13.refs_1_.refs_2_, ...), custom_call_target="tpu_custom_call" | custom-call | flops 11000000512 | bytes 1000000 | tf_op jit(solution)/shard_map/pallas_call | solution.py:455
  39.7 0.0 collective-permute-done.3.refs_4_
  39.7 0.0 collective-permute-done.4.refs_6_
  39.8 0.5 collective-permute-start.7
  40.3 1.0 %collective-permute-start.8 = (bf16[864,256]{1,0:T(8,128)(2,1)}, bf16[864,256]{1,0:T(8,128)(2,1)S(1)}, u32[]{:S(2)}, u32[]{:S(2)}) collective-permute-start(bf16[864,256]{1,0:T(8,128)(2,1)} %collective-permute-done.3.refs_4_), channel_id=1, source_target_pairs={{0,2},{1,3},{2,0},{3,1},{4,6},{5,7},{6,4},{7,5},{8,10},{9,11},{10,... | collective-permute-start | bytes 1327112 | tf_op jit(solution)/shard_map/ppermute | solution.py:406
  41.3 0.0 collective-permute-done.2.refs_5_
  41.3 0.4 collective-permute-done.7.refs_7_
  41.8 5.7 %shard_map.68 = (bf16[1536,768]{1,0:T(8,128)(2,1)S(1)}, f32[16,4,24,128]{3,2,1,0:T(8,128)S(1)}, f32[16,4,24,128]{3,2,1,0:T(8,128)S(1)}, f32[16,4,24,128]{3,2,1,0:T(8,128)S(1)}, f32[16,4,24,128]{3,2,1,0:T(8,128)S(1)}) custom-call(s32[2]{0:T(128)S(1)} %pad_add_fusion.place_ref.refs_0_, s32[8,2,32]{2,1,0:T(2,128)S(1)} %copy-done.3, ...), custom_call_target="tpu_custom_call" | custom-call | flops 6600000000 | bytes 1000000 | tf_op jit(solution)/shard_map/pallas_call | solution.py:470
  47.4 1.1 %shard_map.70 = bf16[384,768]{1,0:T(8,128)(2,1)S(1)} custom-call(bf16[768,1536]{1,0:T(8,128)(2,1)S(1)} %get-tuple-element.38.refs_0_, bf16[1536,768]{1,0:T(8,128)(2,1)S(1)} %get-tuple-element.50.refs_1_), custom_call_target="tpu_custom_call" | custom-call | flops 11000000 | bytes 1000000 | tf_op jit(solution)/shard_map/pallas_call | solution.py:503
  48.5 0.4 collective-permute-start.9
  48.9 1.1 %shard_map.69 = f32[384,768]{1,0:T(8,128)S(1)} custom-call(bf16[768,1536]{1,0:T(8,128)(2,1)S(1)} %get-tuple-element.38.refs_0_, bf16[1536,768]{1,0:T(8,128)(2,1)S(1)} %get-tuple-element.50.refs_1_), custom_call_target="tpu_custom_call" | custom-call | flops 11000000 | bytes 1000000 | tf_op jit(solution)/shard_map/pallas_call | solution.py:503
  50.0 2.7 %collective-permute-done.8.refs_6_ = bf16[864,256]{1,0:T(8,128)(2,1)S(1)} collective-permute-done((bf16[864,256]{1,0:T(8,128)(2,1)}, bf16[864,256]{1,0:T(8,128)(2,1)S(1)}, u32[]{:S(2)}, u32[]{:S(2)}) %collective-permute-start.8) | collective-permute-done | bytes 442400 | tf_op jit(solution)/shard_map/ppermute | solution.py:406
  52.7 0.0 collective-permute-start.10
  52.7 0.5 collective-permute-start.12
  53.2 1.9 %collective-permute-done.10.refs_7_ = bf16[864,256]{1,0:T(8,128)(2,1)S(1)} collective-permute-done((bf16[864,256]{1,0:T(8,128)(2,1)S(1)}, bf16[864,256]{1,0:T(8,128)(2,1)S(1)}, u32[]{:S(2)}, u32[]{:S(2)}) %collective-permute-start.10) | collective-permute-done | bytes 442400 | tf_op jit(solution)/shard_map/ppermute | solution.py:406
  55.1 0.0 collective-permute-done.9
  55.1 0.1 convert_add_fusion.1
  55.3 1.5 %collective-permute-start.11 = (bf16[96,768]{1,0:T(8,128)(2,1)S(1)}, bf16[96,768]{1,0:T(8,128)(2,1)S(1)}, u32[]{:S(2)}, u32[]{:S(2)}) collective-permute-start(bf16[96,768]{1,0:T(8,128)(2,1)S(1)} %get-tuple-element.75), channel_id=1, source_target_pairs={{0,2},{1,3},{2,0},{3,1},{4,6},{5,7},{6,4},{7,5},{8,10},{9,11},{10,... | collective-permute-start | bytes 442376 | tf_op jit(solution)/shard_map/ppermute | solution.py:406
  56.7 0.0 collective-permute-done.12.refs_5_
  56.7 5.7 %shard_map.71.refs_1_ = bf16[1536,768]{1,0:T(8,128)(2,1)S(1)} custom-call(s32[2]{0:T(128)S(1)} %pad_add_fusion.place_ref.refs_0_, s32[8,2,32]{2,1,0:T(2,128)S(1)} %copy-done.3, s32[576]{0:T(1024)S(1)} %reshape.13.refs_1_.refs_2_, s32[576]{0:T(1024)S(1)} %reshape.15.refs_2_.refs_3_, bf16[864,256]{1,0:T(8,128)(2,1)} %collective-permute-done.3.refs_4_, ...), custom_call_target="tpu_custom_call" | custom-call | flops 6600000000 | bytes 1000000 | tf_op jit(solution)/shard_map/pallas_call | solution.py:487
  62.4 0.0 collective-permute-done.11
  62.4 1.1 %shard_map.73 = bf16[384,768]{1,0:T(8,128)(2,1)S(1)} custom-call(bf16[768,1536]{1,0:T(8,128)(2,1)S(1)} %get-tuple-element.38.refs_0_, bf16[1536,768]{1,0:T(8,128)(2,1)S(1)} %shard_map.71.refs_1_), custom_call_target="tpu_custom_call" | custom-call | flops 1650000000 | bytes 1000000 | tf_op jit(solution)/shard_map/pallas_call | solution.py:503
  63.5 0.1 collective-permute-start.13
  63.6 1.1 %shard_map.72 = f32[384,768]{1,0:T(8,128)S(1)} custom-call(bf16[768,1536]{1,0:T(8,128)(2,1)S(1)} %get-tuple-element.38.refs_0_, bf16[1536,768]{1,0:T(8,128)(2,1)S(1)} %shard_map.71.refs_1_), custom_call_target="tpu_custom_call" | custom-call | flops 1650000000 | bytes 1000000 | tf_op jit(solution)/shard_map/pallas_call | solution.py:503
  64.7 0.9 %collective-permute-done.13 = bf16[384,768]{1,0:T(8,128)(2,1)S(1)} collective-permute-done((bf16[384,768]{1,0:T(8,128)(2,1)S(1)}, bf16[384,768]{1,0:T(8,128)(2,1)S(1)}, u32[]{:S(2)}, u32[]{:S(2)}) %collective-permute-start.13) | collective-permute-done | bytes 589856 | tf_op jit(solution)/shard_map/ppermute | solution.py:406
  65.6 0.1 fusion.3
  65.8 3.0 %collective-permute-start.14 = (bf16[192,768]{1,0:T(8,128)(2,1)S(1)}, bf16[192,768]{1,0:T(8,128)(2,1)S(1)}, u32[]{:S(2)}, u32[]{:S(2)}) collective-permute-start(bf16[192,768]{1,0:T(8,128)(2,1)S(1)} %pad_maximum_fusion), channel_id=1, source_target_pairs={{0,4},{1,5},{2,6},{3,7},{4,8},{5,9},{6,10},{7,11},{8,12},{9,13},{1... | collective-permute-start | bytes 884744 | tf_op jit(solution)/shard_map/ppermute | solution.py:406
  68.8 0.6 collective-permute-start.16
  69.4 4.8 %collective-permute-start.15 = (bf16[96,768]{1,0:T(8,128)(2,1)S(1)}, bf16[96,768]{1,0:T(8,128)(2,1)S(1)}, u32[]{:S(2)}, u32[]{:S(2)}) collective-permute-start(bf16[96,768]{1,0:T(8,128)(2,1)S(1)} %get-tuple-element.72), channel_id=1, source_target_pairs={{0,6},{1,7},{2,4},{3,5},{4,10},{5,11},{6,8},{7,9},{8,14},{9,15},{1... | collective-permute-start | bytes 442376 | tf_op jit(solution)/shard_map/ppermute | solution.py:406
  74.2 6.7 %collective-permute-done.15 = bf16[96,768]{1,0:T(8,128)(2,1)S(1)} collective-permute-done((bf16[96,768]{1,0:T(8,128)(2,1)S(1)}, bf16[96,768]{1,0:T(8,128)(2,1)S(1)}, u32[]{:S(2)}, u32[]{:S(2)}) %collective-permute-start.15) | collective-permute-done | bytes 147488 | tf_op jit(solution)/shard_map/ppermute | solution.py:406
  80.8 0.0 collective-permute-done.14
  80.8 0.0 collective-permute-done.16
  80.9 0.1 slice_add_fusion.1
  81.0 0.8 fusion.1
  (14 shorter events, 0.2 us)
Async XLA Ops:
  0.0 9.4 %copy-start = (s32[512,3]{0,1:T(4,128)S(1)}, s32[512,3]{0,1:T(4,128)}, u32[]{:S(2)}) copy-start(s32[512,3]{0,1:T(4,128)} %param.9) | copy-start | bytes 18436
  0.0 1.3 %copy-start.2 = (bf16[64,24,288]{2,1,0:T(8,128)(2,1)S(1)}, bf16[64,24,288]{2,1,0:T(8,128)(2,1)}, u32[]{:S(2)}) copy-start(bf16[64,24,288]{2,1,0:T(8,128)(2,1)} %param.7) | copy-start | bytes 2654212
  1.3 1.9 %copy-start.3 = (s32[8,2,32]{2,1,0:T(2,128)S(1)}, s32[8,2,32]{2,1,0:T(2,128)}, u32[]{:S(2)}) copy-start(s32[8,2,32]{2,1,0:T(2,128)} %refs_1_.3) | copy-start | bytes 6148
  1.4 27.4 %collective-permute-start.5 = (bf16[1728,256]{1,0:T(8,128)(2,1)S(1)}, bf16[1728,256]{1,0:T(8,128)(2,1)}, u32[]{:S(2)}, u32[]{:S(2)}) collective-permute-start(bf16[1728,256]{1,0:T(8,128)(2,1)S(1)} %shard_map.64.p_ref.refs_3_), channel_id=1, source_target_pairs={{0,1},{1,0},{2,3},{3,2},{4,5},{5,4},{6,7},{7,6},{8,9},{9,8},{10,11... | collective-permute-start | bytes 2654216 | tf_op jit(solution)/shard_map/ppermute | solution.py:406
  1.5 22.2 %collective-permute-start = (bf16[1728,256]{1,0:T(8,128)(2,1)S(1)}, bf16[1728,256]{1,0:T(8,128)(2,1)}, u32[]{:S(2)}, u32[]{:S(2)}) collective-permute-start(bf16[1728,256]{1,0:T(8,128)(2,1)S(1)} %shard_map.64.p_ref.refs_3_), channel_id=1, source_target_pairs={{0,2},{1,3},{2,0},{3,1},{4,6},{5,7},{6,4},{7,5},{8,10},{9,11},{10,... | collective-permute-start | bytes 2654216 | tf_op jit(solution)/shard_map/ppermute | solution.py:406
  5.3 15.3 %collective-permute-start.1 = (bf16[864,256]{1,0:T(8,128)(2,1)}, bf16[864,256]{1,0:T(8,128)(2,1)}, u32[]{:S(2)}, u32[]{:S(2)}) collective-permute-start(bf16[864,256]{1,0:T(8,128)(2,1)} %get-tuple-element.36), channel_id=1, source_target_pairs={{0,4},{1,5},{2,6},{3,7},{4,8},{5,9},{6,10},{7,11},{8,12},{9,13},{1... | collective-permute-start | bytes 1327112 | tf_op jit(solution)/shard_map/ppermute | solution.py:406
  9.8 1.8 %copy-start.1 = (bf16[64,24,864]{2,1,0:T(8,128)(2,1)S(1)}, bf16[64,24,864]{2,1,0:T(8,128)(2,1)}, u32[]{:S(2)}) copy-start(bf16[64,24,864]{2,1,0:T(8,128)(2,1)} %param.6) | copy-start | bytes 7962628
  11.6 15.4 %copy-start.7 = (s32[64,9]{0,1:T(8,128)S(1)}, s32[64,9]{0,1:T(8,128)}, u32[]{:S(2)}) copy-start(s32[64,9]{0,1:T(8,128)} %param.8) | copy-start | bytes 6916
  18.5 1.7 %copy-start.4 = (bf16[9,1536,128]{2,1,0:T(8,128)(2,1)}, bf16[9,1536,128]{2,1,0:T(8,128)(2,1)S(1)}, u32[]{:S(2)}) copy-start(bf16[9,1536,128]{2,1,0:T(8,128)(2,1)S(1)} %get-tuple-element.42.refs_7_.refs_8_) | copy-start | bytes 10616836
  23.7 5.1 %collective-permute-start.6 = (bf16[1728,256]{1,0:T(8,128)(2,1)}, bf16[1728,256]{1,0:T(8,128)(2,1)}, u32[]{:S(2)}, u32[]{:S(2)}) collective-permute-start(bf16[1728,256]{1,0:T(8,128)(2,1)} %collective-permute-done.refs_5_), channel_id=1, source_target_pairs={{0,1},{1,0},{2,3},{3,2},{4,5},{5,4},{6,7},{7,6},{8,9},{9,8},{10,11... | collective-permute-start | bytes 2654216 | tf_op jit(solution)/shard_map/ppermute | solution.py:406
  23.7 16.1 %collective-permute-start.3 = (bf16[864,256]{1,0:T(8,128)(2,1)}, bf16[864,256]{1,0:T(8,128)(2,1)}, u32[]{:S(2)}, u32[]{:S(2)}) collective-permute-start(bf16[864,256]{1,0:T(8,128)(2,1)} %get-tuple-element.40), channel_id=1, source_target_pairs={{4,0},{5,1},{6,2},{7,3},{8,4},{9,5},{10,6},{11,7},{12,8},{13,9},{1... | collective-permute-start | bytes 1327112 | tf_op jit(solution)/shard_map/ppermute | solution.py:406
  27.2 12.6 %collective-permute-start.4 = (bf16[864,256]{1,0:T(8,128)(2,1)}, bf16[864,256]{1,0:T(8,128)(2,1)S(1)}, u32[]{:S(2)}, u32[]{:S(2)}) collective-permute-start(bf16[864,256]{1,0:T(8,128)(2,1)} %collective-permute-done.1.refs_4_), channel_id=1, source_target_pairs={{0,2},{1,3},{2,0},{3,1},{4,6},{5,7},{6,4},{7,5},{8,10},{9,11},{10,... | collective-permute-start | bytes 1327112 | tf_op jit(solution)/shard_map/ppermute | solution.py:406
  28.8 12.5 %collective-permute-start.2 = (bf16[864,256]{1,0:T(8,128)(2,1)}, bf16[864,256]{1,0:T(8,128)(2,1)S(1)}, u32[]{:S(2)}, u32[]{:S(2)}) collective-permute-start(bf16[864,256]{1,0:T(8,128)(2,1)} %collective-permute-done.1.refs_4_), channel_id=1, source_target_pairs={{0,1},{1,0},{2,3},{3,2},{4,5},{5,4},{6,7},{7,6},{8,9},{9,8},{10,11... | collective-permute-start | bytes 1327112 | tf_op jit(solution)/shard_map/ppermute | solution.py:406
  28.8 2.0 %copy-start.5 = (bf16[9,1536,128]{2,1,0:T(8,128)(2,1)S(1)}, bf16[9,1536,128]{2,1,0:T(8,128)(2,1)}, u32[]{:S(2)}) copy-start(bf16[9,1536,128]{2,1,0:T(8,128)(2,1)} %copy-done.4) | copy-start | bytes 10616836
  30.8 10.9 %copy-start.6 = (bf16[9,1536,128]{2,1,0:T(8,128)(2,1)S(1)}, bf16[9,1536,128]{2,1,0:T(8,128)(2,1)}, u32[]{:S(2)}) copy-start(bf16[9,1536,128]{2,1,0:T(8,128)(2,1)} %copy-done.4) | copy-start | bytes 10616836
  39.8 2.0 %collective-permute-start.7 = (bf16[864,256]{1,0:T(8,128)(2,1)S(1)}, bf16[864,256]{1,0:T(8,128)(2,1)S(1)}, u32[]{:S(2)}, u32[]{:S(2)}) collective-permute-start(bf16[864,256]{1,0:T(8,128)(2,1)S(1)} %collective-permute-done.4.refs_6_), channel_id=1, source_target_pairs={{0,1},{1,0},{2,3},{3,2},{4,5},{5,4},{6,7},{7,6},{8,9},{9,8},{10,11... | collective-permute-start | bytes 1327112 | tf_op jit(solution)/shard_map/ppermute | solution.py:406
  40.3 12.4 %collective-permute-start.8 = (bf16[864,256]{1,0:T(8,128)(2,1)}, bf16[864,256]{1,0:T(8,128)(2,1)S(1)}, u32[]{:S(2)}, u32[]{:S(2)}) collective-permute-start(bf16[864,256]{1,0:T(8,128)(2,1)} %collective-permute-done.3.refs_4_), channel_id=1, source_target_pairs={{0,2},{1,3},{2,0},{3,1},{4,6},{5,7},{6,4},{7,5},{8,10},{9,11},{10,... | collective-permute-start | bytes 1327112 | tf_op jit(solution)/shard_map/ppermute | solution.py:406
  48.5 6.6 %collective-permute-start.9 = (bf16[384,768]{1,0:T(8,128)(2,1)S(1)}, bf16[384,768]{1,0:T(8,128)(2,1)S(1)}, u32[]{:S(2)}, u32[]{:S(2)}) collective-permute-start(bf16[384,768]{1,0:T(8,128)(2,1)S(1)} %shard_map.70), channel_id=1, source_target_pairs={{0,1},{1,0},{2,3},{3,2},{4,5},{5,4},{6,7},{7,6},{8,9},{9,8},{10,11... | collective-permute-start | bytes 1769480 | tf_op jit(solution)/shard_map/ppermute | solution.py:406
  52.7 2.4 %collective-permute-start.10 = (bf16[864,256]{1,0:T(8,128)(2,1)S(1)}, bf16[864,256]{1,0:T(8,128)(2,1)S(1)}, u32[]{:S(2)}, u32[]{:S(2)}) collective-permute-start(bf16[864,256]{1,0:T(8,128)(2,1)S(1)} %collective-permute-done.8.refs_6_), channel_id=1, source_target_pairs={{0,1},{1,0},{2,3},{3,2},{4,5},{5,4},{6,7},{7,6},{8,9},{9,8},{10,11... | collective-permute-start | bytes 1327112 | tf_op jit(solution)/shard_map/ppermute | solution.py:406
  52.7 4.0 %collective-permute-start.12 = (bf16[864,256]{1,0:T(8,128)(2,1)}, bf16[864,256]{1,0:T(8,128)(2,1)S(1)}, u32[]{:S(2)}, u32[]{:S(2)}) collective-permute-start(bf16[864,256]{1,0:T(8,128)(2,1)} %collective-permute-done.3.refs_4_), channel_id=1, source_target_pairs={{0,1},{1,0},{2,3},{3,2},{4,5},{5,4},{6,7},{7,6},{8,9},{9,8},{10,11... | collective-permute-start | bytes 1327112 | tf_op jit(solution)/shard_map/ppermute | solution.py:406
  55.3 7.2 %collective-permute-start.11 = (bf16[96,768]{1,0:T(8,128)(2,1)S(1)}, bf16[96,768]{1,0:T(8,128)(2,1)S(1)}, u32[]{:S(2)}, u32[]{:S(2)}) collective-permute-start(bf16[96,768]{1,0:T(8,128)(2,1)S(1)} %get-tuple-element.75), channel_id=1, source_target_pairs={{0,2},{1,3},{2,0},{3,1},{4,6},{5,7},{6,4},{7,5},{8,10},{9,11},{10,... | collective-permute-start | bytes 442376 | tf_op jit(solution)/shard_map/ppermute | solution.py:406
  63.5 2.1 %collective-permute-start.13 = (bf16[384,768]{1,0:T(8,128)(2,1)S(1)}, bf16[384,768]{1,0:T(8,128)(2,1)S(1)}, u32[]{:S(2)}, u32[]{:S(2)}) collective-permute-start(bf16[384,768]{1,0:T(8,128)(2,1)S(1)} %shard_map.73), channel_id=1, source_target_pairs={{0,1},{1,0},{2,3},{3,2},{4,5},{5,4},{6,7},{7,6},{8,9},{9,8},{10,11... | collective-permute-start | bytes 1769480 | tf_op jit(solution)/shard_map/ppermute | solution.py:406
  65.8 15.1 %collective-permute-start.14 = (bf16[192,768]{1,0:T(8,128)(2,1)S(1)}, bf16[192,768]{1,0:T(8,128)(2,1)S(1)}, u32[]{:S(2)}, u32[]{:S(2)}) collective-permute-start(bf16[192,768]{1,0:T(8,128)(2,1)S(1)} %pad_maximum_fusion), channel_id=1, source_target_pairs={{0,4},{1,5},{2,6},{3,7},{4,8},{5,9},{6,10},{7,11},{8,12},{9,13},{1... | collective-permute-start | bytes 884744 | tf_op jit(solution)/shard_map/ppermute | solution.py:406
  68.8 12.0 %collective-permute-start.16 = (bf16[192,768]{1,0:T(8,128)(2,1)S(1)}, bf16[192,768]{1,0:T(8,128)(2,1)S(1)}, u32[]{:S(2)}, u32[]{:S(2)}) collective-permute-start(bf16[192,768]{1,0:T(8,128)(2,1)S(1)} %pad_maximum_fusion.1), channel_id=1, source_target_pairs={{0,2},{1,3},{2,0},{3,1},{4,6},{5,7},{6,4},{7,5},{8,10},{9,11},{10,... | collective-permute-start | bytes 884744 | tf_op jit(solution)/shard_map/ppermute | solution.py:406
  69.4 11.4 %collective-permute-start.15 = (bf16[96,768]{1,0:T(8,128)(2,1)S(1)}, bf16[96,768]{1,0:T(8,128)(2,1)S(1)}, u32[]{:S(2)}, u32[]{:S(2)}) collective-permute-start(bf16[96,768]{1,0:T(8,128)(2,1)S(1)} %get-tuple-element.72), channel_id=1, source_target_pairs={{0,6},{1,7},{2,4},{3,5},{4,10},{5,11},{6,8},{7,9},{8,14},{9,15},{1... | collective-permute-start | bytes 442376 | tf_op jit(solution)/shard_map/ppermute | solution.py:406

commit v6 on v5

--- a/solution.py
+++ b/solution.py
@@ -306,7 +306,7 @@
             add_products(n, (7, 8), a_ref, 5, prolong, own_row, swapped, sums)
             return carry
 
-        lax.fori_loop(0, STEPS, step, 0, unroll=2)
+        lax.fori_loop(0, STEPS, step, 0, unroll=4)
         unpack(NS, sources, prolong)
 
         def step(n, carry):
@@ -314,7 +314,7 @@
             finish(n)
             return carry
 
-        lax.fori_loop(0, STEPS, step, 0, unroll=2)
+        lax.fori_loop(0, STEPS, step, 0, unroll=4)
 
     @pl.when(part == 0)
     def _():
@@ -330,7 +330,7 @@
                 above[u][n] = own[u][n, NAG : 2 * NAG] + sums[u][n, 0:NAG]
             return carry
 
-        lax.fori_loop(0, STEPS, step, 0, unroll=2)
+        lax.fori_loop(0, STEPS, step, 0, unroll=4)
 
     @pl.when(jnp.logical_and(part > 0, part < parts - 1))
     def _():
@@ -343,7 +343,7 @@
             finish(n)
             return carry
 
-        lax.fori_loop(0, STEPS, step, 0, unroll=2)
+        lax.fori_loop(0, STEPS, step, 0, unroll=4)
 
 
 def upper_kernel(place_ref, halo_ref, aggs_ref, cols_ref, *refs, parts):
@@ -370,7 +370,7 @@
             couple(n, lambda u, c: sums[u][n, c] + above[u][n, c] if c < NAG else sums[u][n, c], coupled)
             return carry
 
-        lax.fori_loop(0, STEPS, step, 0, unroll=2 if products else 1)
+        lax.fori_loop(0, STEPS, step, 0, unroll=4 if products else 1)
 
     @pl.when(inside)
     def _():
@@ -428,7 +428,6 @@
         cost_estimate=cost(3),
     )(place, halo_rows, own_pack)
     low = moved(upward, 1, 0)
-    up = moved(down, -1, 0)
 
     def both_cores(x, far):
         return (x, moved(x, 0, 1), far, moved(far, 0, 1))
@@ -447,7 +446,9 @@
         compiler_params=params(),
         cost_estimate=cost(9),
     )(place, aggs, live_rows, own_pack, a_flat)
-    near, low, spread = lax.optimization_barrier((near, low, spread))
+    down, low, spread = lax.optimization_barrier((down, low, spread))
+    up = moved(down, -1, 0)
+    near, spread = lax.optimization_barrier((near, spread))
     low_far = moved(low, 0, 2)
 
     sums_type = jax.ShapeDtypeStruct((STEPS, 8, W, 128), F32)

time: 82.6 us -> 81.7 us (0.989)
  waiting for transfers between devices: 16 us -> 18.6 us
  starting transfers between devices: 22.3 us -> 20.4 us
  Pallas kernels: 33.7 us -> 31.9 us
    ppermute x17, waiting for transfers between devices: 16 us -> 18.6 us  [moved(): return lax.ppermute(x, AXES, route)]
    ppermute x17, starting transfers between devices: 22.3 us -> 20.4 us  [moved(): return lax.ppermute(x, AXES, route)]
    pallas_call x1, Pallas kernels: 5.67 us -> 4.49 us  [upper_coupled(): pl.pallas_call(lambda *refs: upper_kernel(*refs, parts=parts), out_shape=...]
    unnamed x17 -> x19, local copies, waits for them, and re-layouts: 6.9 us -> 7.65 us
  transfers between devices with their start and end apart: 17 -> 17, of which waited for: 7 -> 10; matrix products, arithmetic and copies ran while one was open for 1% -> 1% of each run, Pallas kernels for 40% -> 38%
where the time goes in v6:
time: 81.7 us; the launch traced here: 81.3 us
  Pallas kernels  31.9 us (39%)
  starting transfers between devices  20.4 us (25%)
  waiting for transfers between devices  18.6 us (23%)
  local copies, waits for them, and re-layouts  8.27 us (10%)
  other arithmetic  1.33 us (2%)
  between operations  0.92 us (1%)
    ppermute x17, starting transfers between devices, moved(): return lax.ppermute(x, AXES, route)  20.4 us
    ppermute x17, waiting for transfers between devices, moved(): return lax.ppermute(x, AXES, route)  18.6 us
    pallas_call x1, Pallas kernels, local(): pl.pallas_call(lambda *refs: own_kernel(*refs, parts=parts), out_shape=[p...  8.91 us
    unnamed x19, local copies, waits for them, and re-layouts  7.65 us
    pallas_call x1, Pallas kernels, local(): pl.pallas_call(lambda *refs: prepare_kernel(*refs, parts=parts), out_shap...  6.86 us
    pallas_call x1, Pallas kernels, local(): pl.pallas_call(lambda *refs: lower_kernel(*refs, parts=parts), out_shape=...  5.17 us
    pallas_call x1, Pallas kernels, upper_coupled(): pl.pallas_call(lambda *refs: upper_kernel(*refs, parts=parts), out_shape=...  4.49 us
    pallas_call x4, Pallas kernels, coarse_of(): pl.pallas_call(lambda *refs: coarse_kernel(*refs, half=half), out_shape=j...  4.3 us
  transfers between devices with their start and end apart: 17, of which 10 were waited for; matrix products, arithmetic and copies ran while one was open for 1% of the time, Pallas kernels for 38%

profile of v6, /device:TPU:16, one launch (start us, length us, event | category | flops | bytes accessed | tf_op | source)
XLA Modules:
  0.0 81.3 jit_solution(12913449649055541196)
XLA Ops:
  0.0 0.0 copy-start
  0.0 1.3 %copy-done.2 = bf16[64,24,288]{2,1,0:T(8,128)(2,1)S(1)} copy-done((bf16[64,24,288]{2,1,0:T(8,128)(2,1)S(1)}, bf16[64,24,288]{2,1,0:T(8,128)(2,1)}, u32[]{:S(2)}) %copy-start.2) | copy-done | bytes 884760
  1.3 0.1 shard_map.64.p_ref.refs_3_
  1.4 0.1 collective-permute-start.5
  1.5 1.6 %collective-permute-start = (bf16[1728,256]{1,0:T(8,128)(2,1)S(1)}, bf16[1728,256]{1,0:T(8,128)(2,1)}, u32[]{:S(2)}, u32[]{:S(2)}) collective-permute-start(bf16[1728,256]{1,0:T(8,128)(2,1)S(1)} %shard_map.64.p_ref.refs_3_), channel_id=1, source_target_pairs={{0,2},{1,3},{2,0},{3,1},{4,6},{5,7},{6,4},{7,5},{8,10},{9,11},{10,... | collective-permute-start | bytes 2654216 | tf_op jit(solution)/shard_map/ppermute | solution.py:406
  3.1 0.1 pad_add_fusion.place_ref.refs_0_
  3.2 0.0 copy-done.4
  3.2 2.0 %shard_map.65 = (bf16[864,256]{1,0:T(8,128)(2,1)S(1)}, bf16[864,256]{1,0:T(8,128)(2,1)}) custom-call(s32[2]{0:T(128)S(1)} %pad_add_fusion.place_ref.refs_0_, s32[8,2,32]{2,1,0:T(2,128)S(1)} %copy-done.4, bf16[1728,256]{1,0:T(8,128)(2,1)S(1)} %shard_map.64.p_ref.refs_3_), custom_call_target="tpu_custom_call" | custom-call | flops 3300000000 | bytes 1000000 | tf_op jit(solution)/shard_map/pallas_call | solution.py:421
  5.2 0.8 copy-done.3
  5.9 3.4 %collective-permute-start.1 = (bf16[864,256]{1,0:T(8,128)(2,1)}, bf16[864,256]{1,0:T(8,128)(2,1)}, u32[]{:S(2)}, u32[]{:S(2)}) collective-permute-start(bf16[864,256]{1,0:T(8,128)(2,1)} %get-tuple-element.39), channel_id=1, source_target_pairs={{0,4},{1,5},{2,6},{3,7},{4,8},{5,9},{6,10},{7,11},{8,12},{9,13},{1... | collective-permute-start | bytes 1327112 | tf_op jit(solution)/shard_map/ppermute | solution.py:406
  10.0 0.1 constant_dynamic-slice_fusion
  10.1 0.1 copy.7
  10.2 0.2 reshape.13.refs_1_.refs_2_
  10.4 0.0 copy-start.1
  10.4 1.8 %copy-done.1 = bf16[64,24,864]{2,1,0:T(8,128)(2,1)S(1)} copy-done((bf16[64,24,864]{2,1,0:T(8,128)(2,1)S(1)}, bf16[64,24,864]{2,1,0:T(8,128)(2,1)}, u32[]{:S(2)}) %copy-start.1) | copy-done | bytes 2654232
  12.2 6.9 %shard_map.66 = (bf16[768,1536]{1,0:T(8,128)(2,1)S(1)}, bf16[9,1536,128]{2,1,0:T(8,128)(2,1)S(1)}) custom-call(s32[2]{0:T(128)S(1)} %pad_add_fusion.place_ref.refs_0_, s32[576]{0:T(1024)S(1)} %reshape.13.refs_1_.refs_2_, s32[1]{0:T(128)S(6)} %copy.9.refs_2_, bf16[1728,256]{1,0:T(8,128)(2,1)S(1)} %shard_map.64.p_ref.refs_3_, bf16[1536,864]{1,0:T(8,128)(2,1)S(1)} %bitcast.4), custom_call_target="tpu_custom_call" | custom-call | flops 9900000256 | bytes 1000000 | tf_op jit(solution)/shard_map/pallas_call | solution.py:437
  19.1 1.7 %copy-done.5 = bf16[9,1536,128]{2,1,0:T(8,128)(2,1)} copy-done((bf16[9,1536,128]{2,1,0:T(8,128)(2,1)}, bf16[9,1536,128]{2,1,0:T(8,128)(2,1)S(1)}, u32[]{:S(2)}) %copy-start.5) | copy-done | bytes 3538968
  20.8 0.5 collective-permute-done.1.refs_4_
  21.3 2.4 %collective-permute-done.refs_5_ = bf16[1728,256]{1,0:T(8,128)(2,1)} collective-permute-done((bf16[1728,256]{1,0:T(8,128)(2,1)S(1)}, bf16[1728,256]{1,0:T(8,128)(2,1)}, u32[]{:S(2)}, u32[]{:S(2)}) %collective-permute-start) | collective-permute-done | bytes 884768 | tf_op jit(solution)/shard_map/ppermute | solution.py:406
  23.7 0.0 collective-permute-start.6
  23.7 0.0 copy-done.8
  23.7 0.1 copy.8
  23.8 0.1 reshape.15.refs_2_.refs_3_
  23.9 1.6 %collective-permute-start.4 = (bf16[864,256]{1,0:T(8,128)(2,1)}, bf16[864,256]{1,0:T(8,128)(2,1)S(1)}, u32[]{:S(2)}, u32[]{:S(2)}) collective-permute-start(bf16[864,256]{1,0:T(8,128)(2,1)} %collective-permute-done.1.refs_4_), channel_id=1, source_target_pairs={{0,2},{1,3},{2,0},{3,1},{4,6},{5,7},{6,4},{7,5},{8,10},{9,11},{10,... | collective-permute-start | bytes 1327112 | tf_op jit(solution)/shard_map/ppermute | solution.py:406
  25.5 0.2 collective-permute-start.2
  25.7 3.3 %collective-permute-start.3 = (bf16[864,256]{1,0:T(8,128)(2,1)}, bf16[864,256]{1,0:T(8,128)(2,1)S(1)}, u32[]{:S(2)}, u32[]{:S(2)}) collective-permute-start(bf16[864,256]{1,0:T(8,128)(2,1)} %copy-done.3), channel_id=1, source_target_pairs={{4,0},{5,1},{6,2},{7,3},{8,4},{9,5},{10,6},{11,7},{12,8},{13,9},{1... | collective-permute-start | bytes 1327112 | tf_op jit(solution)/shard_map/ppermute | solution.py:406
  29.0 0.0 collective-permute-done.5.refs_4_
  29.0 0.0 collective-permute-done.6.refs_6_
  29.0 2.0 %copy-done.6 = bf16[9,1536,128]{2,1,0:T(8,128)(2,1)S(1)} copy-done((bf16[9,1536,128]{2,1,0:T(8,128)(2,1)S(1)}, bf16[9,1536,128]{2,1,0:T(8,128)(2,1)}, u32[]{:S(2)}) %copy-start.6) | copy-done | bytes 3538968
  31.0 8.9 %shard_map.67 = (bf16[64,96,384]{2,1,0:T(8,128)(2,1)S(1)}, f32[16,8,24,128]{3,2,1,0:T(8,128)S(1)}, f32[16,8,24,128]{3,2,1,0:T(8,128)S(1)}, f32[16,8,24,128]{3,2,1,0:T(8,128)S(1)}, f32[16,8,24,128]{3,2,1,0:T(8,128)S(1)}) custom-call(s32[2]{0:T(128)S(1)} %pad_add_fusion.place_ref.refs_0_, s32[576]{0:T(1024)S(1)} %reshape.13.refs_1_.refs_2_, ...), custom_call_target="tpu_custom_call" | custom-call | flops 11000000512 | bytes 1000000 | tf_op jit(solution)/shard_map/pallas_call | solution.py:456
  40.0 0.2 collective-permute-done.3.refs_4_
  40.2 0.0 collective-permute-done.4.refs_6_
  40.2 0.0 collective-permute-start.7
  40.2 0.5 collective-permute-start.8
  40.7 0.0 collective-permute-done.2.refs_5_
  40.7 1.3 %collective-permute-done.7.refs_7_ = bf16[864,256]{1,0:T(8,128)(2,1)S(1)} collective-permute-done((bf16[864,256]{1,0:T(8,128)(2,1)S(1)}, bf16[864,256]{1,0:T(8,128)(2,1)S(1)}, u32[]{:S(2)}, u32[]{:S(2)}) %collective-permute-start.7) | collective-permute-done | bytes 442400 | tf_op jit(solution)/shard_map/ppermute | solution.py:406
  42.0 0.0 copy-done.7
  42.0 5.2 %shard_map.68 = (bf16[1536,768]{1,0:T(8,128)(2,1)S(1)}, f32[16,4,24,128]{3,2,1,0:T(8,128)S(1)}, f32[16,4,24,128]{3,2,1,0:T(8,128)S(1)}, f32[16,4,24,128]{3,2,1,0:T(8,128)S(1)}, f32[16,4,24,128]{3,2,1,0:T(8,128)S(1)}) custom-call(s32[2]{0:T(128)S(1)} %pad_add_fusion.place_ref.refs_0_, s32[8,2,32]{2,1,0:T(2,128)S(1)} %copy-done.4, ...), custom_call_target="tpu_custom_call" | custom-call | flops 6600000000 | bytes 1000000 | tf_op jit(solution)/shard_map/pallas_call | solution.py:471
  47.2 1.1 %shard_map.70 = bf16[384,768]{1,0:T(8,128)(2,1)S(1)} custom-call(bf16[768,1536]{1,0:T(8,128)(2,1)S(1)} %get-tuple-element.42.refs_0_, bf16[1536,768]{1,0:T(8,128)(2,1)S(1)} %get-tuple-element.54.refs_1_), custom_call_target="tpu_custom_call" | custom-call | flops 11000000 | bytes 1000000 | tf_op jit(solution)/shard_map/pallas_call | solution.py:504
  48.2 0.2 collective-permute-start.9
  48.4 1.1 %shard_map.69 = f32[384,768]{1,0:T(8,128)S(1)} custom-call(bf16[768,1536]{1,0:T(8,128)(2,1)S(1)} %get-tuple-element.42.refs_0_, bf16[1536,768]{1,0:T(8,128)(2,1)S(1)} %get-tuple-element.54.refs_1_), custom_call_target="tpu_custom_call" | custom-call | flops 11000000 | bytes 1000000 | tf_op jit(solution)/shard_map/pallas_call | solution.py:504
  49.5 3.2 %collective-permute-done.8.refs_6_ = bf16[864,256]{1,0:T(8,128)(2,1)S(1)} collective-permute-done((bf16[864,256]{1,0:T(8,128)(2,1)S(1)}, bf16[864,256]{1,0:T(8,128)(2,1)S(1)}, u32[]{:S(2)}, u32[]{:S(2)}) %collective-permute-start.8) | collective-permute-done | bytes 442400 | tf_op jit(solution)/shard_map/ppermute | solution.py:406
  52.8 0.0 collective-permute-start.10
  52.8 0.5 collective-permute-start.12
  53.3 1.3 %collective-permute-done.10.refs_7_ = bf16[864,256]{1,0:T(8,128)(2,1)S(1)} collective-permute-done((bf16[864,256]{1,0:T(8,128)(2,1)S(1)}, bf16[864,256]{1,0:T(8,128)(2,1)S(1)}, u32[]{:S(2)}, u32[]{:S(2)}) %collective-permute-start.10) | collective-permute-done | bytes 442400 | tf_op jit(solution)/shard_map/ppermute | solution.py:406
  54.6 0.0 collective-permute-done.9
  54.6 0.1 convert_add_fusion.1
  54.7 0.6 collective-permute-start.11
  55.3 0.0 collective-permute-done.12.refs_5_
  55.3 4.5 %shard_map.71.refs_1_ = bf16[1536,768]{1,0:T(8,128)(2,1)S(1)} custom-call(s32[2]{0:T(128)S(1)} %pad_add_fusion.place_ref.refs_0_, s32[8,2,32]{2,1,0:T(2,128)S(1)} %copy-done.4, s32[576]{0:T(1024)S(1)} %reshape.13.refs_1_.refs_2_, s32[576]{0:T(1024)S(1)} %reshape.15.refs_2_.refs_3_, bf16[864,256]{1,0:T(8,128)(2,1)S(1)} %collective-permute-done.3.refs_4_, ...), custom_call_target="tpu_custom_call" | custom-call | flops 6600000000 | bytes 1000000 | tf_op jit(solution)/shard_map/pallas_call | solution.py:488
  59.8 0.9 %collective-permute-done.11 = bf16[96,768]{1,0:T(8,128)(2,1)S(1)} collective-permute-done((bf16[96,768]{1,0:T(8,128)(2,1)S(1)}, bf16[96,768]{1,0:T(8,128)(2,1)S(1)}, u32[]{:S(2)}, u32[]{:S(2)}) %collective-permute-start.11) | collective-permute-done | bytes 147488 | tf_op jit(solution)/shard_map/ppermute | solution.py:406
  60.7 1.1 %shard_map.73 = bf16[384,768]{1,0:T(8,128)(2,1)S(1)} custom-call(bf16[768,1536]{1,0:T(8,128)(2,1)S(1)} %get-tuple-element.42.refs_0_, bf16[1536,768]{1,0:T(8,128)(2,1)S(1)} %shard_map.71.refs_1_), custom_call_target="tpu_custom_call" | custom-call | flops 1650000000 | bytes 1000000 | tf_op jit(solution)/shard_map/pallas_call | solution.py:504
  61.8 0.1 collective-permute-start.13
  61.9 1.1 %shard_map.72 = f32[384,768]{1,0:T(8,128)S(1)} custom-call(bf16[768,1536]{1,0:T(8,128)(2,1)S(1)} %get-tuple-element.42.refs_0_, bf16[1536,768]{1,0:T(8,128)(2,1)S(1)} %shard_map.71.refs_1_), custom_call_target="tpu_custom_call" | custom-call | flops 1650000000 | bytes 1000000 | tf_op jit(solution)/shard_map/pallas_call | solution.py:504
  63.0 0.9 %collective-permute-done.13 = bf16[384,768]{1,0:T(8,128)(2,1)S(1)} collective-permute-done((bf16[384,768]{1,0:T(8,128)(2,1)S(1)}, bf16[384,768]{1,0:T(8,128)(2,1)S(1)}, u32[]{:S(2)}, u32[]{:S(2)}) %collective-permute-start.13) | collective-permute-done | bytes 589856 | tf_op jit(solution)/shard_map/ppermute | solution.py:406
  63.9 0.1 fusion.3
  64.0 4.3 %collective-permute-start.14 = (bf16[192,768]{1,0:T(8,128)(2,1)S(1)}, bf16[192,768]{1,0:T(8,128)(2,1)S(1)}, u32[]{:S(2)}, u32[]{:S(2)}) collective-permute-start(bf16[192,768]{1,0:T(8,128)(2,1)S(1)} %pad_maximum_fusion), channel_id=1, source_target_pairs={{0,4},{1,5},{2,6},{3,7},{4,8},{5,9},{6,10},{7,11},{8,12},{9,13},{1... | collective-permute-start | bytes 884744 | tf_op jit(solution)/shard_map/ppermute | solution.py:406
  68.4 0.7 collective-permute-start.16
  69.1 3.3 %collective-permute-start.15 = (bf16[96,768]{1,0:T(8,128)(2,1)S(1)}, bf16[96,768]{1,0:T(8,128)(2,1)S(1)}, u32[]{:S(2)}, u32[]{:S(2)}) collective-permute-start(bf16[96,768]{1,0:T(8,128)(2,1)S(1)} %get-tuple-element.76), channel_id=1, source_target_pairs={{0,6},{1,7},{2,4},{3,5},{4,10},{5,11},{6,8},{7,9},{8,14},{9,15},{1... | collective-permute-start | bytes 442376 | tf_op jit(solution)/shard_map/ppermute | solution.py:406
  72.5 6.8 %collective-permute-done.15 = bf16[96,768]{1,0:T(8,128)(2,1)S(1)} collective-permute-done((bf16[96,768]{1,0:T(8,128)(2,1)S(1)}, bf16[96,768]{1,0:T(8,128)(2,1)S(1)}, u32[]{:S(2)}, u32[]{:S(2)}) %collective-permute-start.15) | collective-permute-done | bytes 147488 | tf_op jit(solution)/shard_map/ppermute | solution.py:406
  79.2 0.0 collective-permute-done.14
  79.2 1.1 %collective-permute-done.16 = bf16[192,768]{1,0:T(8,128)(2,1)S(1)} collective-permute-done((bf16[192,768]{1,0:T(8,128)(2,1)S(1)}, bf16[192,768]{1,0:T(8,128)(2,1)S(1)}, u32[]{:S(2)}, u32[]{:S(2)}) %collective-permute-start.16) | collective-permute-done | bytes 294944 | tf_op jit(solution)/shard_map/ppermute | solution.py:406
  80.5 0.1 slice_add_fusion.1
  80.5 0.8 fusion.1
  (16 shorter events, 0.2 us)
Async XLA Ops:
  0.0 10.0 %copy-start = (s32[512,3]{0,1:T(4,128)S(1)}, s32[512,3]{0,1:T(4,128)}, u32[]{:S(2)}) copy-start(s32[512,3]{0,1:T(4,128)} %param.9) | copy-start | bytes 18436
  0.0 1.3 %copy-start.2 = (bf16[64,24,288]{2,1,0:T(8,128)(2,1)S(1)}, bf16[64,24,288]{2,1,0:T(8,128)(2,1)}, u32[]{:S(2)}) copy-start(bf16[64,24,288]{2,1,0:T(8,128)(2,1)} %param.7) | copy-start | bytes 2654212
  1.3 1.9 %copy-start.4 = (s32[8,2,32]{2,1,0:T(2,128)S(1)}, s32[8,2,32]{2,1,0:T(2,128)}, u32[]{:S(2)}) copy-start(s32[8,2,32]{2,1,0:T(2,128)} %refs_1_.3) | copy-start | bytes 6148
  1.4 27.6 %collective-permute-start.5 = (bf16[1728,256]{1,0:T(8,128)(2,1)S(1)}, bf16[1728,256]{1,0:T(8,128)(2,1)}, u32[]{:S(2)}, u32[]{:S(2)}) collective-permute-start(bf16[1728,256]{1,0:T(8,128)(2,1)S(1)} %shard_map.64.p_ref.refs_3_), channel_id=1, source_target_pairs={{0,1},{1,0},{2,3},{3,2},{4,5},{5,4},{6,7},{7,6},{8,9},{9,8},{10,11... | collective-permute-start | bytes 2654216 | tf_op jit(solution)/shard_map/ppermute | solution.py:406
  1.5 22.2 %collective-permute-start = (bf16[1728,256]{1,0:T(8,128)(2,1)S(1)}, bf16[1728,256]{1,0:T(8,128)(2,1)}, u32[]{:S(2)}, u32[]{:S(2)}) collective-permute-start(bf16[1728,256]{1,0:T(8,128)(2,1)S(1)} %shard_map.64.p_ref.refs_3_), channel_id=1, source_target_pairs={{0,2},{1,3},{2,0},{3,1},{4,6},{5,7},{6,4},{7,5},{8,10},{9,11},{10,... | collective-permute-start | bytes 2654216 | tf_op jit(solution)/shard_map/ppermute | solution.py:406
  5.2 0.8 copy-start.3
  5.9 15.3 %collective-permute-start.1 = (bf16[864,256]{1,0:T(8,128)(2,1)}, bf16[864,256]{1,0:T(8,128)(2,1)}, u32[]{:S(2)}, u32[]{:S(2)}) collective-permute-start(bf16[864,256]{1,0:T(8,128)(2,1)} %get-tuple-element.39), channel_id=1, source_target_pairs={{0,4},{1,5},{2,6},{3,7},{4,8},{5,9},{6,10},{7,11},{8,12},{9,13},{1... | collective-permute-start | bytes 1327112 | tf_op jit(solution)/shard_map/ppermute | solution.py:406
  10.4 1.8 %copy-start.1 = (bf16[64,24,864]{2,1,0:T(8,128)(2,1)S(1)}, bf16[64,24,864]{2,1,0:T(8,128)(2,1)}, u32[]{:S(2)}) copy-start(bf16[64,24,864]{2,1,0:T(8,128)(2,1)} %param.6) | copy-start | bytes 7962628
  12.2 11.5 %copy-start.8 = (s32[64,9]{0,1:T(8,128)S(1)}, s32[64,9]{0,1:T(8,128)}, u32[]{:S(2)}) copy-start(s32[64,9]{0,1:T(8,128)} %param.8) | copy-start | bytes 6916
  19.0 1.7 %copy-start.5 = (bf16[9,1536,128]{2,1,0:T(8,128)(2,1)}, bf16[9,1536,128]{2,1,0:T(8,128)(2,1)S(1)}, u32[]{:S(2)}) copy-start(bf16[9,1536,128]{2,1,0:T(8,128)(2,1)S(1)} %get-tuple-element.46.refs_7_.refs_8_) | copy-start | bytes 10616836
  23.7 5.3 %collective-permute-start.6 = (bf16[1728,256]{1,0:T(8,128)(2,1)}, bf16[1728,256]{1,0:T(8,128)(2,1)}, u32[]{:S(2)}, u32[]{:S(2)}) collective-permute-start(bf16[1728,256]{1,0:T(8,128)(2,1)} %collective-permute-done.refs_5_), channel_id=1, source_target_pairs={{0,1},{1,0},{2,3},{3,2},{4,5},{5,4},{6,7},{7,6},{8,9},{9,8},{10,11... | collective-permute-start | bytes 2654216 | tf_op jit(solution)/shard_map/ppermute | solution.py:406
  23.9 16.3 %collective-permute-start.4 = (bf16[864,256]{1,0:T(8,128)(2,1)}, bf16[864,256]{1,0:T(8,128)(2,1)S(1)}, u32[]{:S(2)}, u32[]{:S(2)}) collective-permute-start(bf16[864,256]{1,0:T(8,128)(2,1)} %collective-permute-done.1.refs_4_), channel_id=1, source_target_pairs={{0,2},{1,3},{2,0},{3,1},{4,6},{5,7},{6,4},{7,5},{8,10},{9,11},{10,... | collective-permute-start | bytes 1327112 | tf_op jit(solution)/shard_map/ppermute | solution.py:406
  25.5 15.2 %collective-permute-start.2 = (bf16[864,256]{1,0:T(8,128)(2,1)}, bf16[864,256]{1,0:T(8,128)(2,1)S(1)}, u32[]{:S(2)}, u32[]{:S(2)}) collective-permute-start(bf16[864,256]{1,0:T(8,128)(2,1)} %collective-permute-done.1.refs_4_), channel_id=1, source_target_pairs={{0,1},{1,0},{2,3},{3,2},{4,5},{5,4},{6,7},{7,6},{8,9},{9,8},{10,11... | collective-permute-start | bytes 1327112 | tf_op jit(solution)/shard_map/ppermute | solution.py:406
  25.7 14.4 %collective-permute-start.3 = (bf16[864,256]{1,0:T(8,128)(2,1)}, bf16[864,256]{1,0:T(8,128)(2,1)S(1)}, u32[]{:S(2)}, u32[]{:S(2)}) collective-permute-start(bf16[864,256]{1,0:T(8,128)(2,1)} %copy-done.3), channel_id=1, source_target_pairs={{4,0},{5,1},{6,2},{7,3},{8,4},{9,5},{10,6},{11,7},{12,8},{13,9},{1... | collective-permute-start | bytes 1327112 | tf_op jit(solution)/shard_map/ppermute | solution.py:406
  29.0 2.0 %copy-start.6 = (bf16[9,1536,128]{2,1,0:T(8,128)(2,1)S(1)}, bf16[9,1536,128]{2,1,0:T(8,128)(2,1)}, u32[]{:S(2)}) copy-start(bf16[9,1536,128]{2,1,0:T(8,128)(2,1)} %copy-done.5) | copy-start | bytes 10616836
  31.0 10.9 %copy-start.7 = (bf16[9,1536,128]{2,1,0:T(8,128)(2,1)S(1)}, bf16[9,1536,128]{2,1,0:T(8,128)(2,1)}, u32[]{:S(2)}) copy-start(bf16[9,1536,128]{2,1,0:T(8,128)(2,1)} %copy-done.5) | copy-start | bytes 10616836
  40.2 1.8 %collective-permute-start.7 = (bf16[864,256]{1,0:T(8,128)(2,1)S(1)}, bf16[864,256]{1,0:T(8,128)(2,1)S(1)}, u32[]{:S(2)}, u32[]{:S(2)}) collective-permute-start(bf16[864,256]{1,0:T(8,128)(2,1)S(1)} %collective-permute-done.4.refs_6_), channel_id=1, source_target_pairs={{0,1},{1,0},{2,3},{3,2},{4,5},{5,4},{6,7},{7,6},{8,9},{9,8},{10,11... | collective-permute-start | bytes 1327112 | tf_op jit(solution)/shard_map/ppermute | solution.py:406
  40.2 12.6 %collective-permute-start.8 = (bf16[864,256]{1,0:T(8,128)(2,1)S(1)}, bf16[864,256]{1,0:T(8,128)(2,1)S(1)}, u32[]{:S(2)}, u32[]{:S(2)}) collective-permute-start(bf16[864,256]{1,0:T(8,128)(2,1)S(1)} %collective-permute-done.3.refs_4_), channel_id=1, source_target_pairs={{0,2},{1,3},{2,0},{3,1},{4,6},{5,7},{6,4},{7,5},{8,10},{9,11},{10,... | collective-permute-start | bytes 1327112 | tf_op jit(solution)/shard_map/ppermute | solution.py:406
  48.2 6.3 %collective-permute-start.9 = (bf16[384,768]{1,0:T(8,128)(2,1)S(1)}, bf16[384,768]{1,0:T(8,128)(2,1)S(1)}, u32[]{:S(2)}, u32[]{:S(2)}) collective-permute-start(bf16[384,768]{1,0:T(8,128)(2,1)S(1)} %shard_map.70), channel_id=1, source_target_pairs={{0,1},{1,0},{2,3},{3,2},{4,5},{5,4},{6,7},{7,6},{8,9},{9,8},{10,11... | collective-permute-start | bytes 1769480 | tf_op jit(solution)/shard_map/ppermute | solution.py:406
  52.8 1.8 %collective-permute-start.10 = (bf16[864,256]{1,0:T(8,128)(2,1)S(1)}, bf16[864,256]{1,0:T(8,128)(2,1)S(1)}, u32[]{:S(2)}, u32[]{:S(2)}) collective-permute-start(bf16[864,256]{1,0:T(8,128)(2,1)S(1)} %collective-permute-done.8.refs_6_), channel_id=1, source_target_pairs={{0,1},{1,0},{2,3},{3,2},{4,5},{5,4},{6,7},{7,6},{8,9},{9,8},{10,11... | collective-permute-start | bytes 1327112 | tf_op jit(solution)/shard_map/ppermute | solution.py:406
  52.8 2.5 %collective-permute-start.12 = (bf16[864,256]{1,0:T(8,128)(2,1)S(1)}, bf16[864,256]{1,0:T(8,128)(2,1)S(1)}, u32[]{:S(2)}, u32[]{:S(2)}) collective-permute-start(bf16[864,256]{1,0:T(8,128)(2,1)S(1)} %collective-permute-done.3.refs_4_), channel_id=1, source_target_pairs={{0,1},{1,0},{2,3},{3,2},{4,5},{5,4},{6,7},{7,6},{8,9},{9,8},{10,11... | collective-permute-start | bytes 1327112 | tf_op jit(solution)/shard_map/ppermute | solution.py:406
  54.7 6.0 %collective-permute-start.11 = (bf16[96,768]{1,0:T(8,128)(2,1)S(1)}, bf16[96,768]{1,0:T(8,128)(2,1)S(1)}, u32[]{:S(2)}, u32[]{:S(2)}) collective-permute-start(bf16[96,768]{1,0:T(8,128)(2,1)S(1)} %get-tuple-element.79), channel_id=1, source_target_pairs={{0,2},{1,3},{2,0},{3,1},{4,6},{5,7},{6,4},{7,5},{8,10},{9,11},{10,... | collective-permute-start | bytes 442376 | tf_op jit(solution)/shard_map/ppermute | solution.py:406
  61.8 2.1 %collective-permute-start.13 = (bf16[384,768]{1,0:T(8,128)(2,1)S(1)}, bf16[384,768]{1,0:T(8,128)(2,1)S(1)}, u32[]{:S(2)}, u32[]{:S(2)}) collective-permute-start(bf16[384,768]{1,0:T(8,128)(2,1)S(1)} %shard_map.73), channel_id=1, source_target_pairs={{0,1},{1,0},{2,3},{3,2},{4,5},{5,4},{6,7},{7,6},{8,9},{9,8},{10,11... | collective-permute-start | bytes 1769480 | tf_op jit(solution)/shard_map/ppermute | solution.py:406
  64.0 15.2 %collective-permute-start.14 = (bf16[192,768]{1,0:T(8,128)(2,1)S(1)}, bf16[192,768]{1,0:T(8,128)(2,1)S(1)}, u32[]{:S(2)}, u32[]{:S(2)}) collective-permute-start(bf16[192,768]{1,0:T(8,128)(2,1)S(1)} %pad_maximum_fusion), channel_id=1, source_target_pairs={{0,4},{1,5},{2,6},{3,7},{4,8},{5,9},{6,10},{7,11},{8,12},{9,13},{1... | collective-permute-start | bytes 884744 | tf_op jit(solution)/shard_map/ppermute | solution.py:406
  68.4 12.0 %collective-permute-start.16 = (bf16[192,768]{1,0:T(8,128)(2,1)S(1)}, bf16[192,768]{1,0:T(8,128)(2,1)S(1)}, u32[]{:S(2)}, u32[]{:S(2)}) collective-permute-start(bf16[192,768]{1,0:T(8,128)(2,1)S(1)} %pad_maximum_fusion.1), channel_id=1, source_target_pairs={{0,2},{1,3},{2,0},{3,1},{4,6},{5,7},{6,4},{7,5},{8,10},{9,11},{10,... | collective-permute-start | bytes 884744 | tf_op jit(solution)/shard_map/ppermute | solution.py:406
  69.1 10.1 %collective-permute-start.15 = (bf16[96,768]{1,0:T(8,128)(2,1)S(1)}, bf16[96,768]{1,0:T(8,128)(2,1)S(1)}, u32[]{:S(2)}, u32[]{:S(2)}) collective-permute-start(bf16[96,768]{1,0:T(8,128)(2,1)S(1)} %get-tuple-element.76), channel_id=1, source_target_pairs={{0,6},{1,7},{2,4},{3,5},{4,10},{5,11},{6,8},{7,9},{8,14},{9,15},{1... | collective-permute-start | bytes 442376 | tf_op jit(solution)/shard_map/ppermute | solution.py:406

commit v7 on v6

--- a/solution.py
+++ b/solution.py
@@ -233,7 +233,7 @@
         add_products(n, range(5), a_ref, 0, prolong, row_of, blocks_of, sums)
         return carry
 
-    lax.fori_loop(0, STEPS, step, 0, unroll=4)
+    lax.fori_loop(0, STEPS, step, 0, unroll=8)
 
 
 def halo_rows_of(part, parts, upper, halo_ref, cols_ref, aggs_ref):
@@ -370,7 +370,7 @@
             couple(n, lambda u, c: sums[u][n, c] + above[u][n, c] if c < NAG else sums[u][n, c], coupled)
             return carry
 
-        lax.fori_loop(0, STEPS, step, 0, unroll=4 if products else 1)
+        lax.fori_loop(0, STEPS, step, 0, unroll=8 if products else 1)
 
     @pl.when(inside)
     def _():

time: 81.7 us -> 81.7 us (level)
  transfers between devices with their start and end apart: 17 -> 17, of which waited for: 10 -> 10; matrix products, arithmetic and copies ran while one was open for 1% -> 1% of each run, Pallas kernels for 38% -> 37%
where the time goes in v7:
time: 81.7 us; the launch traced here: 81.3 us
  Pallas kernels  31.3 us (38%)
  starting transfers between devices  20.4 us (25%)
  waiting for transfers between devices  19.2 us (24%)
  local copies, waits for them, and re-layouts  8.27 us (10%)
  other arithmetic  1.33 us (2%)
  between operations  0.92 us (1%)
    ppermute x17, starting transfers between devices, moved(): return lax.ppermute(x, AXES, route)  20.4 us
    ppermute x17, waiting for transfers between devices, moved(): return lax.ppermute(x, AXES, route)  19.2 us
    pallas_call x1, Pallas kernels, local(): pl.pallas_call(lambda *refs: own_kernel(*refs, parts=parts), out_shape=[p...  8.63 us
    unnamed x19, local copies, waits for them, and re-layouts  7.65 us
    pallas_call x1, Pallas kernels, local(): pl.pallas_call(lambda *refs: prepare_kernel(*refs, parts=parts), out_shap...  6.86 us
    pallas_call x1, Pallas kernels, local(): pl.pallas_call(lambda *refs: lower_kernel(*refs, parts=parts), out_shape=...  5.17 us
    pallas_call x4, Pallas kernels, coarse_of(): pl.pallas_call(lambda *refs: coarse_kernel(*refs, half=half), out_shape=j...  4.3 us
    pallas_call x1, Pallas kernels, upper_coupled(): pl.pallas_call(lambda *refs: upper_kernel(*refs, parts=parts), out_shape=...  4.2 us
  transfers between devices with their start and end apart: 17, of which 10 were waited for; matrix products, arithmetic and copies ran while one was open for 1% of the time, Pallas kernels for 37%

profile of v7, /device:TPU:16, one launch (start us, length us, event | category | flops | bytes accessed | tf_op | source)
XLA Modules:
  0.0 81.3 jit_solution(323059792544363736)
XLA Ops:
  0.0 0.0 copy-start
  0.0 1.3 %copy-done.2 = bf16[64,24,288]{2,1,0:T(8,128)(2,1)S(1)} copy-done((bf16[64,24,288]{2,1,0:T(8,128)(2,1)S(1)}, bf16[64,24,288]{2,1,0:T(8,128)(2,1)}, u32[]{:S(2)}) %copy-start.2) | copy-done | bytes 884760
  1.3 0.1 shard_map.64.p_ref.refs_3_
  1.4 0.1 collective-permute-start.5
  1.5 1.6 %collective-permute-start = (bf16[1728,256]{1,0:T(8,128)(2,1)S(1)}, bf16[1728,256]{1,0:T(8,128)(2,1)}, u32[]{:S(2)}, u32[]{:S(2)}) collective-permute-start(bf16[1728,256]{1,0:T(8,128)(2,1)S(1)} %shard_map.64.p_ref.refs_3_), channel_id=1, source_target_pairs={{0,2},{1,3},{2,0},{3,1},{4,6},{5,7},{6,4},{7,5},{8,10},{9,11},{10,... | collective-permute-start | bytes 2654216 | tf_op jit(solution)/shard_map/ppermute | solution.py:406
  3.1 0.1 pad_add_fusion.place_ref.refs_0_
  3.2 0.0 copy-done.4
  3.2 2.0 %shard_map.65 = (bf16[864,256]{1,0:T(8,128)(2,1)S(1)}, bf16[864,256]{1,0:T(8,128)(2,1)}) custom-call(s32[2]{0:T(128)S(1)} %pad_add_fusion.place_ref.refs_0_, s32[8,2,32]{2,1,0:T(2,128)S(1)} %copy-done.4, bf16[1728,256]{1,0:T(8,128)(2,1)S(1)} %shard_map.64.p_ref.refs_3_), custom_call_target="tpu_custom_call" | custom-call | flops 3300000000 | bytes 1000000 | tf_op jit(solution)/shard_map/pallas_call | solution.py:421
  5.2 0.8 copy-done.3
  5.9 3.4 %collective-permute-start.1 = (bf16[864,256]{1,0:T(8,128)(2,1)}, bf16[864,256]{1,0:T(8,128)(2,1)}, u32[]{:S(2)}, u32[]{:S(2)}) collective-permute-start(bf16[864,256]{1,0:T(8,128)(2,1)} %get-tuple-element.39), channel_id=1, source_target_pairs={{0,4},{1,5},{2,6},{3,7},{4,8},{5,9},{6,10},{7,11},{8,12},{9,13},{1... | collective-permute-start | bytes 1327112 | tf_op jit(solution)/shard_map/ppermute | solution.py:406
  10.0 0.1 constant_dynamic-slice_fusion
  10.1 0.1 copy.7
  10.2 0.2 reshape.13.refs_1_.refs_2_
  10.4 0.0 copy-start.1
  10.4 1.8 %copy-done.1 = bf16[64,24,864]{2,1,0:T(8,128)(2,1)S(1)} copy-done((bf16[64,24,864]{2,1,0:T(8,128)(2,1)S(1)}, bf16[64,24,864]{2,1,0:T(8,128)(2,1)}, u32[]{:S(2)}) %copy-start.1) | copy-done | bytes 2654232
  12.2 6.9 %shard_map.66 = (bf16[768,1536]{1,0:T(8,128)(2,1)S(1)}, bf16[9,1536,128]{2,1,0:T(8,128)(2,1)S(1)}) custom-call(s32[2]{0:T(128)S(1)} %pad_add_fusion.place_ref.refs_0_, s32[576]{0:T(1024)S(1)} %reshape.13.refs_1_.refs_2_, s32[1]{0:T(128)S(6)} %copy.9.refs_2_, bf16[1728,256]{1,0:T(8,128)(2,1)S(1)} %shard_map.64.p_ref.refs_3_, bf16[1536,864]{1,0:T(8,128)(2,1)S(1)} %bitcast.4), custom_call_target="tpu_custom_call" | custom-call | flops 9900000256 | bytes 1000000 | tf_op jit(solution)/shard_map/pallas_call | solution.py:437
  19.1 1.7 %copy-done.5 = bf16[9,1536,128]{2,1,0:T(8,128)(2,1)} copy-done((bf16[9,1536,128]{2,1,0:T(8,128)(2,1)}, bf16[9,1536,128]{2,1,0:T(8,128)(2,1)S(1)}, u32[]{:S(2)}) %copy-start.5) | copy-done | bytes 3538968
  20.8 0.5 collective-permute-done.1.refs_4_
  21.3 2.4 %collective-permute-done.refs_5_ = bf16[1728,256]{1,0:T(8,128)(2,1)} collective-permute-done((bf16[1728,256]{1,0:T(8,128)(2,1)S(1)}, bf16[1728,256]{1,0:T(8,128)(2,1)}, u32[]{:S(2)}, u32[]{:S(2)}) %collective-permute-start) | collective-permute-done | bytes 884768 | tf_op jit(solution)/shard_map/ppermute | solution.py:406
  23.7 0.0 collective-permute-start.6
  23.7 0.0 copy-done.8
  23.7 0.1 copy.8
  23.8 0.1 reshape.15.refs_2_.refs_3_
  23.9 1.6 %collective-permute-start.4 = (bf16[864,256]{1,0:T(8,128)(2,1)}, bf16[864,256]{1,0:T(8,128)(2,1)S(1)}, u32[]{:S(2)}, u32[]{:S(2)}) collective-permute-start(bf16[864,256]{1,0:T(8,128)(2,1)} %collective-permute-done.1.refs_4_), channel_id=1, source_target_pairs={{0,2},{1,3},{2,0},{3,1},{4,6},{5,7},{6,4},{7,5},{8,10},{9,11},{10,... | collective-permute-start | bytes 1327112 | tf_op jit(solution)/shard_map/ppermute | solution.py:406
  25.5 0.2 collective-permute-start.2
  25.7 3.3 %collective-permute-start.3 = (bf16[864,256]{1,0:T(8,128)(2,1)}, bf16[864,256]{1,0:T(8,128)(2,1)S(1)}, u32[]{:S(2)}, u32[]{:S(2)}) collective-permute-start(bf16[864,256]{1,0:T(8,128)(2,1)} %copy-done.3), channel_id=1, source_target_pairs={{4,0},{5,1},{6,2},{7,3},{8,4},{9,5},{10,6},{11,7},{12,8},{13,9},{1... | collective-permute-start | bytes 1327112 | tf_op jit(solution)/shard_map/ppermute | solution.py:406
  29.0 0.0 collective-permute-done.5.refs_4_
  29.0 0.0 collective-permute-done.6.refs_6_
  29.0 2.0 %copy-done.6 = bf16[9,1536,128]{2,1,0:T(8,128)(2,1)S(1)} copy-done((bf16[9,1536,128]{2,1,0:T(8,128)(2,1)S(1)}, bf16[9,1536,128]{2,1,0:T(8,128)(2,1)}, u32[]{:S(2)}) %copy-start.6) | copy-done | bytes 3538968
  31.0 8.6 %shard_map.67 = (bf16[64,96,384]{2,1,0:T(8,128)(2,1)S(1)}, f32[16,8,24,128]{3,2,1,0:T(8,128)S(1)}, f32[16,8,24,128]{3,2,1,0:T(8,128)S(1)}, f32[16,8,24,128]{3,2,1,0:T(8,128)S(1)}, f32[16,8,24,128]{3,2,1,0:T(8,128)S(1)}) custom-call(s32[2]{0:T(128)S(1)} %pad_add_fusion.place_ref.refs_0_, s32[576]{0:T(1024)S(1)} %reshape.13.refs_1_.refs_2_, ...), custom_call_target="tpu_custom_call" | custom-call | flops 11000000512 | bytes 1000000 | tf_op jit(solution)/shard_map/pallas_call | solution.py:456
  39.7 0.5 collective-permute-done.3.refs_4_
  40.2 0.0 collective-permute-done.4.refs_6_
  40.2 0.0 collective-permute-start.7
  40.2 0.5 collective-permute-start.8
  40.7 0.0 collective-permute-done.2.refs_5_
  40.7 1.3 %collective-permute-done.7.refs_7_ = bf16[864,256]{1,0:T(8,128)(2,1)S(1)} collective-permute-done((bf16[864,256]{1,0:T(8,128)(2,1)S(1)}, bf16[864,256]{1,0:T(8,128)(2,1)S(1)}, u32[]{:S(2)}, u32[]{:S(2)}) %collective-permute-start.7) | collective-permute-done | bytes 442400 | tf_op jit(solution)/shard_map/ppermute | solution.py:406
  42.0 0.0 copy-done.7
  42.0 5.2 %shard_map.68 = (bf16[1536,768]{1,0:T(8,128)(2,1)S(1)}, f32[16,4,24,128]{3,2,1,0:T(8,128)S(1)}, f32[16,4,24,128]{3,2,1,0:T(8,128)S(1)}, f32[16,4,24,128]{3,2,1,0:T(8,128)S(1)}, f32[16,4,24,128]{3,2,1,0:T(8,128)S(1)}) custom-call(s32[2]{0:T(128)S(1)} %pad_add_fusion.place_ref.refs_0_, s32[8,2,32]{2,1,0:T(2,128)S(1)} %copy-done.4, ...), custom_call_target="tpu_custom_call" | custom-call | flops 6600000000 | bytes 1000000 | tf_op jit(solution)/shard_map/pallas_call | solution.py:471
  47.2 1.1 %shard_map.70 = bf16[384,768]{1,0:T(8,128)(2,1)S(1)} custom-call(bf16[768,1536]{1,0:T(8,128)(2,1)S(1)} %get-tuple-element.42.refs_0_, bf16[1536,768]{1,0:T(8,128)(2,1)S(1)} %get-tuple-element.54.refs_1_), custom_call_target="tpu_custom_call" | custom-call | flops 11000000 | bytes 1000000 | tf_op jit(solution)/shard_map/pallas_call | solution.py:504
  48.3 0.2 collective-permute-start.9
  48.5 1.1 %shard_map.69 = f32[384,768]{1,0:T(8,128)S(1)} custom-call(bf16[768,1536]{1,0:T(8,128)(2,1)S(1)} %get-tuple-element.42.refs_0_, bf16[1536,768]{1,0:T(8,128)(2,1)S(1)} %get-tuple-element.54.refs_1_), custom_call_target="tpu_custom_call" | custom-call | flops 11000000 | bytes 1000000 | tf_op jit(solution)/shard_map/pallas_call | solution.py:504
  49.5 3.2 %collective-permute-done.8.refs_6_ = bf16[864,256]{1,0:T(8,128)(2,1)S(1)} collective-permute-done((bf16[864,256]{1,0:T(8,128)(2,1)S(1)}, bf16[864,256]{1,0:T(8,128)(2,1)S(1)}, u32[]{:S(2)}, u32[]{:S(2)}) %collective-permute-start.8) | collective-permute-done | bytes 442400 | tf_op jit(solution)/shard_map/ppermute | solution.py:406
  52.8 0.0 collective-permute-start.10
  52.8 0.5 collective-permute-start.12
  53.3 1.3 %collective-permute-done.10.refs_7_ = bf16[864,256]{1,0:T(8,128)(2,1)S(1)} collective-permute-done((bf16[864,256]{1,0:T(8,128)(2,1)S(1)}, bf16[864,256]{1,0:T(8,128)(2,1)S(1)}, u32[]{:S(2)}, u32[]{:S(2)}) %collective-permute-start.10) | collective-permute-done | bytes 442400 | tf_op jit(solution)/shard_map/ppermute | solution.py:406
  54.6 0.0 collective-permute-done.9
  54.6 0.1 convert_add_fusion.1
  54.7 0.6 collective-permute-start.11
  55.3 0.0 collective-permute-done.12.refs_5_
  55.3 4.2 %shard_map.71.refs_1_ = bf16[1536,768]{1,0:T(8,128)(2,1)S(1)} custom-call(s32[2]{0:T(128)S(1)} %pad_add_fusion.place_ref.refs_0_, s32[8,2,32]{2,1,0:T(2,128)S(1)} %copy-done.4, s32[576]{0:T(1024)S(1)} %reshape.13.refs_1_.refs_2_, s32[576]{0:T(1024)S(1)} %reshape.15.refs_2_.refs_3_, bf16[864,256]{1,0:T(8,128)(2,1)S(1)} %collective-permute-done.3.refs_4_, ...), custom_call_target="tpu_custom_call" | custom-call | flops 6600000000 | bytes 1000000 | tf_op jit(solution)/shard_map/pallas_call | solution.py:488
  59.5 1.2 %collective-permute-done.11 = bf16[96,768]{1,0:T(8,128)(2,1)S(1)} collective-permute-done((bf16[96,768]{1,0:T(8,128)(2,1)S(1)}, bf16[96,768]{1,0:T(8,128)(2,1)S(1)}, u32[]{:S(2)}, u32[]{:S(2)}) %collective-permute-start.11) | collective-permute-done | bytes 147488 | tf_op jit(solution)/shard_map/ppermute | solution.py:406
  60.7 1.1 %shard_map.73 = bf16[384,768]{1,0:T(8,128)(2,1)S(1)} custom-call(bf16[768,1536]{1,0:T(8,128)(2,1)S(1)} %get-tuple-element.42.refs_0_, bf16[1536,768]{1,0:T(8,128)(2,1)S(1)} %shard_map.71.refs_1_), custom_call_target="tpu_custom_call" | custom-call | flops 1650000000 | bytes 1000000 | tf_op jit(solution)/shard_map/pallas_call | solution.py:504
  61.8 0.1 collective-permute-start.13
  61.9 1.1 %shard_map.72 = f32[384,768]{1,0:T(8,128)S(1)} custom-call(bf16[768,1536]{1,0:T(8,128)(2,1)S(1)} %get-tuple-element.42.refs_0_, bf16[1536,768]{1,0:T(8,128)(2,1)S(1)} %shard_map.71.refs_1_), custom_call_target="tpu_custom_call" | custom-call | flops 1650000000 | bytes 1000000 | tf_op jit(solution)/shard_map/pallas_call | solution.py:504
  63.0 0.9 %collective-permute-done.13 = bf16[384,768]{1,0:T(8,128)(2,1)S(1)} collective-permute-done((bf16[384,768]{1,0:T(8,128)(2,1)S(1)}, bf16[384,768]{1,0:T(8,128)(2,1)S(1)}, u32[]{:S(2)}, u32[]{:S(2)}) %collective-permute-start.13) | collective-permute-done | bytes 589856 | tf_op jit(solution)/shard_map/ppermute | solution.py:406
  63.9 0.1 fusion.3
  64.0 4.3 %collective-permute-start.14 = (bf16[192,768]{1,0:T(8,128)(2,1)S(1)}, bf16[192,768]{1,0:T(8,128)(2,1)S(1)}, u32[]{:S(2)}, u32[]{:S(2)}) collective-permute-start(bf16[192,768]{1,0:T(8,128)(2,1)S(1)} %pad_maximum_fusion), channel_id=1, source_target_pairs={{0,4},{1,5},{2,6},{3,7},{4,8},{5,9},{6,10},{7,11},{8,12},{9,13},{1... | collective-permute-start | bytes 884744 | tf_op jit(solution)/shard_map/ppermute | solution.py:406
  68.4 0.6 collective-permute-start.16
  69.0 3.5 %collective-permute-start.15 = (bf16[96,768]{1,0:T(8,128)(2,1)S(1)}, bf16[96,768]{1,0:T(8,128)(2,1)S(1)}, u32[]{:S(2)}, u32[]{:S(2)}) collective-permute-start(bf16[96,768]{1,0:T(8,128)(2,1)S(1)} %get-tuple-element.76), channel_id=1, source_target_pairs={{0,6},{1,7},{2,4},{3,5},{4,10},{5,11},{6,8},{7,9},{8,14},{9,15},{1... | collective-permute-start | bytes 442376 | tf_op jit(solution)/shard_map/ppermute | solution.py:406
  72.5 6.6 %collective-permute-done.15 = bf16[96,768]{1,0:T(8,128)(2,1)S(1)} collective-permute-done((bf16[96,768]{1,0:T(8,128)(2,1)S(1)}, bf16[96,768]{1,0:T(8,128)(2,1)S(1)}, u32[]{:S(2)}, u32[]{:S(2)}) %collective-permute-start.15) | collective-permute-done | bytes 147488 | tf_op jit(solution)/shard_map/ppermute | solution.py:406
  79.1 0.0 collective-permute-done.14
  79.1 1.3 %collective-permute-done.16 = bf16[192,768]{1,0:T(8,128)(2,1)S(1)} collective-permute-done((bf16[192,768]{1,0:T(8,128)(2,1)S(1)}, bf16[192,768]{1,0:T(8,128)(2,1)S(1)}, u32[]{:S(2)}, u32[]{:S(2)}) %collective-permute-start.16) | collective-permute-done | bytes 294944 | tf_op jit(solution)/shard_map/ppermute | solution.py:406
  80.5 0.1 slice_add_fusion.1
  80.5 0.8 fusion.1
  (16 shorter events, 0.2 us)
Async XLA Ops:
  0.0 10.0 %copy-start = (s32[512,3]{0,1:T(4,128)S(1)}, s32[512,3]{0,1:T(4,128)}, u32[]{:S(2)}) copy-start(s32[512,3]{0,1:T(4,128)} %param.9) | copy-start | bytes 18436
  0.0 1.3 %copy-start.2 = (bf16[64,24,288]{2,1,0:T(8,128)(2,1)S(1)}, bf16[64,24,288]{2,1,0:T(8,128)(2,1)}, u32[]{:S(2)}) copy-start(bf16[64,24,288]{2,1,0:T(8,128)(2,1)} %param.7) | copy-start | bytes 2654212
  1.3 1.9 %copy-start.4 = (s32[8,2,32]{2,1,0:T(2,128)S(1)}, s32[8,2,32]{2,1,0:T(2,128)}, u32[]{:S(2)}) copy-start(s32[8,2,32]{2,1,0:T(2,128)} %refs_1_.3) | copy-start | bytes 6148
  1.4 27.6 %collective-permute-start.5 = (bf16[1728,256]{1,0:T(8,128)(2,1)S(1)}, bf16[1728,256]{1,0:T(8,128)(2,1)}, u32[]{:S(2)}, u32[]{:S(2)}) collective-permute-start(bf16[1728,256]{1,0:T(8,128)(2,1)S(1)} %shard_map.64.p_ref.refs_3_), channel_id=1, source_target_pairs={{0,1},{1,0},{2,3},{3,2},{4,5},{5,4},{6,7},{7,6},{8,9},{9,8},{10,11... | collective-permute-start | bytes 2654216 | tf_op jit(solution)/shard_map/ppermute | solution.py:406
  1.5 22.2 %collective-permute-start = (bf16[1728,256]{1,0:T(8,128)(2,1)S(1)}, bf16[1728,256]{1,0:T(8,128)(2,1)}, u32[]{:S(2)}, u32[]{:S(2)}) collective-permute-start(bf16[1728,256]{1,0:T(8,128)(2,1)S(1)} %shard_map.64.p_ref.refs_3_), channel_id=1, source_target_pairs={{0,2},{1,3},{2,0},{3,1},{4,6},{5,7},{6,4},{7,5},{8,10},{9,11},{10,... | collective-permute-start | bytes 2654216 | tf_op jit(solution)/shard_map/ppermute | solution.py:406
  5.2 0.8 copy-start.3
  5.9 15.3 %collective-permute-start.1 = (bf16[864,256]{1,0:T(8,128)(2,1)}, bf16[864,256]{1,0:T(8,128)(2,1)}, u32[]{:S(2)}, u32[]{:S(2)}) collective-permute-start(bf16[864,256]{1,0:T(8,128)(2,1)} %get-tuple-element.39), channel_id=1, source_target_pairs={{0,4},{1,5},{2,6},{3,7},{4,8},{5,9},{6,10},{7,11},{8,12},{9,13},{1... | collective-permute-start | bytes 1327112 | tf_op jit(solution)/shard_map/ppermute | solution.py:406
  10.4 1.8 %copy-start.1 = (bf16[64,24,864]{2,1,0:T(8,128)(2,1)S(1)}, bf16[64,24,864]{2,1,0:T(8,128)(2,1)}, u32[]{:S(2)}) copy-start(bf16[64,24,864]{2,1,0:T(8,128)(2,1)} %param.6) | copy-start | bytes 7962628
  12.2 11.5 %copy-start.8 = (s32[64,9]{0,1:T(8,128)S(1)}, s32[64,9]{0,1:T(8,128)}, u32[]{:S(2)}) copy-start(s32[64,9]{0,1:T(8,128)} %param.8) | copy-start | bytes 6916
  19.0 1.7 %copy-start.5 = (bf16[9,1536,128]{2,1,0:T(8,128)(2,1)}, bf16[9,1536,128]{2,1,0:T(8,128)(2,1)S(1)}, u32[]{:S(2)}) copy-start(bf16[9,1536,128]{2,1,0:T(8,128)(2,1)S(1)} %get-tuple-element.46.refs_7_.refs_8_) | copy-start | bytes 10616836
  23.7 5.3 %collective-permute-start.6 = (bf16[1728,256]{1,0:T(8,128)(2,1)}, bf16[1728,256]{1,0:T(8,128)(2,1)}, u32[]{:S(2)}, u32[]{:S(2)}) collective-permute-start(bf16[1728,256]{1,0:T(8,128)(2,1)} %collective-permute-done.refs_5_), channel_id=1, source_target_pairs={{0,1},{1,0},{2,3},{3,2},{4,5},{5,4},{6,7},{7,6},{8,9},{9,8},{10,11... | collective-permute-start | bytes 2654216 | tf_op jit(solution)/shard_map/ppermute | solution.py:406
  23.9 16.3 %collective-permute-start.4 = (bf16[864,256]{1,0:T(8,128)(2,1)}, bf16[864,256]{1,0:T(8,128)(2,1)S(1)}, u32[]{:S(2)}, u32[]{:S(2)}) collective-permute-start(bf16[864,256]{1,0:T(8,128)(2,1)} %collective-permute-done.1.refs_4_), channel_id=1, source_target_pairs={{0,2},{1,3},{2,0},{3,1},{4,6},{5,7},{6,4},{7,5},{8,10},{9,11},{10,... | collective-permute-start | bytes 1327112 | tf_op jit(solution)/shard_map/ppermute | solution.py:406
  25.5 15.2 %collective-permute-start.2 = (bf16[864,256]{1,0:T(8,128)(2,1)}, bf16[864,256]{1,0:T(8,128)(2,1)S(1)}, u32[]{:S(2)}, u32[]{:S(2)}) collective-permute-start(bf16[864,256]{1,0:T(8,128)(2,1)} %collective-permute-done.1.refs_4_), channel_id=1, source_target_pairs={{0,1},{1,0},{2,3},{3,2},{4,5},{5,4},{6,7},{7,6},{8,9},{9,8},{10,11... | collective-permute-start | bytes 1327112 | tf_op jit(solution)/shard_map/ppermute | solution.py:406
  25.7 14.4 %collective-permute-start.3 = (bf16[864,256]{1,0:T(8,128)(2,1)}, bf16[864,256]{1,0:T(8,128)(2,1)S(1)}, u32[]{:S(2)}, u32[]{:S(2)}) collective-permute-start(bf16[864,256]{1,0:T(8,128)(2,1)} %copy-done.3), channel_id=1, source_target_pairs={{4,0},{5,1},{6,2},{7,3},{8,4},{9,5},{10,6},{11,7},{12,8},{13,9},{1... | collective-permute-start | bytes 1327112 | tf_op jit(solution)/shard_map/ppermute | solution.py:406
  29.0 2.0 %copy-start.6 = (bf16[9,1536,128]{2,1,0:T(8,128)(2,1)S(1)}, bf16[9,1536,128]{2,1,0:T(8,128)(2,1)}, u32[]{:S(2)}) copy-start(bf16[9,1536,128]{2,1,0:T(8,128)(2,1)} %copy-done.5) | copy-start | bytes 10616836
  31.0 10.9 %copy-start.7 = (bf16[9,1536,128]{2,1,0:T(8,128)(2,1)S(1)}, bf16[9,1536,128]{2,1,0:T(8,128)(2,1)}, u32[]{:S(2)}) copy-start(bf16[9,1536,128]{2,1,0:T(8,128)(2,1)} %copy-done.5) | copy-start | bytes 10616836
  40.2 1.8 %collective-permute-start.7 = (bf16[864,256]{1,0:T(8,128)(2,1)S(1)}, bf16[864,256]{1,0:T(8,128)(2,1)S(1)}, u32[]{:S(2)}, u32[]{:S(2)}) collective-permute-start(bf16[864,256]{1,0:T(8,128)(2,1)S(1)} %collective-permute-done.4.refs_6_), channel_id=1, source_target_pairs={{0,1},{1,0},{2,3},{3,2},{4,5},{5,4},{6,7},{7,6},{8,9},{9,8},{10,11... | collective-permute-start | bytes 1327112 | tf_op jit(solution)/shard_map/ppermute | solution.py:406
  40.2 12.6 %collective-permute-start.8 = (bf16[864,256]{1,0:T(8,128)(2,1)S(1)}, bf16[864,256]{1,0:T(8,128)(2,1)S(1)}, u32[]{:S(2)}, u32[]{:S(2)}) collective-permute-start(bf16[864,256]{1,0:T(8,128)(2,1)S(1)} %collective-permute-done.3.refs_4_), channel_id=1, source_target_pairs={{0,2},{1,3},{2,0},{3,1},{4,6},{5,7},{6,4},{7,5},{8,10},{9,11},{10,... | collective-permute-start | bytes 1327112 | tf_op jit(solution)/shard_map/ppermute | solution.py:406
  48.3 6.3 %collective-permute-start.9 = (bf16[384,768]{1,0:T(8,128)(2,1)S(1)}, bf16[384,768]{1,0:T(8,128)(2,1)S(1)}, u32[]{:S(2)}, u32[]{:S(2)}) collective-permute-start(bf16[384,768]{1,0:T(8,128)(2,1)S(1)} %shard_map.70), channel_id=1, source_target_pairs={{0,1},{1,0},{2,3},{3,2},{4,5},{5,4},{6,7},{7,6},{8,9},{9,8},{10,11... | collective-permute-start | bytes 1769480 | tf_op jit(solution)/shard_map/ppermute | solution.py:406
  52.8 1.8 %collective-permute-start.10 = (bf16[864,256]{1,0:T(8,128)(2,1)S(1)}, bf16[864,256]{1,0:T(8,128)(2,1)S(1)}, u32[]{:S(2)}, u32[]{:S(2)}) collective-permute-start(bf16[864,256]{1,0:T(8,128)(2,1)S(1)} %collective-permute-done.8.refs_6_), channel_id=1, source_target_pairs={{0,1},{1,0},{2,3},{3,2},{4,5},{5,4},{6,7},{7,6},{8,9},{9,8},{10,11... | collective-permute-start | bytes 1327112 | tf_op jit(solution)/shard_map/ppermute | solution.py:406
  52.8 2.5 %collective-permute-start.12 = (bf16[864,256]{1,0:T(8,128)(2,1)S(1)}, bf16[864,256]{1,0:T(8,128)(2,1)S(1)}, u32[]{:S(2)}, u32[]{:S(2)}) collective-permute-start(bf16[864,256]{1,0:T(8,128)(2,1)S(1)} %collective-permute-done.3.refs_4_), channel_id=1, source_target_pairs={{0,1},{1,0},{2,3},{3,2},{4,5},{5,4},{6,7},{7,6},{8,9},{9,8},{10,11... | collective-permute-start | bytes 1327112 | tf_op jit(solution)/shard_map/ppermute | solution.py:406
  54.7 6.0 %collective-permute-start.11 = (bf16[96,768]{1,0:T(8,128)(2,1)S(1)}, bf16[96,768]{1,0:T(8,128)(2,1)S(1)}, u32[]{:S(2)}, u32[]{:S(2)}) collective-permute-start(bf16[96,768]{1,0:T(8,128)(2,1)S(1)} %get-tuple-element.79), channel_id=1, source_target_pairs={{0,2},{1,3},{2,0},{3,1},{4,6},{5,7},{6,4},{7,5},{8,10},{9,11},{10,... | collective-permute-start | bytes 442376 | tf_op jit(solution)/shard_map/ppermute | solution.py:406
  61.8 2.1 %collective-permute-start.13 = (bf16[384,768]{1,0:T(8,128)(2,1)S(1)}, bf16[384,768]{1,0:T(8,128)(2,1)S(1)}, u32[]{:S(2)}, u32[]{:S(2)}) collective-permute-start(bf16[384,768]{1,0:T(8,128)(2,1)S(1)} %shard_map.73), channel_id=1, source_target_pairs={{0,1},{1,0},{2,3},{3,2},{4,5},{5,4},{6,7},{7,6},{8,9},{9,8},{10,11... | collective-permute-start | bytes 1769480 | tf_op jit(solution)/shard_map/ppermute | solution.py:406
  64.0 15.1 %collective-permute-start.14 = (bf16[192,768]{1,0:T(8,128)(2,1)S(1)}, bf16[192,768]{1,0:T(8,128)(2,1)S(1)}, u32[]{:S(2)}, u32[]{:S(2)}) collective-permute-start(bf16[192,768]{1,0:T(8,128)(2,1)S(1)} %pad_maximum_fusion), channel_id=1, source_target_pairs={{0,4},{1,5},{2,6},{3,7},{4,8},{5,9},{6,10},{7,11},{8,12},{9,13},{1... | collective-permute-start | bytes 884744 | tf_op jit(solution)/shard_map/ppermute | solution.py:406
  68.4 12.0 %collective-permute-start.16 = (bf16[192,768]{1,0:T(8,128)(2,1)S(1)}, bf16[192,768]{1,0:T(8,128)(2,1)S(1)}, u32[]{:S(2)}, u32[]{:S(2)}) collective-permute-start(bf16[192,768]{1,0:T(8,128)(2,1)S(1)} %pad_maximum_fusion.1), channel_id=1, source_target_pairs={{0,2},{1,3},{2,0},{3,1},{4,6},{5,7},{6,4},{7,5},{8,10},{9,11},{10,... | collective-permute-start | bytes 884744 | tf_op jit(solution)/shard_map/ppermute | solution.py:406
  69.0 10.1 %collective-permute-start.15 = (bf16[96,768]{1,0:T(8,128)(2,1)S(1)}, bf16[96,768]{1,0:T(8,128)(2,1)S(1)}, u32[]{:S(2)}, u32[]{:S(2)}) collective-permute-start(bf16[96,768]{1,0:T(8,128)(2,1)S(1)} %get-tuple-element.76), channel_id=1, source_target_pairs={{0,6},{1,7},{2,4},{3,5},{4,10},{5,11},{6,8},{7,9},{8,14},{9,15},{1... | collective-permute-start | bytes 442376 | tf_op jit(solution)/shard_map/ppermute | solution.py:406
